TPU v7x, 128 devices: a whole 4x4x4 slice. The times are simulated.
128 devices in a mesh: group: 8 (over y, core), tp: 16 (over z, x).
Axes of the slice: x: 4, y: 4, z: 4, core: 2. Of those that a mesh axis runs over, the one named last changes fastest.
Arguments:
- vision_rows: bfloat16 [8, 16, 32, 7680], P('group', None, None, 'tp'), may hold values from -6 to 6
- tile_count: int32 [32], replicated, may hold values from 1 to 4, as said below
- tile_source: int32 [8, 16], replicated, may hold values from 0 to 15, as said below
- row_request: int32 [8, 64], P('group'), may hold values from 0 to 3
- proj_weight: bfloat16 [7680, 8192], P(None, 'tp'), may hold values from -0.0625 to 0.0625
- proj_bias: bfloat16 [8192], P('tp'), may hold values from -3 to 3
- kv_weight: bfloat16 [2, 8192, 1024], P(None, 'tp'), may hold values from -0.0625 to 0.0625
- query_weight: bfloat16 [8192, 8192], P(None, 'tp'), may hold values from -4 to 4
- out_weight: bfloat16 [8192, 8192], P('tp'), may hold values from -0.0625 to 0.0625
- norm_gain: bfloat16 [8192], P('tp'), may hold values from 0.25 to 1.75
- attn_gate: float32 [], replicated, may hold values from 0.5 to 1.5
- states: bfloat16 [2, 512, 8192], P(None, 'group', 'tp'), may hold values from -6 to 6
Outputs:
- mixed: bfloat16 [2, 512, 8192], P(None, 'group', 'tp')
Inputs may be any that keep to these rules, and one draw needn't show every extreme that they name: `tile_count`: some request has 4 tiles and some has 1. `tile_source`: each row is a permutation of 0 to 15.
All inputs are finite; a program needn't handle non-finite values.
Results may differ from a plain program's by a relative error of at most 0.02.
Values may be sent and summed in bfloat16 or wider, within the bound.
No kernel may reach another device: no remote copies, remote signals or barrier semaphores. Data moves between devices by JAX's collectives and lax.ppermute only.
A program may use at most 128 MiB of HBM per device.

v0:
```python
import jax
import jax.numpy as jnp
from jax import lax
from jax.sharding import PartitionSpec as P

D = 8192
HEADS = 64
KV_HEADS = 8
HEAD_DIM = 128
MAXT = 4
STEPS = 2


def body(
    vision_rows,
    tile_count,
    tile_source,
    row_request,
    proj_weight,
    proj_bias,
    kv_weight,
    query_weight,
    out_weight,
    norm_gain,
    attn_gate,
    states,
):
    groups = lax.axis_size("group")
    ranks = lax.axis_size("tp")
    group = lax.axis_index("group")
    rank = lax.axis_index("tp")
    tile_rows = vision_rows.shape[2]
    per_group = vision_rows.shape[1] // groups
    slots = groups * per_group
    group_rows = slots * tile_rows
    req_grp = slots // MAXT
    kv_width = kv_weight.shape[2]
    batch = states.shape[1]
    local_heads = HEADS // ranks
    group_size = HEADS // KV_HEADS
    scale = 1.0 / HEAD_DIM**0.5
    gate = jnp.tanh(attn_gate)
    every_tile = lax.all_gather(vision_rows, "group", axis=0, tiled=True)
    mine = lax.dynamic_slice_in_dim(every_tile, group * per_group, per_group, 1)
    by_encoder = mine.reshape(slots, tile_rows, vision_rows.shape[3])
    sources = lax.dynamic_index_in_dim(tile_source, group, 0, keepdims=False)
    ordered = jnp.take(by_encoder, sources, axis=0).reshape(group_rows, vision_rows.shape[3])
    accum = jnp.dot(
        lax.all_gather(ordered, "tp", axis=1, tiled=True),
        proj_weight,
        preferred_element_type=jnp.float32,
    )
    projected = (accum + proj_bias.astype(jnp.float32)).astype(jnp.bfloat16)
    my_counts = lax.dynamic_slice_in_dim(tile_count, group * req_grp, req_grp, 0)
    requests_row = row_request[0]
    share = group_rows // ranks
    both_weights = jnp.concatenate([kv_weight[0], kv_weight[1]], axis=1)
    local_kv = lax.psum_scatter(
        jnp.dot(projected, both_weights, preferred_element_type=jnp.float32),
        "tp",
        scatter_dimension=0,
        tiled=True,
    ).astype(jnp.bfloat16)
    keys = local_kv[:, :kv_width].reshape(share, KV_HEADS, HEAD_DIM)
    values = local_kv[:, kv_width:].reshape(share, KV_HEADS, HEAD_DIM)
    position = (rank * share + jnp.arange(share, dtype=jnp.int32)) // tile_rows
    request = position // MAXT
    hits = request[:, None] == jnp.arange(req_grp, dtype=jnp.int32)[None, :]
    counts = jnp.sum(jnp.where(hits, my_counts[None, :], 0), axis=1)
    valid = position % MAXT < counts
    allowed = valid[None, :] & (request[None, :] == requests_row[:, None])
    masked = allowed[:, None, None, :]
    outputs = []
    for step in range(STEPS):
        hidden = states[step].astype(jnp.float32)
        squares = lax.psum(jnp.sum(hidden * hidden, axis=1), "tp")
        inverse = lax.rsqrt(squares / D + 1e-05)
        normed = (hidden * inverse[:, None] * norm_gain.astype(jnp.float32)).astype(jnp.bfloat16)
        own_query = jnp.dot(
            lax.all_gather(normed, "tp", axis=1, tiled=True),
            query_weight,
            preferred_element_type=jnp.float32,
        ).astype(jnp.bfloat16)
        every_query = lax.all_gather(own_query, "tp", axis=1, tiled=True).reshape(
            batch, KV_HEADS, group_size, HEAD_DIM
        )
        scores = (
            jnp.einsum("bkgd,rkd->bkgr", every_query, keys, preferred_element_type=jnp.float32)
            * scale
        )
        local_top = jnp.max(jnp.where(masked, scores, -1e30), axis=-1)
        largest = lax.pmax(local_top, "tp")
        weights = jnp.where(masked, jnp.exp(scores - largest[..., None]), 0.0)
        total = jnp.sum(weights, axis=-1).reshape(batch, HEADS)
        summed = jnp.einsum(
            "bkgr,rkd->bkgd",
            weights.astype(jnp.bfloat16),
            values,
            preferred_element_type=jnp.float32,
        )
        summed = summed.reshape(batch, HEADS, HEAD_DIM)
        head_num, head_total = (
            lax.psum_scatter(
                summed.astype(jnp.bfloat16), "tp", scatter_dimension=1, tiled=True
            ).astype(jnp.float32),
            lax.psum_scatter(
                total.astype(jnp.bfloat16), "tp", scatter_dimension=1, tiled=True
            ).astype(jnp.float32),
        )
        context = (
            (head_num / head_total[..., None])
            .astype(jnp.bfloat16)
            .reshape(batch, local_heads * HEAD_DIM)
        )
        branch = jnp.dot(context, out_weight, preferred_element_type=jnp.float32)
        reduced = lax.psum_scatter(
            branch.astype(jnp.bfloat16), "tp", scatter_dimension=1, tiled=True
        ).astype(jnp.float32)
        outputs.append((hidden + gate * reduced).astype(jnp.bfloat16))
    return jnp.stack(outputs, axis=0)


def solution(mesh):
    in_specs = (
        P("group", None, None, "tp"),
        P(),
        P(),
        P("group", None),
        P(None, "tp"),
        P("tp"),
        P(None, "tp", None),
        P(None, "tp"),
        P("tp", None),
        P("tp"),
        P(),
        P(None, "group", "tp"),
    )
    out_specs = P(None, "group", "tp")
    return jax.shard_map(body, mesh=mesh, in_specs=in_specs, out_specs=out_specs, check_vma=False)
```

profile of v0, /device:TPU:30, one launch (start us, length us, event | category | flops | bytes accessed | tf_op | source)
XLA Modules:
  0.0 827.8 jit_solution(10779081446146808517)
XLA Ops:
  9.0 33.7 %all-reduce.2 = (f32[64]{0:T(128)S(1)}, f32[64]{0:T(128)S(1)}) all-reduce(f32[64]{0:T(128)S(1)} %get-tuple-element.6, f32[64]{0:T(128)S(1)} %get-tuple-element.5), channel_id=1, replica_groups=mesh['group'=8,'tp'=16] {'tp'}, use_global_device_ids=true, to_apply=%region_11.12 | all-reduce | flops 128 | bytes 1024 | tf_op jit(solution)/shard_map/psum | solution.py:76
  42.7 1.6 fusion.24
  49.6 42.1 %all-gather.11.cloned.1.call-done = bf16[64,8192]{1,0:T(8,128)(2,1)} async-done(((bf16[64,512]{1,0:T(8,128)(2,1)}), bf16[64,8192]{1,0:T(8,128)(2,1)}) %all-gather.11.cloned.1.call-update) | async-done | bytes 1048592 | tf_op jit(solution)/shard_map/all_gather | solution.py:80
  91.8 5.9 convolution_convert_fusion.5
  97.8 1.7 slice_bitcast_fusion.1
  99.5 37.2 %all-gather.15.cloned.1.call-done = bf16[64,8192]{1,0:T(8,128)(2,1)} async-done(((bf16[64,512]{1,0:T(8,128)(2,1)}), bf16[64,8192]{1,0:T(8,128)(2,1)}) %all-gather.15.cloned.1.call-update) | async-done | bytes 1048592 | tf_op jit(solution)/shard_map/all_gather | solution.py:80
  136.6 5.9 convolution_convert_fusion.4
  142.6 64.2 %all-gather.9.cloned.1.call-done = bf16[512,7680]{0,1:T(8,128)(2,1)} async-done(((bf16[512,480]{0,1:T(8,128)(2,1)}), bf16[512,7680]{0,1:T(8,128)(2,1)}) %all-gather.9.cloned.1.call-update) | async-done | bytes 7864336 | tf_op jit(solution)/shard_map/all_gather | solution.py:49
  206.9 12.9 %fusion = f32[512,2048]{1,0:T(8,128)} fusion(bf16[512,1024]{1,0:T(8,128)(2,1)S(1)} %get-tuple-element.14, bf16[512,1024]{1,0:T(8,128)(2,1)S(1)} %get-tuple-element.13, bf16[512,7680]{0,1:T(8,128)(2,1)} %all-gather.9.cloned.1.call-done, bf16[7680,512]{1,0:T(8,128)(2,1)} %param.16, f32[512]{0:T(512)S(1)} %convert_element_type.111), kind=kOutput, calls=%fused_computation.3 | convolution fusion | flops 5104992256 | bytes 22022144 | tf_op jit(solution)/shard_map/dot_general | solution.py:59
  220.1 31.5 %all-gather.13.cloned.1.call-done = bf16[64,8192]{1,0:T(8,128)(2,1)} async-done(((bf16[64,512]{1,0:T(8,128)(2,1)}), bf16[64,8192]{1,0:T(8,128)(2,1)}) %all-gather.13.cloned.1.call-update) | async-done | bytes 1048592 | tf_op jit(solution)/shard_map/all_gather | solution.py:84
  253.1 43.2 %all-gather.17.cloned.1.call-done = bf16[64,8192]{1,0:T(8,128)(2,1)} async-done(((bf16[64,512]{1,0:T(8,128)(2,1)}), bf16[64,8192]{1,0:T(8,128)(2,1)}) %all-gather.17.cloned.1.call-update) | async-done | bytes 1048592 | tf_op jit(solution)/shard_map/all_gather | solution.py:84
  297.8 79.0 %reduce-scatter.6.cloned.1.call-done = f32[32,2048]{1,0:T(8,128)} async-done(((f32[512,2048]{1,0:T(8,128)}), f32[32,2048]{1,0:T(8,128)}) %reduce-scatter.6.cloned.1.call-update) | async-done | bytes 262160 | tf_op jit(solution)/shard_map/reduce_scatter | solution.py:58
  379.0 63.4 %pmax.14 = f32[64,8,8]{0,2,1:T(8,128)S(1)} all-reduce(f32[64,8,8]{0,2,1:T(8,128)S(1)} %get-tuple-element.21), channel_id=1, replica_groups=mesh['group'=8,'tp'=16] {'tp'}, use_global_device_ids=true, to_apply=%region_5.6 | all-reduce | flops 4096 | bytes 32768 | tf_op jit(solution)/shard_map/pmax | solution.py:92
  442.3 1.5 fusion.9
  443.8 71.7 %pmax.15 = f32[64,8,8]{0,2,1:T(8,128)S(1)} all-reduce(f32[64,8,8]{0,2,1:T(8,128)S(1)} %get-tuple-element.8), channel_id=1, replica_groups=mesh['group'=8,'tp'=16] {'tp'}, use_global_device_ids=true, to_apply=%region_13.14 | all-reduce | flops 4096 | bytes 32768 | tf_op jit(solution)/shard_map/pmax | solution.py:92
  515.5 1.5 convolution_convert_fusion.2
  517.1 1.5 convolution_convert_fusion.3
  520.3 69.6 %all-reduce.3 = (bf16[64,64]{0,1:T(8,128)(2,1)S(1)}, bf16[64,64]{0,1:T(8,128)(2,1)S(1)}) all-reduce(bf16[64,64]{0,1:T(8,128)(2,1)S(1)} %bitcast.96, bf16[64,64]{0,1:T(8,128)(2,1)S(1)} %bitcast.97), channel_id=7, replica_groups=mesh['group'=8,'tp'=16] {'tp'}, use_global_device_ids=true, to_apply=%region_16.17.clone | all-reduce | flops 8192 | bytes 32768
  589.9 3.1 reduce-scatter.12.cloned.1.call-done
  593.0 6.0 convolution_convert_fusion
  599.1 69.4 %reduce-scatter.8.cloned.1.call-done = bf16[64,4,128]{2,0,1:T(8,128)(2,1)} async-done(((bf16[64,64,128]{2,0,1:T(8,128)(2,1)}), bf16[64,4,128]{2,0,1:T(8,128)(2,1)}) %reduce-scatter.8.cloned.1.call-update) | async-done | bytes 65552 | tf_op jit(solution)/shard_map/reduce_scatter | solution.py:103
  668.5 6.1 convolution_convert_fusion.1
  675.3 68.8 %reduce-scatter.14.cloned.1.call-done = bf16[64,512]{1,0:T(8,128)(2,1)} async-done(((bf16[64,8192]{1,0:T(8,128)(2,1)}), bf16[64,512]{1,0:T(8,128)(2,1)}) %reduce-scatter.14.cloned.1.call-update) | async-done | bytes 65552 | tf_op jit(solution)/shard_map/reduce_scatter | solution.py:116
  744.1 75.5 %reduce-scatter.10.cloned.1.call-done = bf16[64,512]{1,0:T(8,128)(2,1)} async-done(((bf16[64,8192]{1,0:T(8,128)(2,1)}), bf16[64,512]{1,0:T(8,128)(2,1)}) %reduce-scatter.10.cloned.1.call-update) | async-done | bytes 65552 | tf_op jit(solution)/shard_map/reduce_scatter | solution.py:116
  (66 shorter events, 15.9 us)
Async XLA Ops:
  6.5 40.2 %all-gather.7.cloned.1.call-start = ((), (), s32[]{:S(2)}) async-start(), calls=%async_computation.5 | async-start | bytes 4718592 | tf_op jit(solution)/shard_map/all_gather | solution.py:43
  7.3 84.5 %all-gather.11.cloned.1.call-start = ((), (), s32[]{:S(2)}) async-start(), calls=%async_computation.8 | async-start | bytes 1114112 | tf_op jit(solution)/shard_map/all_gather | solution.py:80
  44.4 92.3 %all-gather.15.cloned.1.call-start = ((), (), s32[]{:S(2)}) async-start(), calls=%async_computation.12 | async-start | bytes 1114112 | tf_op jit(solution)/shard_map/all_gather | solution.py:80
  45.1 161.8 %all-gather.9.cloned.1.call-start = ((), (), s32[]{:S(2)}) async-start(), calls=%async_computation.6 | async-start | bytes 8355840 | tf_op jit(solution)/shard_map/all_gather | solution.py:49
  49.6 48.2 %copy-start.1 = (bf16[512]{0:T(512)(128)(2,1)S(1)}, bf16[512]{0:T(512)(128)(2,1)}, u32[]{:S(2)}) copy-start(bf16[512]{0:T(512)(128)(2,1)} %param.17) | copy-start | bytes 3076
  49.6 202.0 %all-gather.13.cloned.1.call-start = ((), (), s32[]{:S(2)}) async-start(), calls=%async_computation.9 | async-start | bytes 1114112 | tf_op jit(solution)/shard_map/all_gather | solution.py:84
  97.7 198.6 %all-gather.17.cloned.1.call-start = ((), (), s32[]{:S(2)}) async-start(), calls=%async_computation.13 | async-start | bytes 1114112 | tf_op jit(solution)/shard_map/all_gather | solution.py:84
  142.6 234.3 %reduce-scatter.6.cloned.1.call-start = ((), (), s32[]{:S(2)}) async-start(), calls=%async_computation.7 | async-start | bytes 4456448 | tf_op jit(solution)/shard_map/reduce_scatter | solution.py:58
  206.9 12.9 %copy-start.4 = (s32[32]{0:T(128)S(1)}, s32[32]{0:T(128)}, u32[]{:S(2)}) copy-start(s32[32]{0:T(128)} %param.13) | copy-start | bytes 388
  206.9 13.2 %copy-start.2 = (s32[1,64]{1,0:T(1,128)S(1)}, s32[1,64]{1,0:T(1,128)}, u32[]{:S(2)}) copy-start(s32[1,64]{1,0:T(1,128)} %param.15) | copy-start | bytes 772
  219.7 373.3 %reduce-scatter.12.cloned.1.call-start = ((), (), s32[]{:S(2)}) async-start(), calls=%async_computation.14 | async-start | bytes 1114112 | tf_op jit(solution)/shard_map/reduce_scatter | solution.py:103
  253.1 265.6 %copy-start.5 = (u32[128]{0:T(128)S(1)}, u32[128]{0:T(128)}, u32[]{:S(2)}) copy-start(u32[128]{0:T(128)} %constant.90) | copy-start | bytes 1540
  517.1 151.5 %reduce-scatter.8.cloned.1.call-start = ((), (), s32[]{:S(2)}) async-start(), calls=%async_computation.10 | async-start | bytes 1114112 | tf_op jit(solution)/shard_map/reduce_scatter | solution.py:103
  518.7 225.5 %reduce-scatter.14.cloned.1.call-start = ((), (), s32[]{:S(2)}) async-start(), calls=%async_computation.15 | async-start | bytes 1114112 | tf_op jit(solution)/shard_map/reduce_scatter | solution.py:116
  599.0 220.6 %copy-start = (bf16[2,64,512]{2,1,0:T(8,128)(2,1)S(1)}, bf16[2,64,512]{2,1,0:T(8,128)(2,1)}, u32[]{:S(2)}) copy-start(bf16[2,64,512]{2,1,0:T(8,128)(2,1)} %param.23) | copy-start | bytes 393220
  599.1 220.6 %reduce-scatter.10.cloned.1.call-start = ((), (), s32[]{:S(2)}) async-start(), calls=%async_computation.11 | async-start | bytes 1114112 | tf_op jit(solution)/shard_map/reduce_scatter | solution.py:116
  820.6 0.7 copy-start.3
Sparse Core Ops, SparseCore 0:
  9.1 32.2 all-gather.6
  44.5 47.2 all-gather.10
  93.9 42.7 all-gather.14
  138.6 68.1 all-gather.8
  208.8 42.7 all-gather.12
  253.6 42.7 all-gather.16
  299.7 77.1 reduce-scatter.5
  517.2 75.7 reduce-scatter.11
  596.2 72.2 reduce-scatter.7
  671.9 72.1 reduce-scatter.13
  747.3 72.2 reduce-scatter.9
where the time goes:
time: 829 us; the launch traced here: 828 us
  waiting for transfers between devices  516 us (62%)
  blocking collectives  238 us (29%)
  matrix products  42.4 us (5%)
  between operations  14.8 us (2%)
  local copies, waits for them, and re-layouts  8.89 us (1%)
    reduce_scatter x2, waiting for transfers between devices, body(): lax.psum_scatter(branch.astype(jnp.bfloat16), 'tp', scatter_dimension=1,...  144 us
    pmax x2, blocking collectives, body(): largest = lax.pmax(local_top, 'tp')  135 us
    all_gather x2, waiting for transfers between devices, body(): lax.all_gather(normed, 'tp', axis=1, tiled=True)  79.3 us
    reduce_scatter x1, waiting for transfers between devices, body(): lax.psum_scatter(jnp.dot(projected, both_weights, preferred_element_type=...  79 us
    all_gather x2, waiting for transfers between devices, body(): lax.all_gather(own_query, 'tp', axis=1, tiled=True)  74.7 us
    reduce_scatter x2, waiting for transfers between devices, body(): lax.psum_scatter(summed.astype(jnp.bfloat16), 'tp', scatter_dimension=1,...  72.5 us
    unnamed x1, blocking collectives  69.6 us
    all_gather x1, waiting for transfers between devices, body(): lax.all_gather(ordered, 'tp', axis=1, tiled=True)  64.2 us
  transfers between devices with their start and end apart: 11, of which 10 were waited for; matrix products, arithmetic and copies ran while one was open for 6% of the time, Pallas kernels for 0%

commit v1 on v0

v1 whole, which is shorter than its diff:
```python
import functools

import jax
import jax.numpy as jnp
from jax import lax
from jax.experimental import pallas as pl
from jax.experimental.pallas import tpu as pltpu
from jax.sharding import Mesh, PartitionSpec as P

D = 8192
HEADS = 64
KV_HEADS = 8
HEAD_DIM = 128
MAXT = 4
STEPS = 2
F32 = jnp.float32
BF16 = jnp.bfloat16
TP = ("z", "xh", "pr")


def kv_kernel(rows_ref, key_ref, value_ref, out_ref):
    half = out_ref.shape[1]
    weight = jnp.concatenate([key_ref[0], value_ref[0]], axis=1)
    part = jnp.dot(rows_ref[...], weight, preferred_element_type=F32).astype(BF16)
    out_ref[0] = part[:half]
    out_ref[1] = part[half:]


def kv_partials(projected, kv_weight):
    rows, width = projected.shape
    return pl.pallas_call(
        kv_kernel,
        grid=(KV_HEADS,),
        in_specs=[
            pl.BlockSpec((rows, width), lambda h: (0, 0)),
            pl.BlockSpec((1, width, HEAD_DIM), lambda h: (0, 0, h)),
            pl.BlockSpec((1, width, HEAD_DIM), lambda h: (1, 0, h)),
        ],
        out_specs=pl.BlockSpec((2, rows // 2, 2 * HEAD_DIM), lambda h: (h, 0, 0)),
        out_shape=jax.ShapeDtypeStruct((2 * KV_HEADS, rows // 2, 2 * HEAD_DIM), BF16),
        compiler_params=pltpu.CompilerParams(vmem_limit_bytes=32 * 1024 * 1024),
        cost_estimate=pl.CostEstimate(
            flops=2 * rows * width * KV_HEADS * 2 * HEAD_DIM,
            bytes_accessed=8 * 1024 * 1024,
            transcendentals=0,
        ),
    )(projected, kv_weight, kv_weight)


def attend_kernel(query_ref, kv_ref, row_ref, col_ref, weight_ref, out_ref, context_ref):
    batch, width = context_ref.shape

    @pl.when(pl.program_id(0) == 0)
    def _():
        keys = kv_ref[:, :HEAD_DIM]
        values = kv_ref[:, HEAD_DIM:]
        allowed = row_ref[...] == col_ref[...]
        for head in range(width // HEAD_DIM):
            span = slice(head * HEAD_DIM, (head + 1) * HEAD_DIM)
            scores = lax.dot_general(
                query_ref[:, span], keys, (((1,), (1,)), ((), ())), preferred_element_type=F32
            ) * (1.0 / HEAD_DIM**0.5)
            scores = jnp.where(allowed, scores, -1e30)
            largest = jnp.max(scores, axis=1, keepdims=True)
            weights = jnp.where(allowed, jnp.exp(scores - largest), 0.0)
            total = jnp.sum(weights, axis=1, keepdims=True)
            summed = jnp.dot(weights.astype(BF16), values, preferred_element_type=F32)
            context_ref[:, span] = (summed / total).astype(BF16)

    out_ref[0] = jnp.dot(
        context_ref[...], weight_ref[...], preferred_element_type=F32
    ).astype(BF16)


def attend(query, kv, row_request, col_request, out_weight, ranks):
    batch, width = query.shape
    rows = kv.shape[0]
    columns = out_weight.shape[1] // ranks
    return pl.pallas_call(
        attend_kernel,
        grid=(ranks,),
        in_specs=[
            pl.BlockSpec((batch, width), lambda j: (0, 0)),
            pl.BlockSpec((rows, 2 * HEAD_DIM), lambda j: (0, 0)),
            pl.BlockSpec((batch, 1), lambda j: (0, 0)),
            pl.BlockSpec((1, rows), lambda j: (0, 0)),
            pl.BlockSpec((width, columns), lambda j: (0, j)),
        ],
        out_specs=pl.BlockSpec((1, batch, columns), lambda j: (j, 0, 0)),
        out_shape=jax.ShapeDtypeStruct((ranks, batch, columns), BF16),
        scratch_shapes=[pltpu.VMEM((batch, width), BF16)],
        compiler_params=pltpu.CompilerParams(vmem_limit_bytes=32 * 1024 * 1024),
        cost_estimate=pl.CostEstimate(
            flops=2 * batch * width * out_weight.shape[1],
            bytes_accessed=12 * 1024 * 1024,
            transcendentals=batch * rows * 4,
        ),
    )(query, kv, row_request, col_request, out_weight)


def body(
    vision_rows,
    tile_count,
    tile_source,
    row_request,
    proj_weight,
    proj_bias,
    kv_weight,
    query_weight,
    out_weight,
    norm_gain,
    attn_gate,
    states,
):
    groups = lax.axis_size("group")
    ranks = lax.axis_size(TP)
    group = lax.axis_index("group")
    tile_rows, features = vision_rows.shape[2:]
    per_group = vision_rows.shape[1] // groups
    slots = groups * per_group
    group_rows = slots * tile_rows
    req_grp = slots // MAXT
    batch = states.shape[1]
    width = states.shape[2]

    with jax.named_scope("gather_rows"):
        mine = vision_rows[0].reshape(groups, per_group, tile_rows, features)
        mine = mine.transpose(1, 0, 2, 3).reshape(group_rows, features)
        every = lax.all_gather(mine, TP, axis=1, tiled=True)

    with jax.named_scope("query"):
        local = states.reshape(STEPS * batch, width)
        gain_rows = jnp.broadcast_to(norm_gain[None, :], (16, width))
        sent = jnp.concatenate([local, gain_rows], axis=0)
        sent = jnp.broadcast_to(sent[None], (ranks,) + sent.shape)
        full = lax.all_to_all(sent, TP, 0, 0)
        hidden = full[:, : STEPS * batch].astype(F32)
        gain = full[:, STEPS * batch].astype(F32)
        squares = jnp.sum(hidden * hidden, axis=(0, 2))
        inverse = lax.rsqrt(squares / D + 1e-05)
        normed = (hidden * inverse[None, :, None] * gain[:, None, :]).astype(BF16)
        normed = normed.transpose(1, 0, 2).reshape(STEPS * batch, D)
        query = jnp.dot(normed, query_weight, preferred_element_type=F32).astype(BF16)

    with jax.named_scope("project"):
        accum = jnp.dot(every, proj_weight, preferred_element_type=F32)
        projected = (accum + proj_bias.astype(F32)).astype(BF16)

    with jax.named_scope("kv"):
        partial = kv_partials(projected, kv_weight)
        partial = lax.all_to_all(partial, TP, 0, 0)
        kv = jnp.sum(partial.astype(F32), axis=0).astype(BF16)
        kv = kv.reshape(groups, 1, tile_rows, 2 * HEAD_DIM)
        kv = jnp.broadcast_to(kv, (groups, 2, tile_rows, 2 * HEAD_DIM))
        kv = kv.reshape(slots, tile_rows, 2 * HEAD_DIM)
        kv = lax.all_to_all(kv, ("group", "pr"), 0, 0)
        kv = kv.reshape(group_rows, 2 * HEAD_DIM)

    with jax.named_scope("mask"):
        sources = lax.dynamic_index_in_dim(tile_source, group, 0, keepdims=False)
        counts = lax.dynamic_slice_in_dim(tile_count, group * req_grp, req_grp, 0)
        places = jnp.arange(slots, dtype=jnp.int32)
        request = places // MAXT
        valid = places % MAXT < jnp.repeat(counts, MAXT)
        label = jnp.where(valid, request, -1)
        hits = sources[None, :] == places[:, None]
        tile_label = jnp.sum(jnp.where(hits, label[None, :], 0), axis=1)
        col_request = jnp.repeat(tile_label, tile_rows)[None, :]
        rows = jnp.concatenate([row_request[0]] * STEPS)[:, None]

    with jax.named_scope("attend"):
        branch = attend(query, kv, rows, col_request, out_weight, ranks)

    with jax.named_scope("mix"):
        branch = lax.all_to_all(branch, TP, 0, 0)
        reduced = jnp.sum(branch.astype(F32), axis=0)
        mixed = local.astype(F32) + jnp.tanh(attn_gate) * reduced
        return mixed.astype(BF16).reshape(STEPS, batch, width)


def solution(mesh):
    groups = mesh.shape["group"]
    split = Mesh(mesh.devices.reshape(groups, 4, 2, 2), ("group",) + TP)
    in_specs = (
        P("group", None, None, TP),
        P(),
        P(),
        P("group", None),
        P(None, TP),
        P(TP),
        P(None, TP, None),
        P(None, TP),
        P(TP, None),
        P(TP),
        P(),
        P(None, "group", TP),
    )
    out_specs = P(None, "group", TP)
    return jax.shard_map(body, mesh=split, in_specs=in_specs, out_specs=out_specs, check_vma=False)
```

time: 829 us -> 226 us (0.27)
  the two profiles are of different devices: /device:TPU:30 before, /device:TPU:0 now
where the time goes in v1:
time: 226 us
  waiting for transfers between devices  138 us (61%)
  starting transfers between devices  22.2 us (10%)
  local copies, waits for them, and re-layouts  17.5 us (8%)
  matrix products  14.4 us (6%)
  between operations  14.3 us (6%)
  Pallas kernels  12.1 us (5%)
  other arithmetic  7.37 us (3%)
    all_gather x1, waiting for transfers between devices, body(): every = lax.all_gather(mine, TP, axis=1, tiled=True)  82.2 us
    all_to_all x1, waiting for transfers between devices, body(): branch = lax.all_to_all(branch, TP, 0, 0)  32.4 us
    all_to_all x1, waiting for transfers between devices, body(): partial = lax.all_to_all(partial, TP, 0, 0)  20.5 us
    dot_general x1, matrix products, body(): accum = jnp.dot(every, proj_weight, preferred_element_type=F32)  9.71 us
    pallas_call x1, Pallas kernels, attend(): pl.pallas_call(attend_kernel, grid=(ranks,), in_specs=[pl.BlockSpec((batc...  9 us
    all_to_all x1, starting transfers between devices, body(): full = lax.all_to_all(sent, TP, 0, 0)  8.01 us
    unnamed x19, local copies, waits for them, and re-layouts  7.78 us
    all_to_all x1, starting transfers between devices, body(): partial = lax.all_to_all(partial, TP, 0, 0)  5.29 us
  transfers between devices with their start and end apart: 5, of which 4 were waited for; matrix products, arithmetic and copies ran while one was open for 13% of the time, Pallas kernels for 1%

profile of v1, /device:TPU:0, one launch (start us, length us, event | category | flops | bytes accessed | tf_op | source)
XLA Modules:
  0.0 225.6 jit_solution(14034046945432714248)
XLA Ops:
  6.5 1.1 copy.27
  7.6 1.0 copy.28
  9.4 0.9 pad_maximum_fusion
  10.3 1.6 broadcast_in_dim.29
  11.9 8.0 %all-to-all-start = ((bf16[16,144,512]{2,1,0:T(8,128)(2,1)}), bf16[16,144,512]{2,1,0:T(8,128)(2,1)}, u32[]{:S(2)}, u32[]{:S(2)}) async-start(bf16[16,144,512]{2,1,0:T(8,128)(2,1)} %broadcast_in_dim.29), calls=%async_computation | async-start | bytes 4718592 | tf_op jit(solution)/shard_map/query/all_to_all | solution.py:136
  19.9 82.2 %all-gather.2.cloned.1.call-done = bf16[512,7680]{0,1:T(8,128)(2,1)} async-done(((bf16[512,480]{0,1:T(8,128)(2,1)}), bf16[512,7680]{0,1:T(8,128)(2,1)}) %all-gather.2.cloned.1.call-update) | async-done | bytes 7864336 | tf_op jit(solution)/shard_map/gather_rows/all_gather | solution.py:129
  102.2 9.7 %fusion.3.rows_ref = bf16[512,512]{1,0:T(8,128)(2,1)S(1)} fusion(bf16[512,7680]{0,1:T(8,128)(2,1)} %all-gather.2.cloned.1.call-done, bf16[7680,512]{1,0:T(8,128)(2,1)} %param.16, f32[512]{0:T(512)S(1)} %convert_element_type.34), kind=kOutput, calls=%fused_computation.7 | convolution fusion | flops 4027056128 | bytes 16254976 | tf_op jit(solution)/shard_map/project/dot_general | solution.py:146
  111.9 3.1 %kv.1 = bf16[16,256,256]{2,1,0:T(8,128)(2,1)S(1)} custom-call(bf16[512,512]{1,0:T(8,128)(2,1)S(1)} %fusion.3.rows_ref, bf16[2,512,1024]{2,1,0:T(8,128)(2,1)S(1)} %copy-done.2, bf16[2,512,1024]{2,1,0:T(8,128)(2,1)S(1)} %copy-done.2), custom_call_target="tpu_custom_call" | custom-call | flops 1073741824 | bytes 8388608 | tf_op jit(solution)/shard_map/kv/pallas_call | solution.py:31
  115.0 1.3 copy-done.3
  116.3 5.3 %all-to-all-start.1 = ((bf16[16,256,256]{2,1,0:T(8,128)(2,1)}), bf16[16,256,256]{2,1,0:T(8,128)(2,1)}, u32[]{:S(2)}, u32[]{:S(2)}) async-start(bf16[16,256,256]{2,1,0:T(8,128)(2,1)} %copy-done.3), calls=%async_computation.1 | async-start | bytes 4194304 | tf_op jit(solution)/shard_map/kv/all_to_all | solution.py:151
  122.4 3.1 %slice.8 = bf16[16,128,512]{2,1,0:T(8,128)(2,1)} slice(bf16[16,144,512]{2,1,0:T(8,128)(2,1)} %all-to-all-done), slice={[0:16], [0:128], [0:512]} | slice | bytes 4194304 | tf_op jit(solution)/shard_map/query/slice | solution.py:137
  125.5 3.0 %copy.30 = bf16[16,128,512]{1,2,0:T(8,128)(2,1)S(1)} copy(bf16[16,128,512]{2,1,0:T(8,128)(2,1)} %slice.8) | data formatting | bytes 4194304
  128.5 0.9 slice.9
  129.5 1.1 fusion
  130.6 2.3 %fusion.2 = bf16[16,128,512]{1,2,0:T(8,128)(2,1)} fusion(bf16[16,128,512]{1,2,0:T(8,128)(2,1)S(1)} %copy.30, f32[16,512]{1,0:T(8,128)S(1)} %fusion.4, f32[128]{0:T(128)S(1)} %add_rsqrt_fusion), kind=kLoop, calls=%fused_computation.4 | loop fusion | flops 4194304 | bytes 4227584 | tf_op jit(solution)/shard_map/query/convert_element_type | solution.py:141
  132.8 20.5 %all-to-all-done.1 = bf16[16,256,256]{2,1,0:T(8,128)(2,1)} async-done(((bf16[16,256,256]{2,1,0:T(8,128)(2,1)}), bf16[16,256,256]{2,1,0:T(8,128)(2,1)}, u32[]{:S(2)}, u32[]{:S(2)}) %all-to-all-start.1) | async-done | bytes 2097184 | tf_op jit(solution)/shard_map/kv/all_to_all | solution.py:151
  153.4 1.9 reduce_sum.40
  156.0 4.3 %all-to-all-start.2 = ((bf16[16,32,256]{2,1,0:T(8,128)(2,1)}), bf16[16,32,256]{2,1,0:T(8,128)(2,1)S(1)}, u32[]{:S(2)}, u32[]{:S(2)}) async-start(bf16[16,32,256]{2,1,0:T(8,128)(2,1)} %bitcast.8), calls=%async_computation.2 | async-start | bytes 524288 | tf_op jit(solution)/shard_map/kv/all_to_all | solution.py:156
  160.3 4.7 %convolution_convert_fusion.query_ref = bf16[128,512]{1,0:T(8,128)(2,1)S(1)} fusion(bf16[128,8192]{0,1:T(8,128)(2,1)S(1)} %bitcast.27, bf16[8192,512]{1,0:T(8,128)(2,1)} %param.19), kind=kOutput, calls=%fused_computation.8 | convolution fusion | flops 1073807360 | bytes 10616832 | tf_op jit(solution)/shard_map/query/dot_general | solution.py:143
  165.0 2.7 %all-to-all-done.2 = bf16[16,32,256]{2,1,0:T(8,128)(2,1)S(1)} async-done(((bf16[16,32,256]{2,1,0:T(8,128)(2,1)}), bf16[16,32,256]{2,1,0:T(8,128)(2,1)S(1)}, u32[]{:S(2)}, u32[]{:S(2)}) %all-to-all-start.2) | async-done | bytes 262176 | tf_op jit(solution)/shard_map/kv/all_to_all | solution.py:156
  167.7 3.4 %copy-done.1 = bf16[512,8192]{1,0:T(8,128)(2,1)S(1)} copy-done((bf16[512,8192]{1,0:T(8,128)(2,1)S(1)}, bf16[512,8192]{1,0:T(8,128)(2,1)}, u32[]{:S(2)}) %copy-start.1) | copy-done | bytes 8388632
  171.1 9.0 %attend.1 = bf16[16,128,512]{2,1,0:T(8,128)(2,1)} custom-call(bf16[128,512]{1,0:T(8,128)(2,1)S(1)} %convolution_convert_fusion.query_ref, bf16[512,256]{1,0:T(8,128)(2,1)S(1)} %bitcast.26, s32[128,1]{1,0:T(8,128)S(1)} %copy.29.row_ref, s32[1,512]{1,0:T(1,128)S(1)} %reshape.67.col_ref, bf16[512,8192]{1,0:T(8,128)(2,1)S(1)} %copy-done.1), custom_call_target="tpu_custom_call" | custom-call | flops 1073741824 | bytes 12582912 | tf_op jit(solution)/shard_map/attend/pallas_call | solution.py:79
  180.1 4.6 %all-to-all-start.3 = ((bf16[16,128,512]{2,1,0:T(8,128)(2,1)}), bf16[16,128,512]{2,1,0:T(8,128)(2,1)S(1)}, u32[]{:S(2)}, u32[]{:S(2)}) async-start(bf16[16,128,512]{2,1,0:T(8,128)(2,1)} %attend.1), calls=%async_computation.3 | async-start | bytes 4194304 | tf_op jit(solution)/shard_map/mix/all_to_all | solution.py:175
  185.4 32.4 %all-to-all-done.3 = bf16[16,128,512]{2,1,0:T(8,128)(2,1)S(1)} async-done(((bf16[16,128,512]{2,1,0:T(8,128)(2,1)}), bf16[16,128,512]{2,1,0:T(8,128)(2,1)S(1)}, u32[]{:S(2)}, u32[]{:S(2)}) %all-to-all-start.3) | async-done | bytes 2097184 | tf_op jit(solution)/shard_map/mix/all_to_all | solution.py:175
  (37 shorter events, 3.2 us)
Async XLA Ops:
  6.5 115.6 %copy-start = (s32[8,16]{1,0:T(8,128)S(1)}, s32[8,16]{1,0:T(8,128)}, u32[]{:S(2)}) copy-start(s32[8,16]{1,0:T(8,128)} %param.14) | copy-start | bytes 1540
  6.5 95.6 %all-gather.2.cloned.1.call-start = ((), (), s32[]{:S(2)}) async-start(), calls=%async_computation.4 | async-start | bytes 8355840 | tf_op jit(solution)/shard_map/gather_rows/all_gather | solution.py:129
  8.6 11.3 %copy-start.6 = (bf16[512]{0:T(512)(128)(2,1)S(1)}, bf16[512]{0:T(512)(128)(2,1)}, u32[]{:S(2)}) copy-start(bf16[512]{0:T(512)(128)(2,1)} %param.17) | copy-start | bytes 3076
  11.9 104.4 %all-to-all-start = ((bf16[16,144,512]{2,1,0:T(8,128)(2,1)}), bf16[16,144,512]{2,1,0:T(8,128)(2,1)}, u32[]{:S(2)}, u32[]{:S(2)}) async-start(bf16[16,144,512]{2,1,0:T(8,128)(2,1)} %broadcast_in_dim.29), calls=%async_computation | async-start | bytes 4718592 | tf_op jit(solution)/shard_map/query/all_to_all | solution.py:136
  19.9 91.9 %copy-start.2 = (bf16[2,512,1024]{2,1,0:T(8,128)(2,1)S(1)}, bf16[2,512,1024]{2,1,0:T(8,128)(2,1)}, u32[]{:S(2)}) copy-start(bf16[2,512,1024]{2,1,0:T(8,128)(2,1)} %value_ref.1) | copy-start | bytes 6291460
  111.9 9.8 %copy-start.7 = (s32[1,64]{1,0:T(1,128)S(1)}, s32[1,64]{1,0:T(1,128)}, u32[]{:S(2)}) copy-start(s32[1,64]{1,0:T(1,128)} %param.15) | copy-start | bytes 772
  111.9 9.9 %copy-start.8 = (s32[32]{0:T(128)S(1)}, s32[32]{0:T(128)}, u32[]{:S(2)}) copy-start(s32[32]{0:T(128)} %param.13) | copy-start | bytes 388
  115.0 1.3 copy-start.3
  116.3 37.0 %all-to-all-start.1 = ((bf16[16,256,256]{2,1,0:T(8,128)(2,1)}), bf16[16,256,256]{2,1,0:T(8,128)(2,1)}, u32[]{:S(2)}, u32[]{:S(2)}) async-start(bf16[16,256,256]{2,1,0:T(8,128)(2,1)} %copy-done.3), calls=%async_computation.1 | async-start | bytes 4194304 | tf_op jit(solution)/shard_map/kv/all_to_all | solution.py:151
  132.8 27.5 %copy-start.4 = (bf16[16,128,512]{1,2,0:T(8,128)(2,1)S(1)}, bf16[16,128,512]{1,2,0:T(8,128)(2,1)}, u32[]{:S(2)}) copy-start(bf16[16,128,512]{1,2,0:T(8,128)(2,1)} %fusion.2) | copy-start | bytes 6291460
  156.0 11.8 %all-to-all-start.2 = ((bf16[16,32,256]{2,1,0:T(8,128)(2,1)}), bf16[16,32,256]{2,1,0:T(8,128)(2,1)S(1)}, u32[]{:S(2)}, u32[]{:S(2)}) async-start(bf16[16,32,256]{2,1,0:T(8,128)(2,1)} %bitcast.8), calls=%async_computation.2 | async-start | bytes 524288 | tf_op jit(solution)/shard_map/kv/all_to_all | solution.py:156
  167.7 3.4 %copy-start.1 = (bf16[512,8192]{1,0:T(8,128)(2,1)S(1)}, bf16[512,8192]{1,0:T(8,128)(2,1)}, u32[]{:S(2)}) copy-start(bf16[512,8192]{1,0:T(8,128)(2,1)} %weight_ref.1) | copy-start | bytes 25165828
  180.1 38.0 %copy-start.5 = (bf16[2,64,512]{2,1,0:T(8,128)(2,1)S(1)}, bf16[2,64,512]{2,1,0:T(8,128)(2,1)}, u32[]{:S(2)}) copy-start(bf16[2,64,512]{2,1,0:T(8,128)(2,1)} %param.23) | copy-start | bytes 393220
  180.1 37.7 %all-to-all-start.3 = ((bf16[16,128,512]{2,1,0:T(8,128)(2,1)}), bf16[16,128,512]{2,1,0:T(8,128)(2,1)S(1)}, u32[]{:S(2)}, u32[]{:S(2)}) async-start(bf16[16,128,512]{2,1,0:T(8,128)(2,1)} %attend.1), calls=%async_computation.3 | async-start | bytes 4194304 | tf_op jit(solution)/shard_map/mix/all_to_all | solution.py:175
Sparse Core Ops, SparseCore 0:
  9.5 92.6 all-gather.1

commit v2 on v1

v2 whole, which is shorter than its diff:
```python
import functools

import jax
import jax.numpy as jnp
from jax import lax
from jax.experimental import pallas as pl
from jax.experimental.pallas import tpu as pltpu
from jax.sharding import Mesh, PartitionSpec as P

D = 8192
HEADS = 64
KV_HEADS = 8
HEAD_DIM = 128
MAXT = 4
STEPS = 2
SIDE = 4
F32 = jnp.float32
BF16 = jnp.bfloat16
TP = ("z", "xh", "pr")
X = ("xh", "pr")
Z = "z"
VMEM = 40 * 1024 * 1024


def shift(value, axis, by):
    return lax.ppermute(value, axis, [(i, (i + by) % SIDE) for i in range(SIDE)])


def project_kernel(spans, final, index_ref, *refs):
    blocks = refs[: len(spans)]
    weight_ref, start_ref, out_ref, accum_ref = refs[len(spans) :]
    step = pl.program_id(0)

    @pl.when(step == 0)
    def _():
        accum_ref[...] = jnp.broadcast_to(start_ref[...], accum_ref.shape)

    for block, (begin, count, half) in zip(blocks, spans):

        @pl.when((step >= begin) & (step < begin + count))
        def _():
            accum_ref[half] += jnp.dot(block[0], weight_ref[0], preferred_element_type=F32)

    @pl.when(step == pl.num_programs(0) - 1)
    def _():
        out_ref[...] = accum_ref[...].astype(out_ref.dtype)


def project(start, blocks, halves, index, weight, final):
    rows, features = blocks[0].shape[1:]
    width = weight.shape[2]
    spans, begin = [], 0
    for block, half in zip(blocks, halves):
        spans.append((begin, block.shape[0], half))
        begin += block.shape[0]
    shape = (2, rows, width)

    def block_spec(begin, count):
        return pl.BlockSpec(
            (1, rows, features), lambda i, _: (jnp.clip(i - begin, 0, count - 1), 0, 0)
        )

    whole = lambda i, _: (0, 0, 0)
    return pl.pallas_call(
        functools.partial(project_kernel, spans, final),
        grid_spec=pltpu.PrefetchScalarGridSpec(
            num_scalar_prefetch=1,
            grid=(begin,),
            in_specs=[block_spec(at, count) for at, count, _ in spans]
            + [
                pl.BlockSpec((1, features, width), lambda i, index: (index[i], 0, 0)),
                pl.BlockSpec(start.shape, whole),
            ],
            out_specs=pl.BlockSpec(shape, whole),
            scratch_shapes=[pltpu.VMEM(shape, F32)],
        ),
        out_shape=jax.ShapeDtypeStruct(shape, BF16 if final else F32),
        compiler_params=pltpu.CompilerParams(vmem_limit_bytes=VMEM),
        cost_estimate=pl.CostEstimate(
            flops=2 * begin * rows * features * width,
            bytes_accessed=2 * begin * (rows + width) * features,
            transcendentals=0,
        ),
    )(index, *blocks, weight, start)


def kv_kernel(index_ref, rows_ref, key_ref, value_ref, keys_ref, values_ref):
    rows = rows_ref[0]
    keys_ref[0, 0] = jnp.dot(rows, key_ref[0], preferred_element_type=F32).astype(BF16)
    values_ref[0, 0] = jnp.dot(rows, value_ref[0], preferred_element_type=F32).astype(BF16)


def kv_partials(index, projected, kv_weight):
    _, rows, width = projected.shape
    out_shape = jax.ShapeDtypeStruct((SIDE, SIDE, rows, HEAD_DIM), BF16)
    return pl.pallas_call(
        kv_kernel,
        grid_spec=pltpu.PrefetchScalarGridSpec(
            num_scalar_prefetch=1,
            grid=(SIDE, SIDE),
            in_specs=[
                pl.BlockSpec((1, rows, width), lambda a, b, index: (index[a * SIDE + b] % 2, 0, 0)),
                pl.BlockSpec(
                    (1, width, HEAD_DIM), lambda a, b, index: (0, 0, index[a * SIDE + b] // 2)
                ),
                pl.BlockSpec(
                    (1, width, HEAD_DIM), lambda a, b, index: (1, 0, index[a * SIDE + b] // 2)
                ),
            ],
            out_specs=[
                pl.BlockSpec((1, 1, rows, HEAD_DIM), lambda a, b, _: (a, b, 0, 0)),
                pl.BlockSpec((1, 1, rows, HEAD_DIM), lambda a, b, _: (b, a, 0, 0)),
            ],
        ),
        out_shape=[out_shape, out_shape],
        compiler_params=pltpu.CompilerParams(vmem_limit_bytes=VMEM),
        cost_estimate=pl.CostEstimate(
            flops=2 * 32 * rows * width * HEAD_DIM,
            bytes_accessed=8 * 1024 * 1024,
            transcendentals=0,
        ),
    )(index, projected, kv_weight, kv_weight)


def query_kernel(full_ref, weight_ref, out_ref, inverse_ref, accum_ref):
    batch = out_ref.shape[0]
    step = pl.program_id(0)
    steps = pl.num_programs(0)

    @pl.when(step == 0)
    def _():
        total = jnp.zeros((batch, 1), F32)
        for rank in range(full_ref.shape[0]):
            hidden = full_ref[rank, :batch].astype(F32)
            total += jnp.sum(hidden * hidden, axis=1, keepdims=True)
        inverse_ref[...] = lax.rsqrt(total / D + 1e-05)
        accum_ref[...] = jnp.zeros_like(accum_ref)

    hidden = full_ref[step, :batch].astype(F32)
    gain = full_ref[step, batch : batch + 16].astype(F32)[:1]
    normed = (hidden * inverse_ref[...] * gain).astype(BF16)
    accum_ref[...] += jnp.dot(normed, weight_ref[...], preferred_element_type=F32)

    @pl.when(step == steps - 1)
    def _():
        out_ref[...] = accum_ref[...].astype(BF16)


def queries(full, query_weight, batch):
    ranks, rows, width = full.shape
    columns = query_weight.shape[1]
    return pl.pallas_call(
        query_kernel,
        grid=(ranks,),
        in_specs=[
            pl.BlockSpec((ranks, rows, width), lambda i: (0, 0, 0)),
            pl.BlockSpec((width, columns), lambda i: (i, 0)),
        ],
        out_specs=pl.BlockSpec((batch, columns), lambda i: (0, 0)),
        out_shape=jax.ShapeDtypeStruct((batch, columns), BF16),
        scratch_shapes=[pltpu.VMEM((batch, 1), F32), pltpu.VMEM((batch, columns), F32)],
        compiler_params=pltpu.CompilerParams(vmem_limit_bytes=VMEM),
        cost_estimate=pl.CostEstimate(
            flops=2 * batch * ranks * width * columns,
            bytes_accessed=12 * 1024 * 1024,
            transcendentals=0,
        ),
    )(full, query_weight)


def attend_kernel(
    index_ref, query_ref, kv_ref, row_ref, col_ref, weight_ref, first_ref, second_ref, context_ref
):
    batch, width = context_ref.shape

    @pl.when((pl.program_id(0) == 0) & (pl.program_id(1) == 0))
    def _():
        keys = kv_ref[:, :HEAD_DIM]
        values = kv_ref[:, HEAD_DIM:]
        allowed = row_ref[...] == col_ref[...]
        for head in range(width // HEAD_DIM):
            span = slice(head * HEAD_DIM, (head + 1) * HEAD_DIM)
            scores = lax.dot_general(
                query_ref[:, span], keys, (((1,), (1,)), ((), ())), preferred_element_type=F32
            ) * (1.0 / HEAD_DIM**0.5)
            scores = jnp.where(allowed, scores, -1e30)
            largest = jnp.max(scores, axis=1, keepdims=True)
            weights = jnp.where(allowed, jnp.exp(scores - largest), 0.0)
            total = jnp.sum(weights, axis=1, keepdims=True)
            summed = jnp.dot(weights.astype(BF16), values, preferred_element_type=F32)
            context_ref[:, span] = (summed / total).astype(BF16)

    branch = jnp.dot(context_ref[...], weight_ref[...], preferred_element_type=F32).astype(BF16)
    half = branch.shape[1] // 2
    first_ref[0, 0] = branch[:, :half]
    second_ref[0, 0] = branch[:, half:]


def attend(index, query, kv, row_request, col_request, out_weight):
    batch, width = query.shape
    rows = kv.shape[0]
    columns = out_weight.shape[1] // (SIDE * SIDE)
    half = columns // 2
    out_shape = jax.ShapeDtypeStruct((SIDE, SIDE, batch, half), BF16)
    fixed = lambda a, b, _: (0, 0)
    return pl.pallas_call(
        attend_kernel,
        grid_spec=pltpu.PrefetchScalarGridSpec(
            num_scalar_prefetch=1,
            grid=(SIDE, SIDE),
            in_specs=[
                pl.BlockSpec((batch, width), fixed),
                pl.BlockSpec((rows, 2 * HEAD_DIM), fixed),
                pl.BlockSpec((batch, 1), fixed),
                pl.BlockSpec((1, rows), fixed),
                pl.BlockSpec((width, columns), lambda a, b, index: (0, index[a * SIDE + b])),
            ],
            out_specs=[
                pl.BlockSpec((1, 1, batch, half), lambda a, b, _: (a, b, 0, 0)),
                pl.BlockSpec((1, 1, batch, half), lambda a, b, _: (b, a, 0, 0)),
            ],
            scratch_shapes=[pltpu.VMEM((batch, width), BF16)],
        ),
        out_shape=[out_shape, out_shape],
        compiler_params=pltpu.CompilerParams(vmem_limit_bytes=VMEM),
        cost_estimate=pl.CostEstimate(
            flops=2 * batch * width * out_weight.shape[1],
            bytes_accessed=12 * 1024 * 1024,
            transcendentals=batch * rows * 4,
        ),
    )(index, query, kv, row_request, col_request, out_weight)


def sum_phase(blocks, axis):
    arrived = [blocks[0]] + [shift(blocks[by], axis, by) for by in range(1, SIDE)]
    total = arrived[0].astype(F32)
    for block in arrived[1:]:
        total += block.astype(F32)
    return total


def gather_phase(block, axis):
    return [block] + [shift(block, axis, by) for by in (1, 3, 2)]


def forward_phase(stacked, axis):
    after = shift(stacked, axis, 1)
    before = shift(stacked, axis, 3)
    middle = stacked.shape[0] // 2
    return after, before, shift(after[:middle], axis, 1), shift(before[middle:], axis, 3)


def body(
    vision_rows,
    tile_count,
    tile_source,
    row_request,
    proj_weight,
    proj_bias,
    kv_weight,
    query_weight,
    out_weight,
    norm_gain,
    attn_gate,
    states,
):
    groups = lax.axis_size("group")
    ranks = lax.axis_size(TP)
    group = lax.axis_index("group")
    along_z = lax.axis_index(Z)
    along_x = lax.axis_index(X)
    tile_rows, features = vision_rows.shape[2:]
    per_group = vision_rows.shape[1] // groups
    slots = groups * per_group
    group_rows = slots * tile_rows
    half_rows = group_rows // 2
    req_grp = slots // MAXT
    batch = states.shape[1]
    width = states.shape[2]

    with jax.named_scope("gather_states"):
        local = states.reshape(STEPS * batch, width)
        gain_rows = jnp.broadcast_to(norm_gain[None, :], (16, width))
        full = lax.all_gather(jnp.concatenate([local, gain_rows], axis=0), TP)

    with jax.named_scope("gather_rows"):
        mine = vision_rows[0].reshape(groups, per_group, tile_rows, features)
        rows_a = gather_phase(mine[:, 0].reshape(half_rows, features), X)
        rows_b = gather_phase(mine[:, 1].reshape(half_rows, features), Z)
        stack_a = jnp.stack(rows_a)
        stack_b = jnp.stack(rows_b)
        far_a = forward_phase(stack_a, Z)
        far_b = forward_phase(stack_b, X)

    with jax.named_scope("project"):
        weight = proj_weight.reshape(ranks, features, proj_weight.shape[1])
        hops = jnp.array([0, 1, 3, 2], jnp.int32)

        def feature_blocks(z_hops, x_hops):
            return (along_z - z_hops) % SIDE * SIDE + (along_x - x_hops) % SIDE

        def both(far, chosen):
            return jnp.concatenate(
                [feature_blocks(far, chosen), feature_blocks(chosen, far)]
            ).astype(jnp.int32)

        start = proj_bias.astype(F32).reshape(1, 1, -1)
        accum = project(start, [stack_a, stack_b], (0, 1), both(0, hops), weight, False)
        accum = project(accum, [far_a[0], far_b[0]], (0, 1), both(1, hops), weight, False)
        accum = project(accum, [far_a[1], far_b[1]], (0, 1), both(3, hops), weight, False)
        projected = project(
            accum,
            [far_a[2], far_a[3], far_b[2], far_b[3]],
            (0, 0, 1, 1),
            both(2, hops),
            weight,
            True,
        )

    with jax.named_scope("kv"):
        steps = jnp.arange(SIDE, dtype=jnp.int32)
        targets = (along_z + steps[:, None]) % SIDE * SIDE + (along_x + steps[None, :]) % SIDE
        targets = targets.reshape(-1).astype(jnp.int32)
        part_keys, part_values = kv_partials(targets, projected, kv_weight)
        keys = sum_phase(part_keys, Z).astype(BF16)
        values = sum_phase(part_values, X).astype(BF16)
        keys = sum_phase(keys, X).astype(BF16)
        values = sum_phase(values, Z).astype(BF16)
        kv = jnp.concatenate([keys, values], axis=1)
        kv = kv.reshape(groups, 1, tile_rows, 2 * HEAD_DIM)
        kv = jnp.broadcast_to(kv, (groups, 2, tile_rows, 2 * HEAD_DIM))
        kv = kv.reshape(slots, tile_rows, 2 * HEAD_DIM)
        kv = lax.all_to_all(kv, ("group", "pr"), 0, 0)
        kv = kv.reshape(group_rows, 2 * HEAD_DIM)

    with jax.named_scope("query"):
        query = queries(full, query_weight, STEPS * batch)

    with jax.named_scope("mask"):
        sources = lax.dynamic_index_in_dim(tile_source, group, 0, keepdims=False)
        counts = lax.dynamic_slice_in_dim(tile_count, group * req_grp, req_grp, 0)
        places = jnp.arange(slots, dtype=jnp.int32)
        request = places // MAXT
        valid = places % MAXT < jnp.repeat(counts, MAXT)
        label = jnp.where(valid, request, -1)
        hits = sources[None, :] == places[:, None]
        tile_label = jnp.sum(jnp.where(hits, label[None, :], 0), axis=1)
        col_request = jnp.repeat(tile_label, tile_rows)[None, :]
        rows = jnp.concatenate([row_request[0]] * STEPS)[:, None]

    with jax.named_scope("attend"):
        first, second = attend(targets, query, kv, rows, col_request, out_weight)

    with jax.named_scope("mix"):
        first = sum_phase(first, Z).astype(BF16)
        second = sum_phase(second, X).astype(BF16)
        first = sum_phase(first, X)
        second = sum_phase(second, Z)
        reduced = jnp.concatenate([first, second], axis=1)
        mixed = local.astype(F32) + jnp.tanh(attn_gate) * reduced
        return mixed.astype(BF16).reshape(STEPS, batch, width)


def solution(mesh):
    groups = mesh.shape["group"]
    split = Mesh(mesh.devices.reshape(groups, SIDE, 2, 2), ("group",) + TP)
    in_specs = (
        P("group", None, None, TP),
        P(),
        P(),
        P("group", None),
        P(None, TP),
        P(TP),
        P(None, TP, None),
        P(None, TP),
        P(TP, None),
        P(TP),
        P(),
        P(None, "group", TP),
    )
    out_specs = P(None, "group", TP)
    return jax.shard_map(body, mesh=split, in_specs=in_specs, out_specs=out_specs, check_vma=False)
```

time: 226 us -> 195 us (0.86)
  the two profiles are of different devices: /device:TPU:0 before, /device:TPU:30 now
where the time goes in v2:
time: 195 us; the launch traced here: 192 us
  starting transfers between devices  56.4 us (29%)
  waiting for transfers between devices  46.5 us (24%)
  local copies, waits for them, and re-layouts  35.9 us (18%)
  Pallas kernels  34.1 us (17%)
  between operations  14.5 us (7%)
  other arithmetic  4.59 us (2%)
    ppermute x38, starting transfers between devices, shift(): lax.ppermute(value, axis, [(i, (i + by) % SIDE) for i in range(SIDE)])  50.8 us
    ppermute x38, waiting for transfers between devices, shift(): lax.ppermute(value, axis, [(i, (i + by) % SIDE) for i in range(SIDE)])  46.5 us
    pallas_call x4, Pallas kernels, project(): pl.pallas_call(functools.partial(project_kernel, spans, final), grid_spec...  15.6 us
    unnamed x28, local copies, waits for them, and re-layouts  14.9 us
    ppermute x4, local copies, waits for them, and re-layouts, shift(): lax.ppermute(value, axis, [(i, (i + by) % SIDE) for i in range(SIDE)])  8.29 us
    pallas_call x1, Pallas kernels, kv_partials(): pl.pallas_call(kv_kernel, grid_spec=pltpu.PrefetchScalarGridSpec(num_scal...  6.86 us
    pallas_call x1, Pallas kernels, attend(): pl.pallas_call(attend_kernel, grid_spec=pltpu.PrefetchScalarGridSpec(num_...  6.52 us
    all_to_all x1, starting transfers between devices, body(): kv = lax.all_to_all(kv, ('group', 'pr'), 0, 0)  5.62 us
  transfers between devices with their start and end apart: 40, of which 15 were waited for; matrix products, arithmetic and copies ran while one was open for 12% of the time, Pallas kernels for 14%

profile of v2, /device:TPU:30, one launch (start us, length us, event | category | flops | bytes accessed | tf_op | source)
XLA Modules:
  0.0 192.0 jit_solution(15677594735314226640)
XLA Ops:
  20.1 2.9 %collective-permute-done.8 = bf16[256,480]{1,0:T(8,128)(2,1)S(1)} collective-permute-done((bf16[256,480]{1,0:T(8,128)(2,1)S(1)}, bf16[256,480]{1,0:T(8,128)(2,1)S(1)}, u32[]{:S(2)}, u32[]{:S(2)}) %collective-permute-start.8) | collective-permute-done | bytes 245792 | tf_op jit(solution)/shard_map/gather_rows/ppermute | solution.py:26
  29.9 2.8 %collective-permute-start.3 = (bf16[4,256,480]{1,2,0:T(8,128)(2,1)}, bf16[4,256,480]{1,2,0:T(8,128)(2,1)}, u32[]{:S(2)}, u32[]{:S(2)}) collective-permute-start(bf16[4,256,480]{1,2,0:T(8,128)(2,1)} %copy.33), channel_id=1, source_target_pairs={{0,4},{4,8},{8,12},{12,0},{1,5},{5,9},{9,13},{13,1},{2,6},{6,10},{... | collective-permute-start | bytes 2949128 | tf_op jit(solution)/shard_map/gather_rows/ppermute | solution.py:26
  33.8 18.5 %collective-permute-done.10 = bf16[4,256,480]{1,2,0:T(8,128)(2,1)} collective-permute-done((bf16[4,256,480]{1,2,0:T(8,128)(2,1)}, bf16[4,256,480]{1,2,0:T(8,128)(2,1)}, u32[]{:S(2)}, u32[]{:S(2)}) %collective-permute-start.10) | collective-permute-done | bytes 983072 | tf_op jit(solution)/shard_map/gather_rows/ppermute | solution.py:26
  65.0 3.3 %collective-permute-start.4 = (bf16[2,256,480]{2,1,0:T(8,128)(2,1)}, bf16[2,256,480]{2,1,0:T(8,128)(2,1)}, u32[]{:S(2)}, u32[]{:S(2)}) collective-permute-start(bf16[2,256,480]{2,1,0:T(8,128)(2,1)} %slice.153), channel_id=1, source_target_pairs={{0,4},{4,8},{8,12},{12,0},{1,5},{5,9},{9,13},{13,1},{2,6},{6,10},{... | collective-permute-start | bytes 1474568 | tf_op jit(solution)/shard_map/gather_rows/ppermute | solution.py:26
  71.9 3.2 %copy-done.1 = bf16[7680,512]{1,0:T(8,128)(2,1)S(1)} copy-done((bf16[7680,512]{1,0:T(8,128)(2,1)S(1)}, bf16[7680,512]{1,0:T(8,128)(2,1)}, u32[]{:S(2)}) %copy-start.1) | copy-done | bytes 7864344
  75.1 3.3 %project.4.refs_3_ = f32[2,256,512]{2,1,0:T(8,128)S(1)} custom-call(s32[8]{0:T(128)S(1)} %pad_add_fusion.3.index_ref, bf16[4,256,480]{2,1,0:T(8,128)(2,1)S(1)} %pad_maximum_fusion.refs_0_, bf16[4,256,480]{2,1,0:T(8,128)(2,1)S(1)} %pad_maximum_fusion.1.refs_1_, bf16[16,480,512]{2,1,0:T(8,128)(2,1)S(1)} %bitcast.111, f32[1,1,512]{2,1,0:T(1,128)S(1)} %bitcast.117), custom_call_target="tpu_custom_call" | custom-call | flops 1006632960 | bytes 5898240 | tf_op jit(solution)/shard_map/project/pallas_call | solution.py:64
  78.4 3.2 %copy-done.2 = bf16[7680,512]{1,0:T(8,128)(2,1)S(1)} copy-done((bf16[7680,512]{1,0:T(8,128)(2,1)S(1)}, bf16[7680,512]{1,0:T(8,128)(2,1)}, u32[]{:S(2)}) %copy-start.2) | copy-done | bytes 7864344
  81.7 3.3 %project.5.refs_3_ = f32[2,256,512]{2,1,0:T(8,128)S(1)} custom-call(s32[8]{0:T(128)S(1)} %pad_add_fusion.2.index_ref, bf16[4,256,480]{2,1,0:T(8,128)(2,1)S(1)} %copy-done.7, bf16[4,256,480]{2,1,0:T(8,128)(2,1)S(1)} %copy.39.refs_1_, bf16[16,480,512]{2,1,0:T(8,128)(2,1)S(1)} %bitcast.112, f32[2,256,512]{2,1,0:T(8,128)S(1)} %project.4.refs_3_), custom_call_target="tpu_custom_call" | custom-call | flops 1006632960 | bytes 5898240 | tf_op jit(solution)/shard_map/project/pallas_call | solution.py:64
  84.9 3.3 %project.6.refs_5_ = f32[2,256,512]{2,1,0:T(8,128)S(1)} custom-call(s32[8]{0:T(128)S(1)} %pad_add_fusion.1.index_ref, bf16[4,256,480]{2,1,0:T(8,128)(2,1)S(1)} %copy-done.8, bf16[4,256,480]{2,1,0:T(8,128)(2,1)S(1)} %copy-done.6, bf16[16,480,512]{2,1,0:T(8,128)(2,1)S(1)} %bitcast.113, f32[2,256,512]{2,1,0:T(8,128)S(1)} %project.5.refs_3_), custom_call_target="tpu_custom_call" | custom-call | flops 1006632960 | bytes 5898240 | tf_op jit(solution)/shard_map/project/pallas_call | solution.py:64
  88.3 5.8 %project.7.rows_ref = bf16[2,256,512]{2,1,0:T(8,128)(2,1)S(1)} custom-call(s32[8]{0:T(128)S(1)} %pad_add_fusion.index_ref, bf16[2,256,480]{2,1,0:T(8,128)(2,1)} %collective-permute-done.4.refs_0_, bf16[2,256,480]{2,1,0:T(8,128)(2,1)S(1)} %collective-permute-done.6.refs_1_, bf16[2,256,480]{2,1,0:T(8,128)(2,1)} %collective-permute-done.11.refs_2_, ...), custom_call_target="tpu_custom_call" | custom-call | flops 1006632960 | bytes 5898240 | tf_op jit(solution)/shard_map/project/pallas_call | solution.py:64
  94.1 6.9 %kv.1 = (bf16[4,4,256,128]{3,2,1,0:T(8,128)(2,1)S(1)}, bf16[4,4,256,128]{3,2,1,0:T(8,128)(2,1)S(1)}) custom-call(s32[16]{0:T(128)S(1)} %add.273.index_ref, bf16[2,256,512]{2,1,0:T(8,128)(2,1)S(1)} %project.7.rows_ref, bf16[2,512,1024]{2,1,0:T(8,128)(2,1)S(1)} %copy-done.3, bf16[2,512,1024]{2,1,0:T(8,128)(2,1)S(1)} %copy-done.3), custom_call_target="tpu_custom_call" | custom-call | flops 1073741824 | bytes 8388608 | tf_op jit(solution)/shard_map/kv/pallas_call | solution.py:96
  103.2 2.6 %collective-permute-start.16 = (bf16[4,256,128]{2,1,0:T(8,128)(2,1)S(1)}, bf16[4,256,128]{2,1,0:T(8,128)(2,1)S(1)}, u32[]{:S(2)}, u32[]{:S(2)}) collective-permute-start(bf16[4,256,128]{2,1,0:T(8,128)(2,1)S(1)} %get-tuple-element.24), channel_id=1, source_target_pairs={{0,12},{4,0},{8,4},{12,8},{1,13},{5,1},{9,5},{13,9},{2,14},{6,2},{... | collective-permute-start | bytes 786440 | tf_op jit(solution)/shard_map/kv/ppermute | solution.py:26
  109.8 2.9 %collective-permute-done.14 = bf16[4,256,128]{2,1,0:T(8,128)(2,1)S(1)} collective-permute-done((bf16[4,256,128]{2,1,0:T(8,128)(2,1)S(1)}, bf16[4,256,128]{2,1,0:T(8,128)(2,1)S(1)}, u32[]{:S(2)}, u32[]{:S(2)}) %collective-permute-start.14) | collective-permute-done | bytes 262176 | tf_op jit(solution)/shard_map/kv/ppermute | solution.py:26
  118.9 2.5 %collective-permute-done.22 = bf16[4,256,128]{2,1,0:T(8,128)(2,1)S(1)} collective-permute-done((bf16[4,256,128]{2,1,0:T(8,128)(2,1)S(1)}, bf16[4,256,128]{2,1,0:T(8,128)(2,1)S(1)}, u32[]{:S(2)}, u32[]{:S(2)}) %collective-permute-start.22) | collective-permute-done | bytes 262176 | tf_op jit(solution)/shard_map/kv/ppermute | solution.py:26
  124.9 2.9 %collective-permute-done.23 = bf16[256,128]{1,0:T(8,128)(2,1)S(1)} collective-permute-done((bf16[256,128]{1,0:T(8,128)(2,1)S(1)}, bf16[256,128]{1,0:T(8,128)(2,1)S(1)}, u32[]{:S(2)}, u32[]{:S(2)}) %collective-permute-start.23) | collective-permute-done | bytes 65568 | tf_op jit(solution)/shard_map/kv/ppermute | solution.py:26
  129.4 5.6 %all-to-all-start = ((bf16[16,32,256]{2,1,0:T(8,128)(2,1)}), bf16[16,32,256]{2,1,0:T(8,128)(2,1)S(1)}, u32[]{:S(2)}, u32[]{:S(2)}) async-start(bf16[16,32,256]{2,1,0:T(8,128)(2,1)} %bitcast.32), calls=%async_computation | async-start | bytes 524288 | tf_op jit(solution)/shard_map/kv/all_to_all | solution.py:333
  135.5 3.4 %copy-done.5 = bf16[8192,512]{1,0:T(8,128)(2,1)S(1)} copy-done((bf16[8192,512]{1,0:T(8,128)(2,1)S(1)}, bf16[8192,512]{1,0:T(8,128)(2,1)}, u32[]{:S(2)}) %copy-start.5) | copy-done | bytes 8388632
  140.6 5.1 %query.1.query_ref = bf16[128,512]{1,0:T(8,128)(2,1)S(1)} custom-call(bf16[16,144,512]{2,1,0:T(8,128)(2,1)S(1)} %bitcast.115, bf16[8192,512]{1,0:T(8,128)(2,1)S(1)} %copy-done.5), custom_call_target="tpu_custom_call" | custom-call | flops 1073741824 | bytes 12582912 | tf_op jit(solution)/shard_map/query/pallas_call | solution.py:152
  145.7 3.4 %copy-done.4 = bf16[512,8192]{1,0:T(8,128)(2,1)S(1)} copy-done((bf16[512,8192]{1,0:T(8,128)(2,1)S(1)}, bf16[512,8192]{1,0:T(8,128)(2,1)}, u32[]{:S(2)}) %copy-start.4) | copy-done | bytes 8388632
  149.0 6.5 %attend.1 = (bf16[4,4,128,256]{3,2,1,0:T(8,128)(2,1)S(1)}, bf16[4,4,128,256]{3,2,1,0:T(8,128)(2,1)S(1)}) custom-call(s32[16]{0:T(128)S(1)} %add.273.index_ref, bf16[128,512]{1,0:T(8,128)(2,1)S(1)} %query.1.query_ref, bf16[512,256]{1,0:T(8,128)(2,1)S(1)} %bitcast.116, s32[128,1]{1,0:T(8,128)S(1)} %copy.46.row_ref, s32[1,512]{1,0:T(1,128)S(1)} %reshape.128.col_ref, ...), custom_call_target="tpu_custom_call" | custom-call | flops 1073741824 | bytes 12582912 | tf_op jit(solution)/shard_map/attend/pallas_call | solution.py:206
  157.8 2.5 %collective-permute-start.27 = (bf16[4,128,256]{2,1,0:T(8,128)(2,1)}, bf16[4,128,256]{2,1,0:T(8,128)(2,1)S(1)}, u32[]{:S(2)}, u32[]{:S(2)}) collective-permute-start(bf16[4,128,256]{2,1,0:T(8,128)(2,1)} %get-tuple-element.19), channel_id=1, source_target_pairs={{0,8},{4,12},{8,0},{12,4},{1,9},{5,13},{9,1},{13,5},{2,10},{6,14},... | collective-permute-start | bytes 786440 | tf_op jit(solution)/shard_map/mix/ppermute | solution.py:26
  161.5 2.4 %collective-permute-start.33 = (bf16[4,128,256]{2,1,0:T(8,128)(2,1)S(1)}, bf16[4,128,256]{2,1,0:T(8,128)(2,1)S(1)}, u32[]{:S(2)}, u32[]{:S(2)}) collective-permute-start(bf16[4,128,256]{2,1,0:T(8,128)(2,1)S(1)} %get-tuple-element.22), channel_id=1, source_target_pairs={{0,2},{1,3},{2,0},{3,1},{4,6},{5,7},{6,4},{7,5},{8,10},{9,11},{10,... | collective-permute-start | bytes 786440 | tf_op jit(solution)/shard_map/mix/ppermute | solution.py:26
  164.0 2.5 %collective-permute-done.26 = bf16[4,128,256]{2,1,0:T(8,128)(2,1)S(1)} collective-permute-done((bf16[4,128,256]{2,1,0:T(8,128)(2,1)}, bf16[4,128,256]{2,1,0:T(8,128)(2,1)S(1)}, u32[]{:S(2)}, u32[]{:S(2)}) %collective-permute-start.26) | collective-permute-done | bytes 262176 | tf_op jit(solution)/shard_map/mix/ppermute | solution.py:26
  167.0 5.5 %collective-permute-done.27 = bf16[4,128,256]{2,1,0:T(8,128)(2,1)S(1)} collective-permute-done((bf16[4,128,256]{2,1,0:T(8,128)(2,1)}, bf16[4,128,256]{2,1,0:T(8,128)(2,1)S(1)}, u32[]{:S(2)}, u32[]{:S(2)}) %collective-permute-start.27) | collective-permute-done | bytes 262176 | tf_op jit(solution)/shard_map/mix/ppermute | solution.py:26
  (147 shorter events, 73.2 us)
Async XLA Ops:
  6.5 129.0 %all-gather.3.cloned.1.call-start = ((), (), s32[]{:S(2)}) async-start(), calls=%async_computation.1 | async-start | bytes 2506752 | tf_op jit(solution)/shard_map/gather_states/all_gather | solution.py:284
  7.7 11.0 %collective-permute-start.7 = (bf16[256,480]{1,0:T(8,128)(2,1)S(1)}, bf16[256,480]{1,0:T(8,128)(2,1)S(1)}, u32[]{:S(2)}, u32[]{:S(2)}) collective-permute-start(bf16[256,480]{1,0:T(8,128)(2,1)S(1)} %bitcast.122), channel_id=1, source_target_pairs={{0,4},{4,8},{8,12},{12,0},{1,5},{5,9},{9,13},{13,1},{2,6},{6,10},{... | collective-permute-start | bytes 737288 | tf_op jit(solution)/shard_map/gather_rows/ppermute | solution.py:26
  9.6 13.4 %collective-permute-start.8 = (bf16[256,480]{1,0:T(8,128)(2,1)S(1)}, bf16[256,480]{1,0:T(8,128)(2,1)S(1)}, u32[]{:S(2)}, u32[]{:S(2)}) collective-permute-start(bf16[256,480]{1,0:T(8,128)(2,1)S(1)} %bitcast.123), channel_id=1, source_target_pairs={{0,12},{4,0},{8,4},{12,8},{1,13},{5,1},{9,5},{13,9},{2,14},{6,2},{... | collective-permute-start | bytes 737288 | tf_op jit(solution)/shard_map/gather_rows/ppermute | solution.py:26
  11.8 13.0 %collective-permute-start.9 = (bf16[256,480]{1,0:T(8,128)(2,1)S(1)}, bf16[256,480]{1,0:T(8,128)(2,1)S(1)}, u32[]{:S(2)}, u32[]{:S(2)}) collective-permute-start(bf16[256,480]{1,0:T(8,128)(2,1)S(1)} %bitcast.124), channel_id=1, source_target_pairs={{0,8},{4,12},{8,0},{12,4},{1,9},{5,13},{9,1},{13,5},{2,10},{6,14},... | collective-permute-start | bytes 737288 | tf_op jit(solution)/shard_map/gather_rows/ppermute | solution.py:26
  13.6 14.8 %collective-permute-start = (bf16[256,480]{1,0:T(8,128)(2,1)S(1)}, bf16[256,480]{1,0:T(8,128)(2,1)S(1)}, u32[]{:S(2)}, u32[]{:S(2)}) collective-permute-start(bf16[256,480]{1,0:T(8,128)(2,1)S(1)} %bitcast.118), channel_id=1, source_target_pairs={{0,1},{1,2},{2,3},{3,0},{4,5},{5,6},{6,7},{7,4},{8,9},{9,10},{10,1... | collective-permute-start | bytes 737288 | tf_op jit(solution)/shard_map/gather_rows/ppermute | solution.py:26
  14.1 14.3 %collective-permute-start.1 = (bf16[256,480]{1,0:T(8,128)(2,1)S(1)}, bf16[256,480]{1,0:T(8,128)(2,1)S(1)}, u32[]{:S(2)}, u32[]{:S(2)}) collective-permute-start(bf16[256,480]{1,0:T(8,128)(2,1)S(1)} %bitcast.119), channel_id=1, source_target_pairs={{0,3},{1,0},{2,1},{3,2},{4,7},{5,4},{6,5},{7,6},{8,11},{9,8},{10,9... | collective-permute-start | bytes 737288 | tf_op jit(solution)/shard_map/gather_rows/ppermute | solution.py:26
  26.3 26.0 %collective-permute-start.10 = (bf16[4,256,480]{1,2,0:T(8,128)(2,1)}, bf16[4,256,480]{1,2,0:T(8,128)(2,1)}, u32[]{:S(2)}, u32[]{:S(2)}) collective-permute-start(bf16[4,256,480]{1,2,0:T(8,128)(2,1)} %copy.38), channel_id=1, source_target_pairs={{0,1},{1,2},{2,3},{3,0},{4,5},{5,6},{6,7},{7,4},{8,9},{9,10},{10,1... | collective-permute-start | bytes 2949128 | tf_op jit(solution)/shard_map/gather_rows/ppermute | solution.py:26
  26.8 29.3 %collective-permute-start.12 = (bf16[4,256,480]{1,2,0:T(8,128)(2,1)}, bf16[4,256,480]{1,2,0:T(8,128)(2,1)}, u32[]{:S(2)}, u32[]{:S(2)}) collective-permute-start(bf16[4,256,480]{1,2,0:T(8,128)(2,1)} %copy.38), channel_id=1, source_target_pairs={{0,3},{1,0},{2,1},{3,2},{4,7},{5,4},{6,5},{7,6},{8,11},{9,8},{10,9... | collective-permute-start | bytes 2949128 | tf_op jit(solution)/shard_map/gather_rows/ppermute | solution.py:26
  29.9 31.0 %collective-permute-start.3 = (bf16[4,256,480]{1,2,0:T(8,128)(2,1)}, bf16[4,256,480]{1,2,0:T(8,128)(2,1)}, u32[]{:S(2)}, u32[]{:S(2)}) collective-permute-start(bf16[4,256,480]{1,2,0:T(8,128)(2,1)} %copy.33), channel_id=1, source_target_pairs={{0,4},{4,8},{8,12},{12,0},{1,5},{5,9},{9,13},{13,1},{2,6},{6,10},{... | collective-permute-start | bytes 2949128 | tf_op jit(solution)/shard_map/gather_rows/ppermute | solution.py:26
  32.7 35.6 %collective-permute-start.5 = (bf16[4,256,480]{1,2,0:T(8,128)(2,1)}, bf16[4,256,480]{1,2,0:T(8,128)(2,1)}, u32[]{:S(2)}, u32[]{:S(2)}) collective-permute-start(bf16[4,256,480]{1,2,0:T(8,128)(2,1)} %copy.33), channel_id=1, source_target_pairs={{0,12},{4,0},{8,4},{12,8},{1,13},{5,1},{9,5},{13,9},{2,14},{6,2},{... | collective-permute-start | bytes 2949128 | tf_op jit(solution)/shard_map/gather_rows/ppermute | solution.py:26
  54.7 33.5 %collective-permute-start.11 = (bf16[2,256,480]{2,1,0:T(8,128)(2,1)}, bf16[2,256,480]{2,1,0:T(8,128)(2,1)}, u32[]{:S(2)}, u32[]{:S(2)}) collective-permute-start(bf16[2,256,480]{2,1,0:T(8,128)(2,1)} %slice.156), channel_id=1, source_target_pairs={{0,1},{1,2},{2,3},{3,0},{4,5},{5,6},{6,7},{7,4},{8,9},{9,10},{10,1... | collective-permute-start | bytes 1474568 | tf_op jit(solution)/shard_map/gather_rows/ppermute | solution.py:26
  60.3 27.9 %collective-permute-start.13 = (bf16[2,256,480]{2,1,0:T(8,128)(2,1)}, bf16[2,256,480]{2,1,0:T(8,128)(2,1)}, u32[]{:S(2)}, u32[]{:S(2)}) collective-permute-start(bf16[2,256,480]{2,1,0:T(8,128)(2,1)} %slice.157), channel_id=1, source_target_pairs={{0,3},{1,0},{2,1},{3,2},{4,7},{5,4},{6,5},{7,6},{8,11},{9,8},{10,9... | collective-permute-start | bytes 1474568 | tf_op jit(solution)/shard_map/gather_rows/ppermute | solution.py:26
  65.0 23.2 %collective-permute-start.4 = (bf16[2,256,480]{2,1,0:T(8,128)(2,1)}, bf16[2,256,480]{2,1,0:T(8,128)(2,1)}, u32[]{:S(2)}, u32[]{:S(2)}) collective-permute-start(bf16[2,256,480]{2,1,0:T(8,128)(2,1)} %slice.153), channel_id=1, source_target_pairs={{0,4},{4,8},{8,12},{12,0},{1,5},{5,9},{9,13},{13,1},{2,6},{6,10},{... | collective-permute-start | bytes 1474568 | tf_op jit(solution)/shard_map/gather_rows/ppermute | solution.py:26
  71.8 16.5 %collective-permute-start.6 = (bf16[2,256,480]{2,1,0:T(8,128)(2,1)S(1)}, bf16[2,256,480]{2,1,0:T(8,128)(2,1)S(1)}, u32[]{:S(2)}, u32[]{:S(2)}) collective-permute-start(bf16[2,256,480]{2,1,0:T(8,128)(2,1)S(1)} %slice.154), channel_id=1, source_target_pairs={{0,12},{4,0},{8,4},{12,8},{1,13},{5,1},{9,5},{13,9},{2,14},{6,2},{... | collective-permute-start | bytes 1474568 | tf_op jit(solution)/shard_map/gather_rows/ppermute | solution.py:26
  101.0 11.7 %collective-permute-start.14 = (bf16[4,256,128]{2,1,0:T(8,128)(2,1)S(1)}, bf16[4,256,128]{2,1,0:T(8,128)(2,1)S(1)}, u32[]{:S(2)}, u32[]{:S(2)}) collective-permute-start(bf16[4,256,128]{2,1,0:T(8,128)(2,1)S(1)} %get-tuple-element.23), channel_id=1, source_target_pairs={{0,4},{4,8},{8,12},{12,0},{1,5},{5,9},{9,13},{13,1},{2,6},{6,10},{... | collective-permute-start | bytes 786440 | tf_op jit(solution)/shard_map/kv/ppermute | solution.py:26
  103.1 10.7 %collective-permute-start.15 = (bf16[4,256,128]{2,1,0:T(8,128)(2,1)S(1)}, bf16[4,256,128]{2,1,0:T(8,128)(2,1)S(1)}, u32[]{:S(2)}, u32[]{:S(2)}) collective-permute-start(bf16[4,256,128]{2,1,0:T(8,128)(2,1)S(1)} %get-tuple-element.25), channel_id=1, source_target_pairs={{0,8},{4,12},{8,0},{12,4},{1,9},{5,13},{9,1},{13,5},{2,10},{6,14},... | collective-permute-start | bytes 786440 | tf_op jit(solution)/shard_map/kv/ppermute | solution.py:26
  105.9 11.0 %collective-permute-start.20 = (bf16[4,256,128]{2,1,0:T(8,128)(2,1)S(1)}, bf16[4,256,128]{2,1,0:T(8,128)(2,1)S(1)}, u32[]{:S(2)}, u32[]{:S(2)}) collective-permute-start(bf16[4,256,128]{2,1,0:T(8,128)(2,1)S(1)} %get-tuple-element.26), channel_id=1, source_target_pairs={{0,1},{1,2},{2,3},{3,0},{4,5},{5,6},{6,7},{7,4},{8,9},{9,10},{10,1... | collective-permute-start | bytes 786440 | tf_op jit(solution)/shard_map/kv/ppermute | solution.py:26
  108.1 10.7 %collective-permute-start.21 = (bf16[4,256,128]{2,1,0:T(8,128)(2,1)S(1)}, bf16[4,256,128]{2,1,0:T(8,128)(2,1)S(1)}, u32[]{:S(2)}, u32[]{:S(2)}) collective-permute-start(bf16[4,256,128]{2,1,0:T(8,128)(2,1)S(1)} %get-tuple-element.28), channel_id=1, source_target_pairs={{0,2},{1,3},{2,0},{3,1},{4,6},{5,7},{6,4},{7,5},{8,10},{9,11},{10,... | collective-permute-start | bytes 786440 | tf_op jit(solution)/shard_map/kv/ppermute | solution.py:26
  129.4 16.3 %all-to-all-start = ((bf16[16,32,256]{2,1,0:T(8,128)(2,1)}), bf16[16,32,256]{2,1,0:T(8,128)(2,1)S(1)}, u32[]{:S(2)}, u32[]{:S(2)}) async-start(bf16[16,32,256]{2,1,0:T(8,128)(2,1)} %bitcast.32), calls=%async_computation | async-start | bytes 524288 | tf_op jit(solution)/shard_map/kv/all_to_all | solution.py:333
  157.8 14.7 %collective-permute-start.27 = (bf16[4,128,256]{2,1,0:T(8,128)(2,1)}, bf16[4,128,256]{2,1,0:T(8,128)(2,1)S(1)}, u32[]{:S(2)}, u32[]{:S(2)}) collective-permute-start(bf16[4,128,256]{2,1,0:T(8,128)(2,1)} %get-tuple-element.19), channel_id=1, source_target_pairs={{0,8},{4,12},{8,0},{12,4},{1,9},{5,13},{9,1},{13,5},{2,10},{6,14},... | collective-permute-start | bytes 786440 | tf_op jit(solution)/shard_map/mix/ppermute | solution.py:26
  160.3 12.2 %collective-permute-start.28 = (bf16[4,128,256]{2,1,0:T(8,128)(2,1)}, bf16[4,128,256]{2,1,0:T(8,128)(2,1)S(1)}, u32[]{:S(2)}, u32[]{:S(2)}) collective-permute-start(bf16[4,128,256]{2,1,0:T(8,128)(2,1)} %get-tuple-element.18), channel_id=1, source_target_pairs={{0,12},{4,0},{8,4},{12,8},{1,13},{5,1},{9,5},{13,9},{2,14},{6,2},{... | collective-permute-start | bytes 786440 | tf_op jit(solution)/shard_map/mix/ppermute | solution.py:26
  161.3 14.1 %collective-permute-start.32 = (bf16[4,128,256]{2,1,0:T(8,128)(2,1)S(1)}, bf16[4,128,256]{2,1,0:T(8,128)(2,1)S(1)}, u32[]{:S(2)}, u32[]{:S(2)}) collective-permute-start(bf16[4,128,256]{2,1,0:T(8,128)(2,1)S(1)} %get-tuple-element.20), channel_id=1, source_target_pairs={{0,1},{1,2},{2,3},{3,0},{4,5},{5,6},{6,7},{7,4},{8,9},{9,10},{10,1... | collective-permute-start | bytes 786440 | tf_op jit(solution)/shard_map/mix/ppermute | solution.py:26
  161.5 13.9 %collective-permute-start.33 = (bf16[4,128,256]{2,1,0:T(8,128)(2,1)S(1)}, bf16[4,128,256]{2,1,0:T(8,128)(2,1)S(1)}, u32[]{:S(2)}, u32[]{:S(2)}) collective-permute-start(bf16[4,128,256]{2,1,0:T(8,128)(2,1)S(1)} %get-tuple-element.22), channel_id=1, source_target_pairs={{0,2},{1,3},{2,0},{3,1},{4,6},{5,7},{6,4},{7,5},{8,10},{9,11},{10,... | collective-permute-start | bytes 786440 | tf_op jit(solution)/shard_map/mix/ppermute | solution.py:26
  166.4 10.7 %collective-permute-start.34 = (bf16[4,128,256]{2,1,0:T(8,128)(2,1)S(1)}, bf16[4,128,256]{2,1,0:T(8,128)(2,1)S(1)}, u32[]{:S(2)}, u32[]{:S(2)}) collective-permute-start(bf16[4,128,256]{2,1,0:T(8,128)(2,1)S(1)} %get-tuple-element.21), channel_id=1, source_target_pairs={{0,3},{1,0},{2,1},{3,2},{4,7},{5,4},{6,5},{7,6},{8,11},{9,8},{10,9... | collective-permute-start | bytes 786440 | tf_op jit(solution)/shard_map/mix/ppermute | solution.py:26
  (30 other events, 384.5 us)
Sparse Core Ops, SparseCore 0:
  18.0 51.4 all-gather.2

commit v3 on v2

v3 whole, which is shorter than its diff:
```python
import functools

import jax
import jax.numpy as jnp
from jax import lax
from jax.experimental import pallas as pl
from jax.experimental.pallas import tpu as pltpu
from jax.sharding import Mesh, PartitionSpec as P

D = 8192
HEADS = 64
KV_HEADS = 8
HEAD_DIM = 128
MAXT = 4
STEPS = 2
SIDE = 4
F32 = jnp.float32
BF16 = jnp.bfloat16
TP = ("z", "xh", "pr")
EVERY = ("group",) + TP
FIRST, SECOND = 0, 1
VMEM = 58 * 1024 * 1024


def place(core, first, second):
    return jnp.where(core == 0, second * SIDE + first, first * SIDE + second)


def shift(value, groups, order, by):
    pairs = []
    for group in range(groups):
        for z in range(SIDE):
            for x in range(SIDE):
                if group % 2 == order:
                    other = z * SIDE + (x + by) % SIDE
                else:
                    other = (z + by) % SIDE * SIDE + x
                base = group * SIDE * SIDE
                pairs.append((base + z * SIDE + x, base + other))
    return lax.ppermute(value, EVERY, pairs)


def project_kernel(spans, index_ref, *refs):
    blocks = refs[: len(spans)]
    weight_ref, start_ref, out_ref, accum_ref = refs[len(spans) :]
    step = pl.program_id(0)

    @pl.when(step == 0)
    def _():
        accum_ref[...] = jnp.broadcast_to(start_ref[...], accum_ref.shape)

    for block, (begin, count) in zip(blocks, spans):

        @pl.when((step >= begin) & (step < begin + count))
        def _():
            accum_ref[...] += lax.dot_general(
                block[0], weight_ref[0], (((0,), (0,)), ((), ())), preferred_element_type=F32
            )

    @pl.when(step == pl.num_programs(0) - 1)
    def _():
        out_ref[...] = accum_ref[...].astype(out_ref.dtype)


def project(start, blocks, index, weight, kind):
    features, rows = blocks[0].shape[1:]
    width = weight.shape[2]
    spans, begin = [], 0
    for block in blocks:
        spans.append((begin, block.shape[0]))
        begin += block.shape[0]
    shape = (rows, width)

    def block_spec(begin, count):
        return pl.BlockSpec(
            (1, features, rows), lambda i, _: (jnp.clip(i - begin, 0, count - 1), 0, 0)
        )

    return pl.pallas_call(
        functools.partial(project_kernel, spans),
        grid_spec=pltpu.PrefetchScalarGridSpec(
            num_scalar_prefetch=1,
            grid=(begin,),
            in_specs=[block_spec(at, count) for at, count in spans]
            + [
                pl.BlockSpec((1, features, width), lambda i, index: (index[i], 0, 0)),
                pl.BlockSpec(start.shape, lambda i, _: (0, 0)),
            ],
            out_specs=pl.BlockSpec(shape, lambda i, _: (0, 0)),
            scratch_shapes=[pltpu.VMEM(shape, F32)],
        ),
        out_shape=jax.ShapeDtypeStruct(shape, kind),
        compiler_params=pltpu.CompilerParams(vmem_limit_bytes=VMEM),
        cost_estimate=pl.CostEstimate(
            flops=2 * begin * rows * features * width,
            bytes_accessed=2 * begin * (rows + width) * features,
            transcendentals=0,
        ),
    )(index, *blocks, weight, start)


def kv_kernel(place_ref, rows_ref, weight_ref, out_ref):
    half = out_ref.shape[2]
    for head in range(KV_HEADS):
        span = slice(head * HEAD_DIM, (head + 1) * HEAD_DIM)
        weight = jnp.concatenate([weight_ref[0, :, span], weight_ref[1, :, span]], axis=1)
        part = jnp.dot(rows_ref[...], weight, preferred_element_type=F32).astype(BF16)
        for parity in range(2):
            at = place_ref[2 * head + parity]
            out_ref[at // SIDE, at % SIDE] = part[parity * half : (parity + 1) * half]


def kv_partials(places, projected, kv_weight):
    rows, width = projected.shape
    vmem = pl.BlockSpec(memory_space=pltpu.VMEM)
    return pl.pallas_call(
        kv_kernel,
        in_specs=[pl.BlockSpec(memory_space=pltpu.SMEM), vmem, vmem],
        out_specs=vmem,
        out_shape=jax.ShapeDtypeStruct((SIDE, SIDE, rows // 2, 2 * HEAD_DIM), BF16),
        compiler_params=pltpu.CompilerParams(vmem_limit_bytes=VMEM),
        cost_estimate=pl.CostEstimate(
            flops=2 * rows * width * 2 * KV_HEADS * HEAD_DIM,
            bytes_accessed=5 * 1024 * 1024,
            transcendentals=0,
        ),
    )(places, projected, kv_weight)


def query_kernel(full_ref, weight_ref, out_ref, inverse_ref, accum_ref):
    batch = out_ref.shape[0]
    width = full_ref.shape[2]
    part = weight_ref.shape[0] // width
    step = pl.program_id(0)

    @pl.when(step == 0)
    def _():
        total = jnp.zeros((batch, 1), F32)
        for rank in range(full_ref.shape[0]):
            hidden = full_ref[rank, :batch].astype(F32)
            total += jnp.sum(hidden * hidden, axis=1, keepdims=True)
        inverse_ref[...] = lax.rsqrt(total / D + 1e-05)
        accum_ref[...] = jnp.zeros_like(accum_ref)

    for inner in range(part):
        rank = step * part + inner
        hidden = full_ref[rank, :batch].astype(F32)
        gain = full_ref[rank, batch : batch + 16].astype(F32)[:1]
        normed = (hidden * inverse_ref[...] * gain).astype(BF16)
        span = slice(inner * width, (inner + 1) * width)
        accum_ref[...] += jnp.dot(normed, weight_ref[span, :], preferred_element_type=F32)

    @pl.when(step == pl.num_programs(0) - 1)
    def _():
        out_ref[...] = accum_ref[...].astype(BF16)


def queries(full, query_weight, batch):
    ranks, rows, width = full.shape
    columns = query_weight.shape[1]
    return pl.pallas_call(
        query_kernel,
        grid=(ranks // 4,),
        in_specs=[
            pl.BlockSpec((ranks, rows, width), lambda i: (0, 0, 0)),
            pl.BlockSpec((4 * width, columns), lambda i: (i, 0)),
        ],
        out_specs=pl.BlockSpec((batch, columns), lambda i: (0, 0)),
        out_shape=jax.ShapeDtypeStruct((batch, columns), BF16),
        scratch_shapes=[pltpu.VMEM((batch, 1), F32), pltpu.VMEM((batch, columns), F32)],
        compiler_params=pltpu.CompilerParams(vmem_limit_bytes=VMEM),
        cost_estimate=pl.CostEstimate(
            flops=2 * batch * ranks * width * columns,
            bytes_accessed=12 * 1024 * 1024,
            transcendentals=0,
        ),
    )(full, query_weight)


def attend_kernel(
    place_ref, query_ref, kv_ref, row_ref, col_ref, weight_ref, out_ref, context_ref
):
    batch, width = context_ref.shape
    columns = out_ref.shape[3]
    part = weight_ref.shape[1] // columns
    step = pl.program_id(0)

    @pl.when(step == 0)
    def _():
        keys = kv_ref[:, :HEAD_DIM]
        values = kv_ref[:, HEAD_DIM:]
        allowed = row_ref[...] == col_ref[...]
        for head in range(width // HEAD_DIM):
            span = slice(head * HEAD_DIM, (head + 1) * HEAD_DIM)
            scores = lax.dot_general(
                query_ref[:, span], keys, (((1,), (1,)), ((), ())), preferred_element_type=F32
            ) * (1.0 / HEAD_DIM**0.5)
            scores = jnp.where(allowed, scores, -1e30)
            largest = jnp.max(scores, axis=1, keepdims=True)
            weights = jnp.where(allowed, jnp.exp(scores - largest), 0.0)
            total = jnp.sum(weights, axis=1, keepdims=True)
            summed = jnp.dot(weights.astype(BF16), values, preferred_element_type=F32)
            context_ref[:, span] = (summed / total).astype(BF16)

    for inner in range(part):
        span = slice(inner * columns, (inner + 1) * columns)
        branch = jnp.dot(context_ref[...], weight_ref[:, span], preferred_element_type=F32)
        at = place_ref[step * part + inner]
        out_ref[at // SIDE, at % SIDE] = branch.astype(BF16)


def attend(places, query, kv, row_request, col_request, out_weight):
    batch, width = query.shape
    rows = kv.shape[0]
    columns = out_weight.shape[1] // (SIDE * SIDE)
    shape = (SIDE, SIDE, batch, columns)
    fixed = lambda i, _: (0, 0)
    return pl.pallas_call(
        attend_kernel,
        grid_spec=pltpu.PrefetchScalarGridSpec(
            num_scalar_prefetch=1,
            grid=(SIDE,),
            in_specs=[
                pl.BlockSpec((batch, width), fixed),
                pl.BlockSpec((rows, 2 * HEAD_DIM), fixed),
                pl.BlockSpec((batch, 1), fixed),
                pl.BlockSpec((1, rows), fixed),
                pl.BlockSpec((width, SIDE * columns), lambda i, _: (0, i)),
            ],
            out_specs=pl.BlockSpec(shape, lambda i, _: (0, 0, 0, 0)),
            scratch_shapes=[pltpu.VMEM((batch, width), BF16)],
        ),
        out_shape=jax.ShapeDtypeStruct(shape, BF16),
        compiler_params=pltpu.CompilerParams(vmem_limit_bytes=VMEM),
        cost_estimate=pl.CostEstimate(
            flops=2 * batch * width * out_weight.shape[1],
            bytes_accessed=12 * 1024 * 1024,
            transcendentals=batch * rows * 4,
        ),
    )(places, query, kv, row_request, col_request, out_weight)


def sum_phase(blocks, groups, order):
    total = blocks[0].astype(F32)
    for by in (1, 3, 2):
        total += shift(blocks[by], groups, order, by).astype(F32)
    return total


def body(
    vision_rows,
    tile_count,
    tile_source,
    row_request,
    proj_weight,
    proj_bias,
    kv_weight,
    query_weight,
    out_weight,
    norm_gain,
    attn_gate,
    states,
):
    groups = lax.axis_size("group")
    ranks = lax.axis_size(TP)
    group = lax.axis_index("group")
    along_z = lax.axis_index("z")
    along_x = lax.axis_index(("xh", "pr"))
    core = group % 2
    first = jnp.where(core == 0, along_x, along_z)
    second = jnp.where(core == 0, along_z, along_x)
    tile_rows, features = vision_rows.shape[2:]
    per_group = vision_rows.shape[1] // groups
    slots = groups * per_group
    group_rows = slots * tile_rows
    req_grp = slots // MAXT
    batch = states.shape[1]
    width = states.shape[2]

    with jax.named_scope("gather_rows"):
        mine = vision_rows[0].reshape(groups, per_group, tile_rows, features)
        mine = mine.transpose(3, 1, 0, 2).reshape(1, features, group_rows)
        near = [mine] + [shift(mine, groups, FIRST, by) for by in (1, 3, 2)]
        near = jnp.concatenate(near)
        after = shift(near, groups, SECOND, 1)
        before = shift(near, groups, SECOND, 3)

    with jax.named_scope("gather_states"):
        local = states.reshape(STEPS * batch, width)
        gain_rows = jnp.broadcast_to(norm_gain[None, :], (16, width))
        full = lax.all_gather(jnp.concatenate([local, gain_rows], axis=0), TP)

    with jax.named_scope("project"):
        weight = proj_weight.reshape(ranks, features, proj_weight.shape[1])
        hops = jnp.array([0, 1, 3, 2], jnp.int32)

        def index(far):
            return place(core, (first - hops) % SIDE, (second - far) % SIDE).astype(jnp.int32)

        bias = proj_bias.astype(F32)[None, :]
        accum = project(bias, [near], index(0), weight, F32)
        after, before, accum = lax.optimization_barrier((after, before, accum))

    with jax.named_scope("gather_rows"):
        across_after = shift(after[:2], groups, SECOND, 1)
        across_before = shift(before[2:], groups, SECOND, 3)

    with jax.named_scope("project"):
        accum = project(accum, [after], index(1), weight, F32)
        accum = project(accum, [before], index(3), weight, F32)
        projected = project(accum, [across_after, across_before], index(2), weight, BF16)

    with jax.named_scope("kv"):
        rank = jnp.arange(ranks, dtype=jnp.int32)
        of_x, of_z = rank % SIDE, rank // SIDE
        to_first = (jnp.where(core == 0, of_x, of_z) - first) % SIDE
        to_second = (jnp.where(core == 0, of_z, of_x) - second) % SIDE
        places = (to_first * SIDE + to_second).astype(jnp.int32)
        kv = kv_partials(places, projected, kv_weight)
        kv = sum_phase(kv, groups, FIRST).astype(BF16)
        kv = sum_phase(kv, groups, SECOND).astype(BF16)
        kv = kv.reshape(groups, 1, tile_rows, 2 * HEAD_DIM)
        kv = jnp.broadcast_to(kv, (groups, 2, tile_rows, 2 * HEAD_DIM))
        kv = kv.reshape(slots, tile_rows, 2 * HEAD_DIM)
        kv = lax.all_to_all(kv, ("group", "pr"), 0, 0)
        kv = kv.reshape(group_rows, 2 * HEAD_DIM)

    with jax.named_scope("query"):
        query = queries(full, query_weight, STEPS * batch)

    with jax.named_scope("mask"):
        sources = lax.dynamic_index_in_dim(tile_source, group, 0, keepdims=False)
        counts = lax.dynamic_slice_in_dim(tile_count, group * req_grp, req_grp, 0)
        spots = jnp.arange(slots, dtype=jnp.int32)
        request = spots // MAXT
        valid = spots % MAXT < jnp.repeat(counts, MAXT)
        label = jnp.where(valid, request, -1)
        hits = sources[None, :] == spots[:, None]
        tile_label = jnp.sum(jnp.where(hits, label[None, :], 0), axis=1)
        col_request = jnp.repeat(tile_label, tile_rows)[None, :]
        rows = jnp.concatenate([row_request[0]] * STEPS)[:, None]

    with jax.named_scope("attend"):
        branch = attend(places, query, kv, rows, col_request, out_weight)

    with jax.named_scope("mix"):
        branch = sum_phase(branch, groups, FIRST).astype(BF16)
        reduced = sum_phase(branch, groups, SECOND)
        mixed = local.astype(F32) + jnp.tanh(attn_gate) * reduced
        return mixed.astype(BF16).reshape(STEPS, batch, width)


def solution(mesh):
    groups = mesh.shape["group"]
    split = Mesh(mesh.devices.reshape(groups, SIDE, 2, 2), ("group",) + TP)
    in_specs = (
        P("group", None, None, TP),
        P(),
        P(),
        P("group", None),
        P(None, TP),
        P(TP),
        P(None, TP, None),
        P(None, TP),
        P(TP, None),
        P(TP),
        P(),
        P(None, "group", TP),
    )
    out_specs = P(None, "group", TP)
    return jax.shard_map(body, mesh=split, in_specs=in_specs, out_specs=out_specs, check_vma=False)
```

time: 195 us -> 185 us (0.949)
  waiting for transfers between devices: 46.5 us -> 74.3 us
  local copies, waits for them, and re-layouts: 35.9 us -> 11.8 us
  starting transfers between devices: 56.4 us -> 33 us
  Pallas kernels: 34.1 us -> 43.5 us
  other arithmetic: 4.59 us -> 6.88 us
    ppermute x38 -> x19, waiting for transfers between devices: 46.5 us -> 74.3 us  [shift(): return lax.ppermute(value, EVERY, pairs)]
    ppermute x38 -> x19, starting transfers between devices: 50.8 us -> 27.3 us  [shift(): return lax.ppermute(value, EVERY, pairs)]
    unnamed x28 -> x22, local copies, waits for them, and re-layouts: 14.9 us -> 1.7 us
    ppermute x4 -> x0, local copies, waits for them, and re-layouts: 8.29 us -> none  [shift(): lax.ppermute(value, axis, [(i, (i + by) % SIDE) for i in range(SIDE)])]
    pallas_call x6, Pallas kernels: 27.6 us -> 35.3 us  [the longest x4 23.9 us: project(): pl.pallas_call(functools.partial(project_kernel, spans), grid_spec=pltpu....]
    slice x5 -> x2, local copies, waits for them, and re-layouts: 6.91 us -> 2.53 us  [the longest x1 1.27 us: body(): across_after = shift(after[:2], groups, SECOND, 1)]
    squeeze x8 -> x5, local copies, waits for them, and re-layouts: 1.15 us -> 4.86 us  [the longest x4 3.78 us: sum_phase(): total += shift(blocks[by], groups, order, by).astype(F32)]
    another operation x2 -> x0, local copies, waits for them, and re-layouts: 2.64 us -> none  [the longest x1 1.32 us: body(): stack_a = jnp.stack(rows_a)]
  transfers between devices with their start and end apart: 40 -> 21, of which waited for: 15 -> 15; matrix products, arithmetic and copies ran while one was open for 12% -> 6% of each run, Pallas kernels for 14% -> 19%
where the time goes in v3:
time: 185 us; the launch traced here: 184 us
  waiting for transfers between devices  74.3 us (40%)
  Pallas kernels  43.5 us (24%)
  starting transfers between devices  33 us (18%)
  between operations  14.3 us (8%)
  local copies, waits for them, and re-layouts  11.8 us (6%)
  other arithmetic  6.88 us (4%)
    ppermute x19, waiting for transfers between devices, shift(): return lax.ppermute(value, EVERY, pairs)  74.3 us
    ppermute x19, starting transfers between devices, shift(): return lax.ppermute(value, EVERY, pairs)  27.3 us
    pallas_call x4, Pallas kernels, project(): pl.pallas_call(functools.partial(project_kernel, spans), grid_spec=pltpu....  23.9 us
    pallas_call x1, Pallas kernels, attend(): pl.pallas_call(attend_kernel, grid_spec=pltpu.PrefetchScalarGridSpec(num_...  8.19 us
    pallas_call x1, Pallas kernels, queries(): pl.pallas_call(query_kernel, grid=(ranks // 4,), in_specs=[pl.BlockSpec((...  6.81 us
    all_to_all x1, starting transfers between devices, body(): kv = lax.all_to_all(kv, ('group', 'pr'), 0, 0)  5.69 us
    pallas_call x1, Pallas kernels, kv_partials(): pl.pallas_call(kv_kernel, in_specs=[pl.BlockSpec(memory_space=pltpu.SMEM)...  4.5 us
    squeeze x4, local copies, waits for them, and re-layouts, sum_phase(): total += shift(blocks[by], groups, order, by).astype(F32)  3.78 us
  transfers between devices with their start and end apart: 21, of which 15 were waited for; matrix products, arithmetic and copies ran while one was open for 6% of the time, Pallas kernels for 19%

profile of v3, /device:TPU:30, one launch (start us, length us, event | category | flops | bytes accessed | tf_op | source)
XLA Modules:
  0.0 183.7 jit_solution(8896807000610110369)
XLA Ops:
  11.4 5.4 %collective-permute-done = bf16[1,480,512]{2,1,0:T(8,128)(2,1)S(1)} collective-permute-done((bf16[1,480,512]{2,1,0:T(8,128)(2,1)S(1)}, bf16[1,480,512]{2,1,0:T(8,128)(2,1)S(1)}, u32[]{:S(2)}, u32[]{:S(2)}) %collective-permute-start) | collective-permute-done | bytes 491552 | tf_op jit(solution)/shard_map/gather_rows/ppermute | solution.py:40
  16.8 7.0 %collective-permute-done.1 = bf16[1,480,512]{2,1,0:T(8,128)(2,1)S(1)} collective-permute-done((bf16[1,480,512]{2,1,0:T(8,128)(2,1)S(1)}, bf16[1,480,512]{2,1,0:T(8,128)(2,1)S(1)}, u32[]{:S(2)}, u32[]{:S(2)}) %collective-permute-start.1) | collective-permute-done | bytes 491552 | tf_op jit(solution)/shard_map/gather_rows/ppermute | solution.py:40
  24.0 2.0 %collective-permute-start.3 = (bf16[4,480,512]{2,1,0:T(8,128)(2,1)S(1)}, bf16[4,480,512]{2,1,0:T(8,128)(2,1)}, u32[]{:S(2)}, u32[]{:S(2)}) collective-permute-start(bf16[4,480,512]{2,1,0:T(8,128)(2,1)S(1)} %pad_maximum_fusion.refs_0_), channel_id=1, source_target_pairs={{0,4},{1,5},{2,6},{3,7},{4,8},{5,9},{6,10},{7,11},{8,12},{9,13},{1... | collective-permute-start | bytes 5898248 | tf_op jit(solution)/shard_map/gather_rows/ppermute | solution.py:40
  26.0 2.2 %collective-permute-start.4 = (bf16[4,480,512]{2,1,0:T(8,128)(2,1)S(1)}, bf16[4,480,512]{2,1,0:T(8,128)(2,1)}, u32[]{:S(2)}, u32[]{:S(2)}) collective-permute-start(bf16[4,480,512]{2,1,0:T(8,128)(2,1)S(1)} %pad_maximum_fusion.refs_0_), channel_id=1, source_target_pairs={{0,12},{1,13},{2,14},{3,15},{4,0},{5,1},{6,2},{7,3},{8,4},{9,5},{1... | collective-permute-start | bytes 5898248 | tf_op jit(solution)/shard_map/gather_rows/ppermute | solution.py:40
  30.7 5.8 %project.4.refs_2_ = f32[512,512]{1,0:T(8,128)} custom-call(s32[4]{0:T(128)} %get-tuple-element.26.index_ref, bf16[4,480,512]{2,1,0:T(8,128)(2,1)} %copy-done.1, bf16[16,480,512]{2,1,0:T(8,128)(2,1)} %bitcast.62, f32[1,512]{1,0:T(1,128)} %bitcast.72), custom_call_target="tpu_custom_call" | custom-call | flops 1006632960 | bytes 3932160 | tf_op jit(solution)/shard_map/project/pallas_call | solution.py:79
  36.5 16.7 %collective-permute-done.3.refs_0_ = bf16[4,480,512]{2,1,0:T(8,128)(2,1)} collective-permute-done((bf16[4,480,512]{2,1,0:T(8,128)(2,1)S(1)}, bf16[4,480,512]{2,1,0:T(8,128)(2,1)}, u32[]{:S(2)}, u32[]{:S(2)}) %collective-permute-start.3) | collective-permute-done | bytes 1966112 | tf_op jit(solution)/shard_map/gather_rows/ppermute | solution.py:40
  54.5 1.9 %collective-permute-start.5 = (bf16[2,480,512]{2,1,0:T(8,128)(2,1)S(1)}, bf16[2,480,512]{2,1,0:T(8,128)(2,1)S(1)}, u32[]{:S(2)}, u32[]{:S(2)}) collective-permute-start(bf16[2,480,512]{2,1,0:T(8,128)(2,1)S(1)} %slice.54), channel_id=1, source_target_pairs={{0,4},{1,5},{2,6},{3,7},{4,8},{5,9},{6,10},{7,11},{8,12},{9,13},{1... | collective-permute-start | bytes 2949128 | tf_op jit(solution)/shard_map/gather_rows/ppermute | solution.py:40
  59.8 6.0 %project.5.refs_2_ = f32[512,512]{1,0:T(8,128)} custom-call(s32[4]{0:T(128)} %get-tuple-element.11.index_ref, bf16[4,480,512]{2,1,0:T(8,128)(2,1)} %collective-permute-done.3.refs_0_, bf16[16,480,512]{2,1,0:T(8,128)(2,1)} %bitcast.63, f32[512,512]{1,0:T(8,128)} %project.4.refs_2_), custom_call_target="tpu_custom_call" | custom-call | flops 1006632960 | bytes 3932160 | tf_op jit(solution)/shard_map/project/pallas_call | solution.py:79
  65.8 6.1 %project.6.refs_3_ = f32[512,512]{1,0:T(8,128)} custom-call(s32[4]{0:T(128)} %get-tuple-element.25.index_ref, bf16[4,480,512]{2,1,0:T(8,128)(2,1)} %collective-permute-done.4.refs_0_, bf16[16,480,512]{2,1,0:T(8,128)(2,1)} %bitcast.64, f32[512,512]{1,0:T(8,128)} %project.5.refs_2_), custom_call_target="tpu_custom_call" | custom-call | flops 1006632960 | bytes 3932160 | tf_op jit(solution)/shard_map/project/pallas_call | solution.py:79
  71.9 7.5 %collective-permute-done.5.refs_0_ = bf16[2,480,512]{2,1,0:T(8,128)(2,1)S(1)} collective-permute-done((bf16[2,480,512]{2,1,0:T(8,128)(2,1)S(1)}, bf16[2,480,512]{2,1,0:T(8,128)(2,1)S(1)}, u32[]{:S(2)}, u32[]{:S(2)}) %collective-permute-start.5) | collective-permute-done | bytes 983072 | tf_op jit(solution)/shard_map/gather_rows/ppermute | solution.py:40
  79.4 1.9 %collective-permute-done.6.refs_1_ = bf16[2,480,512]{2,1,0:T(8,128)(2,1)S(1)} collective-permute-done((bf16[2,480,512]{2,1,0:T(8,128)(2,1)S(1)}, bf16[2,480,512]{2,1,0:T(8,128)(2,1)S(1)}, u32[]{:S(2)}, u32[]{:S(2)}) %collective-permute-start.6) | collective-permute-done | bytes 983072 | tf_op jit(solution)/shard_map/gather_rows/ppermute | solution.py:40
  82.2 6.0 %project.7.rows_ref = bf16[512,512]{1,0:T(8,128)(2,1)} custom-call(s32[4]{0:T(128)} %get-tuple-element.27.index_ref, bf16[2,480,512]{2,1,0:T(8,128)(2,1)} %copy-done.3, bf16[2,480,512]{2,1,0:T(8,128)(2,1)} %copy-done.4, bf16[16,480,512]{2,1,0:T(8,128)(2,1)} %bitcast.65, f32[512,512]{1,0:T(8,128)} %project.6.refs_3_), custom_call_target="tpu_custom_call" | custom-call | flops 1006632960 | bytes 3932160 | tf_op jit(solution)/shard_map/project/pallas_call | solution.py:79
  88.2 4.5 %kv.1 = bf16[4,4,256,256]{3,2,1,0:T(8,128)(2,1)} custom-call(s32[16]{0:T(128)} %fusion.14.place_ref, bf16[512,512]{1,0:T(8,128)(2,1)} %project.7.rows_ref, bf16[2,512,1024]{2,1,0:T(8,128)(2,1)} %weight_ref.4), custom_call_target="tpu_custom_call" | custom-call | flops 1073741824 | bytes 5242880 | tf_op jit(solution)/shard_map/kv/pallas_call | solution.py:116
  92.7 2.3 %slice_bitcast_fusion.6 = (bf16[4,256,256]{2,1,0:T(8,128)(2,1)}, bf16[4,256,256]{2,1,0:T(8,128)(2,1)S(1)}, bf16[4,256,256]{2,1,0:T(8,128)(2,1)S(1)}) fusion(bf16[4,4,256,256]{3,2,1,0:T(8,128)(2,1)} %kv.1), kind=kLoop, calls=%fused_computation.15 | loop fusion | bytes 3145728 | tf_op jit(solution)/shard_map/kv/squeeze | solution.py:246
  98.9 5.5 %collective-permute-done.7 = bf16[4,256,256]{2,1,0:T(8,128)(2,1)S(1)} collective-permute-done((bf16[4,256,256]{2,1,0:T(8,128)(2,1)}, bf16[4,256,256]{2,1,0:T(8,128)(2,1)S(1)}, u32[]{:S(2)}, u32[]{:S(2)}) %collective-permute-start.7) | collective-permute-done | bytes 524320 | tf_op jit(solution)/shard_map/kv/ppermute | solution.py:40
  104.4 7.4 %collective-permute-done.8 = bf16[4,256,256]{2,1,0:T(8,128)(2,1)S(1)} collective-permute-done((bf16[4,256,256]{2,1,0:T(8,128)(2,1)S(1)}, bf16[4,256,256]{2,1,0:T(8,128)(2,1)S(1)}, u32[]{:S(2)}, u32[]{:S(2)}) %collective-permute-start.8) | collective-permute-done | bytes 524320 | tf_op jit(solution)/shard_map/kv/ppermute | solution.py:40
  119.7 3.2 %collective-permute-done.12 = bf16[256,256]{1,0:T(8,128)(2,1)S(1)} collective-permute-done((bf16[256,256]{1,0:T(8,128)(2,1)S(1)}, bf16[256,256]{1,0:T(8,128)(2,1)S(1)}, u32[]{:S(2)}, u32[]{:S(2)}) %collective-permute-start.12) | collective-permute-done | bytes 131104 | tf_op jit(solution)/shard_map/kv/ppermute | solution.py:40
  123.7 5.7 %all-to-all-start = ((bf16[16,32,256]{2,1,0:T(8,128)(2,1)}), bf16[16,32,256]{2,1,0:T(8,128)(2,1)S(1)}, u32[]{:S(2)}, u32[]{:S(2)}) async-start(bf16[16,32,256]{2,1,0:T(8,128)(2,1)} %bitcast.16), calls=%async_computation | async-start | bytes 524288 | tf_op jit(solution)/shard_map/kv/all_to_all | solution.py:325
  131.1 6.8 %query.1.query_ref = bf16[128,512]{1,0:T(8,128)(2,1)} custom-call(bf16[16,144,512]{2,1,0:T(8,128)(2,1)} %bitcast.66, bf16[8192,512]{1,0:T(8,128)(2,1)} %weight_ref.3), custom_call_target="tpu_custom_call" | custom-call | flops 1073741824 | bytes 12582912 | tf_op jit(solution)/shard_map/query/pallas_call | solution.py:161
  138.6 8.2 %attend.1 = bf16[4,4,128,512]{3,2,1,0:T(8,128)(2,1)} custom-call(s32[16]{0:T(128)} %fusion.14.place_ref, bf16[128,512]{1,0:T(8,128)(2,1)} %query.1.query_ref, bf16[512,256]{1,0:T(8,128)(2,1)} %bitcast.68, s32[128,1]{1,0:T(8,128)} %copy.27.row_ref, s32[1,512]{1,0:T(1,128)} %reshape.67.col_ref, bf16[512,8192]{1,0:T(8,128)(2,1)} %weight_ref.5), custom_call_target="tpu_custom_call" | custom-call | flops 1073741824 | bytes 12582912 | tf_op jit(solution)/shard_map/attend/pallas_call | solution.py:218
  151.8 5.7 %collective-permute-done.13 = bf16[4,128,512]{2,1,0:T(8,128)(2,1)S(1)} collective-permute-done((bf16[4,128,512]{2,1,0:T(8,128)(2,1)S(1)}, bf16[4,128,512]{2,1,0:T(8,128)(2,1)S(1)}, u32[]{:S(2)}, u32[]{:S(2)}) %collective-permute-start.13) | collective-permute-done | bytes 524320 | tf_op jit(solution)/shard_map/mix/ppermute | solution.py:40
  157.5 7.4 %collective-permute-done.14 = bf16[4,128,512]{2,1,0:T(8,128)(2,1)S(1)} collective-permute-done((bf16[4,128,512]{2,1,0:T(8,128)(2,1)S(1)}, bf16[4,128,512]{2,1,0:T(8,128)(2,1)S(1)}, u32[]{:S(2)}, u32[]{:S(2)}) %collective-permute-start.14) | collective-permute-done | bytes 524320 | tf_op jit(solution)/shard_map/mix/ppermute | solution.py:40
  166.8 2.8 %collective-permute-start.17 = (bf16[128,512]{1,0:T(8,128)(2,1)S(1)}, bf16[128,512]{1,0:T(8,128)(2,1)S(1)}, u32[]{:S(2)}, u32[]{:S(2)}) collective-permute-start(bf16[128,512]{1,0:T(8,128)(2,1)S(1)} %get-tuple-element.21), channel_id=1, source_target_pairs={{0,12},{1,13},{2,14},{3,15},{4,0},{5,1},{6,2},{7,3},{8,4},{9,5},{1... | collective-permute-start | bytes 393224 | tf_op jit(solution)/shard_map/mix/ppermute | solution.py:40
  173.5 2.5 %collective-permute-done.18 = bf16[128,512]{1,0:T(8,128)(2,1)S(1)} collective-permute-done((bf16[128,512]{1,0:T(8,128)(2,1)S(1)}, bf16[128,512]{1,0:T(8,128)(2,1)S(1)}, u32[]{:S(2)}, u32[]{:S(2)}) %collective-permute-start.18) | collective-permute-done | bytes 131104 | tf_op jit(solution)/shard_map/mix/ppermute | solution.py:40
  (78 shorter events, 39.0 us)
Async XLA Ops:
  6.5 111.6 %copy-start = (s32[8,16]{1,0:T(8,128)S(1)}, s32[8,16]{1,0:T(8,128)}, u32[]{:S(2)}) copy-start(s32[8,16]{1,0:T(8,128)} %param.15) | copy-start | bytes 1540
  6.5 124.6 %all-gather.3.cloned.1.call-start = ((), (), s32[]{:S(2)}) async-start(), calls=%async_computation.1 | async-start | bytes 2506752 | tf_op jit(solution)/shard_map/gather_states/all_gather | solution.py:291
  7.9 21.7 %copy-start.8 = (s32[4]{0:T(128)S(1)}, s32[4]{0:T(128)}, u32[]{:S(2)}) copy-start(s32[4]{0:T(128)} %constant.134) | copy-start | bytes 52
  7.9 8.9 %collective-permute-start = (bf16[1,480,512]{2,1,0:T(8,128)(2,1)S(1)}, bf16[1,480,512]{2,1,0:T(8,128)(2,1)S(1)}, u32[]{:S(2)}, u32[]{:S(2)}) collective-permute-start(bf16[1,480,512]{2,1,0:T(8,128)(2,1)S(1)} %copy.26), channel_id=1, source_target_pairs={{0,1},{1,2},{2,3},{3,0},{4,5},{5,6},{6,7},{7,4},{8,9},{9,10},{10,1... | collective-permute-start | bytes 1474568 | tf_op jit(solution)/shard_map/gather_rows/ppermute | solution.py:40
  8.4 15.3 %collective-permute-start.1 = (bf16[1,480,512]{2,1,0:T(8,128)(2,1)S(1)}, bf16[1,480,512]{2,1,0:T(8,128)(2,1)S(1)}, u32[]{:S(2)}, u32[]{:S(2)}) collective-permute-start(bf16[1,480,512]{2,1,0:T(8,128)(2,1)S(1)} %copy.26), channel_id=1, source_target_pairs={{0,3},{1,0},{2,1},{3,2},{4,7},{5,4},{6,5},{7,6},{8,11},{9,8},{10,9... | collective-permute-start | bytes 1474568 | tf_op jit(solution)/shard_map/gather_rows/ppermute | solution.py:40
  10.0 13.8 %collective-permute-start.2 = (bf16[1,480,512]{2,1,0:T(8,128)(2,1)S(1)}, bf16[1,480,512]{2,1,0:T(8,128)(2,1)S(1)}, u32[]{:S(2)}, u32[]{:S(2)}) collective-permute-start(bf16[1,480,512]{2,1,0:T(8,128)(2,1)S(1)} %copy.26), channel_id=1, source_target_pairs={{0,2},{1,3},{2,0},{3,1},{4,6},{5,7},{6,4},{7,5},{8,10},{9,11},{10,... | collective-permute-start | bytes 1474568 | tf_op jit(solution)/shard_map/gather_rows/ppermute | solution.py:40
  24.0 29.2 %collective-permute-start.3 = (bf16[4,480,512]{2,1,0:T(8,128)(2,1)S(1)}, bf16[4,480,512]{2,1,0:T(8,128)(2,1)}, u32[]{:S(2)}, u32[]{:S(2)}) collective-permute-start(bf16[4,480,512]{2,1,0:T(8,128)(2,1)S(1)} %pad_maximum_fusion.refs_0_), channel_id=1, source_target_pairs={{0,4},{1,5},{2,6},{3,7},{4,8},{5,9},{6,10},{7,11},{8,12},{9,13},{1... | collective-permute-start | bytes 5898248 | tf_op jit(solution)/shard_map/gather_rows/ppermute | solution.py:40
  26.0 27.2 %collective-permute-start.4 = (bf16[4,480,512]{2,1,0:T(8,128)(2,1)S(1)}, bf16[4,480,512]{2,1,0:T(8,128)(2,1)}, u32[]{:S(2)}, u32[]{:S(2)}) collective-permute-start(bf16[4,480,512]{2,1,0:T(8,128)(2,1)S(1)} %pad_maximum_fusion.refs_0_), channel_id=1, source_target_pairs={{0,12},{1,13},{2,14},{3,15},{4,0},{5,1},{6,2},{7,3},{8,4},{9,5},{1... | collective-permute-start | bytes 5898248 | tf_op jit(solution)/shard_map/gather_rows/ppermute | solution.py:40
  54.5 24.9 %collective-permute-start.5 = (bf16[2,480,512]{2,1,0:T(8,128)(2,1)S(1)}, bf16[2,480,512]{2,1,0:T(8,128)(2,1)S(1)}, u32[]{:S(2)}, u32[]{:S(2)}) collective-permute-start(bf16[2,480,512]{2,1,0:T(8,128)(2,1)S(1)} %slice.54), channel_id=1, source_target_pairs={{0,4},{1,5},{2,6},{3,7},{4,8},{5,9},{6,10},{7,11},{8,12},{9,13},{1... | collective-permute-start | bytes 2949128 | tf_op jit(solution)/shard_map/gather_rows/ppermute | solution.py:40
  57.6 23.6 %collective-permute-start.6 = (bf16[2,480,512]{2,1,0:T(8,128)(2,1)S(1)}, bf16[2,480,512]{2,1,0:T(8,128)(2,1)S(1)}, u32[]{:S(2)}, u32[]{:S(2)}) collective-permute-start(bf16[2,480,512]{2,1,0:T(8,128)(2,1)S(1)} %slice.55), channel_id=1, source_target_pairs={{0,12},{1,13},{2,14},{3,15},{4,0},{5,1},{6,2},{7,3},{8,4},{9,5},{1... | collective-permute-start | bytes 2949128 | tf_op jit(solution)/shard_map/gather_rows/ppermute | solution.py:40
  95.0 9.4 %collective-permute-start.7 = (bf16[4,256,256]{2,1,0:T(8,128)(2,1)}, bf16[4,256,256]{2,1,0:T(8,128)(2,1)S(1)}, u32[]{:S(2)}, u32[]{:S(2)}) collective-permute-start(bf16[4,256,256]{2,1,0:T(8,128)(2,1)} %get-tuple-element.16), channel_id=1, source_target_pairs={{0,1},{1,2},{2,3},{3,0},{4,5},{5,6},{6,7},{7,4},{8,9},{9,10},{10,1... | collective-permute-start | bytes 1572872 | tf_op jit(solution)/shard_map/kv/ppermute | solution.py:40
  95.8 16.0 %collective-permute-start.8 = (bf16[4,256,256]{2,1,0:T(8,128)(2,1)S(1)}, bf16[4,256,256]{2,1,0:T(8,128)(2,1)S(1)}, u32[]{:S(2)}, u32[]{:S(2)}) collective-permute-start(bf16[4,256,256]{2,1,0:T(8,128)(2,1)S(1)} %get-tuple-element.18), channel_id=1, source_target_pairs={{0,3},{1,0},{2,1},{3,2},{4,7},{5,4},{6,5},{7,6},{8,11},{9,8},{10,9... | collective-permute-start | bytes 1572872 | tf_op jit(solution)/shard_map/kv/ppermute | solution.py:40
  97.0 14.8 %collective-permute-start.9 = (bf16[4,256,256]{2,1,0:T(8,128)(2,1)S(1)}, bf16[4,256,256]{2,1,0:T(8,128)(2,1)S(1)}, u32[]{:S(2)}, u32[]{:S(2)}) collective-permute-start(bf16[4,256,256]{2,1,0:T(8,128)(2,1)S(1)} %get-tuple-element.17), channel_id=1, source_target_pairs={{0,2},{1,3},{2,0},{3,1},{4,6},{5,7},{6,4},{7,5},{8,10},{9,11},{10,... | collective-permute-start | bytes 1572872 | tf_op jit(solution)/shard_map/kv/ppermute | solution.py:40
  98.9 31.3 %copy-start.10 = (s32[1,64]{1,0:T(1,128)S(1)}, s32[1,64]{1,0:T(1,128)}, u32[]{:S(2)}) copy-start(s32[1,64]{1,0:T(1,128)} %param.16) | copy-start | bytes 772
  113.1 6.2 %collective-permute-start.10 = (bf16[256,256]{1,0:T(8,128)(2,1)S(1)}, bf16[256,256]{1,0:T(8,128)(2,1)S(1)}, u32[]{:S(2)}, u32[]{:S(2)}) collective-permute-start(bf16[256,256]{1,0:T(8,128)(2,1)S(1)} %get-tuple-element.22), channel_id=1, source_target_pairs={{0,4},{1,5},{2,6},{3,7},{4,8},{5,9},{6,10},{7,11},{8,12},{9,13},{1... | collective-permute-start | bytes 393224 | tf_op jit(solution)/shard_map/kv/ppermute | solution.py:40
  114.8 5.0 %collective-permute-start.11 = (bf16[256,256]{1,0:T(8,128)(2,1)S(1)}, bf16[256,256]{1,0:T(8,128)(2,1)S(1)}, u32[]{:S(2)}, u32[]{:S(2)}) collective-permute-start(bf16[256,256]{1,0:T(8,128)(2,1)S(1)} %get-tuple-element.24), channel_id=1, source_target_pairs={{0,12},{1,13},{2,14},{3,15},{4,0},{5,1},{6,2},{7,3},{8,4},{9,5},{1... | collective-permute-start | bytes 393224 | tf_op jit(solution)/shard_map/kv/ppermute | solution.py:40
  116.4 6.5 %collective-permute-start.12 = (bf16[256,256]{1,0:T(8,128)(2,1)S(1)}, bf16[256,256]{1,0:T(8,128)(2,1)S(1)}, u32[]{:S(2)}, u32[]{:S(2)}) collective-permute-start(bf16[256,256]{1,0:T(8,128)(2,1)S(1)} %get-tuple-element.23), channel_id=1, source_target_pairs={{0,8},{1,9},{2,10},{3,11},{4,12},{5,13},{6,14},{7,15},{8,0},{9,1},... | collective-permute-start | bytes 393224 | tf_op jit(solution)/shard_map/kv/ppermute | solution.py:40
  123.7 14.2 %all-to-all-start = ((bf16[16,32,256]{2,1,0:T(8,128)(2,1)}), bf16[16,32,256]{2,1,0:T(8,128)(2,1)S(1)}, u32[]{:S(2)}, u32[]{:S(2)}) async-start(bf16[16,32,256]{2,1,0:T(8,128)(2,1)} %bitcast.16), calls=%async_computation | async-start | bytes 524288 | tf_op jit(solution)/shard_map/kv/all_to_all | solution.py:325
  148.3 9.2 %collective-permute-start.13 = (bf16[4,128,512]{2,1,0:T(8,128)(2,1)S(1)}, bf16[4,128,512]{2,1,0:T(8,128)(2,1)S(1)}, u32[]{:S(2)}, u32[]{:S(2)}) collective-permute-start(bf16[4,128,512]{2,1,0:T(8,128)(2,1)S(1)} %get-tuple-element.13), channel_id=1, source_target_pairs={{0,1},{1,2},{2,3},{3,0},{4,5},{5,6},{6,7},{7,4},{8,9},{9,10},{10,1... | collective-permute-start | bytes 1572872 | tf_op jit(solution)/shard_map/mix/ppermute | solution.py:40
  148.9 16.0 %collective-permute-start.14 = (bf16[4,128,512]{2,1,0:T(8,128)(2,1)S(1)}, bf16[4,128,512]{2,1,0:T(8,128)(2,1)S(1)}, u32[]{:S(2)}, u32[]{:S(2)}) collective-permute-start(bf16[4,128,512]{2,1,0:T(8,128)(2,1)S(1)} %get-tuple-element.15), channel_id=1, source_target_pairs={{0,3},{1,0},{2,1},{3,2},{4,7},{5,4},{6,5},{7,6},{8,11},{9,8},{10,9... | collective-permute-start | bytes 1572872 | tf_op jit(solution)/shard_map/mix/ppermute | solution.py:40
  150.4 14.5 %collective-permute-start.15 = (bf16[4,128,512]{2,1,0:T(8,128)(2,1)S(1)}, bf16[4,128,512]{2,1,0:T(8,128)(2,1)S(1)}, u32[]{:S(2)}, u32[]{:S(2)}) collective-permute-start(bf16[4,128,512]{2,1,0:T(8,128)(2,1)S(1)} %get-tuple-element.14), channel_id=1, source_target_pairs={{0,2},{1,3},{2,0},{3,1},{4,6},{5,7},{6,4},{7,5},{8,10},{9,11},{10,... | collective-permute-start | bytes 1572872 | tf_op jit(solution)/shard_map/mix/ppermute | solution.py:40
  166.3 6.2 %collective-permute-start.16 = (bf16[128,512]{1,0:T(8,128)(2,1)S(1)}, bf16[128,512]{1,0:T(8,128)(2,1)S(1)}, u32[]{:S(2)}, u32[]{:S(2)}) collective-permute-start(bf16[128,512]{1,0:T(8,128)(2,1)S(1)} %get-tuple-element.19), channel_id=1, source_target_pairs={{0,4},{1,5},{2,6},{3,7},{4,8},{5,9},{6,10},{7,11},{8,12},{9,13},{1... | collective-permute-start | bytes 393224 | tf_op jit(solution)/shard_map/mix/ppermute | solution.py:40
  166.8 6.7 %collective-permute-start.17 = (bf16[128,512]{1,0:T(8,128)(2,1)S(1)}, bf16[128,512]{1,0:T(8,128)(2,1)S(1)}, u32[]{:S(2)}, u32[]{:S(2)}) collective-permute-start(bf16[128,512]{1,0:T(8,128)(2,1)S(1)} %get-tuple-element.21), channel_id=1, source_target_pairs={{0,12},{1,13},{2,14},{3,15},{4,0},{5,1},{6,2},{7,3},{8,4},{9,5},{1... | collective-permute-start | bytes 393224 | tf_op jit(solution)/shard_map/mix/ppermute | solution.py:40
  169.6 6.5 %collective-permute-start.18 = (bf16[128,512]{1,0:T(8,128)(2,1)S(1)}, bf16[128,512]{1,0:T(8,128)(2,1)S(1)}, u32[]{:S(2)}, u32[]{:S(2)}) collective-permute-start(bf16[128,512]{1,0:T(8,128)(2,1)S(1)} %get-tuple-element.20), channel_id=1, source_target_pairs={{0,8},{1,9},{2,10},{3,11},{4,12},{5,13},{6,14},{7,15},{8,0},{9,1},... | collective-permute-start | bytes 393224 | tf_op jit(solution)/shard_map/mix/ppermute | solution.py:40
  (8 other events, 78.0 us)
Sparse Core Ops, SparseCore 0:
  29.0 48.5 all-gather.2

commit v4 on v1

v4 whole, which is shorter than its diff:
```python
import functools

import jax
import jax.numpy as jnp
from jax import lax
from jax.experimental import pallas as pl
from jax.experimental.pallas import tpu as pltpu
from jax.sharding import Mesh, PartitionSpec as P

D = 8192
KV_HEADS = 8
HEAD_DIM = 128
MAXT = 4
STEPS = 2
SIDE = 4
F32 = jnp.float32
BF16 = jnp.bfloat16
TP = ("z", "xh", "pr")
X = ("xh", "pr")
Z = "z"
EVERY = ("group",) + TP
FIRST, SECOND = 0, 1
HOPS = (0, 1, 3, 2)
GRANT = 16 * 1024 * 1024
ANY = pl.BlockSpec(memory_space=pl.ANY)
IN_HBM = pl.BlockSpec(memory_space=pltpu.HBM)
IN_VMEM = pl.BlockSpec(memory_space=pltpu.VMEM)
IN_SMEM = pl.BlockSpec(memory_space=pltpu.SMEM)


def along(value, axis, by):
    return lax.ppermute(value, axis, [(i, (i + by) % SIDE) for i in range(SIDE)])


def shift(value, groups, order, by):
    pairs = []
    for group in range(groups):
        for z in range(SIDE):
            for x in range(SIDE):
                if group % 2 == order:
                    other = z * SIDE + (x + by) % SIDE
                else:
                    other = (z + by) % SIDE * SIDE + x
                base = group * SIDE * SIDE
                pairs.append((base + z * SIDE + x, base + other))
    return lax.ppermute(value, EVERY, pairs)


def in_hbm(value):
    return pltpu.with_memory_space_constraint(value, pltpu.HBM)


def in_vmem(value):
    return pltpu.with_memory_space_constraint(value, pltpu.VMEM)


def kernel_call(kernel, operands, specs, out, scratch=(), flops=0, moved=0, transcendentals=0):
    return pl.pallas_call(
        kernel,
        in_specs=specs,
        out_specs=jax.tree.map(lambda _: IN_VMEM, out),
        out_shape=out,
        scratch_shapes=list(scratch),
        compiler_params=pltpu.CompilerParams(vmem_limit_bytes=GRANT),
        cost_estimate=pl.CostEstimate(
            flops=flops, bytes_accessed=moved, transcendentals=transcendentals
        ),
    )(*operands)


def wrap(value):
    return lax.rem(value + SIDE, SIDE)


def position():
    z = lax.axis_index("z")
    x = lax.axis_index("xh") * 2 + lax.axis_index("pr")
    return z, x, lax.rem(lax.axis_index("group"), 2)


def rank_from_here(first_by, second_by):
    z, x, core = position()
    first = jnp.where(core == 0, x, z)
    second = jnp.where(core == 0, z, x)
    first, second = wrap(first + first_by), wrap(second + second_by)
    return jnp.where(core == 0, second * SIDE + first, first * SIDE + second)


def rank_by_hops(z_hops, x_hops):
    z, x, _ = position()
    return wrap(z - z_hops) * SIDE + wrap(x - x_hops)


def join_kernel(moves, *refs):
    copies = []
    sem = refs[-1]
    for at, (source, low, target, first, count) in enumerate(moves):
        copies.append(
            pltpu.make_async_copy(
                refs[source].at[pl.ds(low, count)], refs[target].at[pl.ds(first, count)], sem.at[at]
            )
        )
    for copy in copies:
        copy.start()
    for copy in copies:
        copy.wait()


def join(arrays, moves, shapes, after=()):
    offset = len(arrays) + len(after)
    moves = [(a, low, offset + b, first, count) for a, low, b, first, count in moves]
    moved = 4 * sum(a.size for a in arrays)
    return kernel_call(
        functools.partial(join_kernel, moves),
        [*arrays, *after],
        [ANY] * offset,
        [pltpu.VMEM(shape, BF16) for shape in shapes],
        [pltpu.SemaphoreType.DMA((len(moves),))],
        moved=moved,
    )


def load_kernel(*refs):
    count = len(refs) // 3
    copies = [
        pltpu.make_async_copy(refs[i], refs[count + i], refs[2 * count + i]) for i in range(count)
    ]
    for copy in copies:
        copy.start()
    for copy in copies:
        copy.wait()


def load(*values):
    return kernel_call(
        load_kernel,
        [in_hbm(value) for value in values],
        [IN_HBM] * len(values),
        [pltpu.VMEM(value.shape, value.dtype) for value in values],
        [pltpu.SemaphoreType.DMA(()) for _ in values],
        moved=4 * sum(value.size for value in values),
    )


def add_products(sums, blocks, weight_ref):
    for ref, half, origins in blocks:
        for inner, hops in enumerate(origins):
            sums[half] = sums[half] + lax.dot_general(
                ref[inner],
                weight_ref[rank_by_hops(*hops)],
                (((0,), (0,)), ((), ())),
                preferred_element_type=F32,
            )


def project_kernel(parts, *refs):
    blocks = [(ref, *part) for ref, part in zip(refs, parts)]
    weight_ref, start_ref, out_ref, token_ref = refs[len(parts) : len(parts) + 4]
    if len(start_ref.shape) == 3:
        sums = [start_ref[0], start_ref[1]]
    else:
        rows = blocks[0][0].shape[2]
        bias = jnp.broadcast_to(start_ref[...].astype(F32), (rows, start_ref.shape[1]))
        sums = [bias, bias]
    add_products(sums, blocks, weight_ref)
    for half in range(2):
        out_ref[half] = sums[half]
    token_ref[...] = jnp.zeros_like(token_ref)


def project(start, blocks, parts, weight):
    features, rows = blocks[0].shape[1:]
    width = weight.shape[2]
    count = sum(block.shape[0] for block in blocks)
    return kernel_call(
        functools.partial(project_kernel, parts),
        [*map(in_vmem, blocks), in_vmem(weight), start],
        [IN_VMEM] * (len(blocks) + 2),
        [pltpu.VMEM((2, rows, width), F32), jax.ShapeDtypeStruct((8, 128), F32)],
        flops=2 * count * rows * features * width,
        moved=2 * count * (rows + width) * features,
    )


def kv_kernel(parts, tokens, *refs):
    blocks = [(ref, *part) for ref, part in zip(refs, parts)]
    weight_ref, kv_weight_ref, start_ref = refs[len(parts) : len(parts) + 3]
    outs = refs[len(parts) + 3 + tokens : -1]
    rows_ref = refs[-1]
    sums = [start_ref[0], start_ref[1]]
    add_products(sums, blocks, weight_ref)
    half_rows = sums[0].shape[0]
    for half in range(2):
        rows_ref[half] = sums[half].astype(BF16)
    for first_by in range(SIDE):
        for second_by in range(SIDE):
            rank = rank_from_here(first_by, second_by)
            span = pl.ds(pl.multiple_of(rank // 2 * HEAD_DIM, HEAD_DIM), HEAD_DIM)
            weight = jnp.concatenate([kv_weight_ref[0, :, span], kv_weight_ref[1, :, span]], axis=1)
            outs[first_by][second_by] = jnp.dot(
                rows_ref[lax.rem(rank, 2)], weight, preferred_element_type=F32
            ).astype(BF16)


def kv_partials(start, blocks, parts, weight, kv_weight, after):
    _, rows, width = start.shape
    return kernel_call(
        functools.partial(kv_kernel, parts, len(after)),
        [*map(in_vmem, blocks), in_vmem(weight), in_vmem(kv_weight), start, *after],
        [IN_VMEM] * (len(blocks) + 3) + [ANY] * len(after),
        [pltpu.VMEM((SIDE, rows, 2 * HEAD_DIM), BF16) for _ in range(SIDE)],
        [pltpu.VMEM((2, rows, width), BF16)],
        flops=4 * rows * width * 2 * KV_HEADS * HEAD_DIM,
        moved=8 * 1024 * 1024,
    )


def sum_kernel(copies, tokens, *refs):
    sources, outs = refs[:SIDE], refs[SIDE + tokens :]
    for at in range(sources[0].shape[0]):
        total = sources[0][at].astype(F32)
        for source in sources[1:]:
            total = total + source[at].astype(F32)
        total = total.astype(BF16)
        if copies == 1:
            outs[at][...] = total
        else:
            for twin in range(copies):
                outs[0][copies * at + twin] = total


def sum_blocks(sources, copies=1, after=()):
    count, rows, width = sources[0].shape
    if copies == 1:
        out = [pltpu.VMEM((rows, width), BF16) for _ in range(count)]
    else:
        out = [jax.ShapeDtypeStruct((count * copies, rows, width), BF16)]
    return kernel_call(
        functools.partial(sum_kernel, copies, len(after)),
        [*map(in_vmem, sources), *after],
        [IN_VMEM] * SIDE + [ANY] * len(after),
        out,
        flops=SIDE * sources[0].size,
        moved=10 * sources[0].size,
    )


def query_kernel(batch, *refs):
    parts, (weight_ref, out_ref, buffer, sem) = refs[:SIDE], refs[SIDE:]
    pieces = sem.shape[0]
    deep = buffer.shape[0] // pieces
    copies = [
        pltpu.make_async_copy(
            weight_ref.at[pl.ds(i * deep, deep)], buffer.at[pl.ds(i * deep, deep)], sem.at[i]
        )
        for i in range(pieces)
    ]
    for copy in copies:
        copy.start()
    total = jnp.zeros((batch, 1), F32)
    for part in parts:
        for block in range(SIDE):
            hidden = part[block, :batch, :].astype(F32)
            total += jnp.sum(hidden * hidden, axis=1, keepdims=True)
    inverse = lax.rsqrt(total / D + 1e-05)
    for copy in copies:
        copy.wait()
    accum = jnp.zeros(out_ref.shape, F32)
    for part, far in zip(parts, HOPS):
        width = part.shape[2]
        for block, near in enumerate(HOPS):
            hidden = part[block, :batch, :].astype(F32)
            gain = part[block, batch : batch + 16, :].astype(F32)[:1]
            normed = (hidden * inverse * gain).astype(BF16)
            rank = rank_from_here(-far, -near)
            rows = pl.ds(pl.multiple_of(rank * width, width), width)
            accum += jnp.dot(normed, buffer[rows, :], preferred_element_type=F32)
    out_ref[...] = accum.astype(BF16)


def queries(parts, query_weight, batch):
    columns = query_weight.shape[1]
    return kernel_call(
        functools.partial(query_kernel, batch),
        [*parts, in_hbm(query_weight)],
        [IN_VMEM] * SIDE + [IN_HBM],
        jax.ShapeDtypeStruct((batch, columns), BF16),
        [pltpu.VMEM(query_weight.shape, BF16), pltpu.SemaphoreType.DMA((8,))],
        flops=2 * batch * D * columns,
        moved=12 * 1024 * 1024,
    )


def attend_kernel(
    source_ref, count_ref, request_ref, query_ref, kv_ref, weight_ref, *refs
):
    outs, (buffer, sem) = refs[:SIDE], refs[SIDE:]
    batch, width = query_ref.shape
    columns = outs[0].shape[2]
    slots, tile_rows, both = kv_ref.shape
    rows = slots * tile_rows
    group = lax.axis_index("group")
    pieces = sem.shape[0]
    wide = buffer.shape[1] // pieces
    copies = []
    for first_by in range(SIDE):
        for second_by in range(SIDE):
            at = first_by * SIDE + second_by
            span = pl.ds(pl.multiple_of(rank_from_here(first_by, second_by) * wide, wide), wide)
            copies.append(
                pltpu.make_async_copy(
                    weight_ref.at[:, span], buffer.at[:, pl.ds(at * wide, wide)], sem.at[at]
                )
            )
    for copy in copies[:4]:
        copy.start()

    tile = lax.broadcasted_iota(jnp.int32, (1, rows), 1) // tile_rows
    owner = jnp.full((1, rows), -1, jnp.int32)
    for place in range(slots):
        request = place // MAXT
        valid = place % MAXT < count_ref[group * (slots // MAXT) + request]
        label = jnp.where(valid, request, -1)
        owner = jnp.where(tile == source_ref[group, place], label, owner)
    per_step = request_ref.shape[1]
    here = lax.broadcasted_iota(jnp.int32, (per_step, per_step), 0)
    there = lax.broadcasted_iota(jnp.int32, (per_step, per_step), 1)
    asked = jnp.where(here == there, request_ref[...], 0)
    asked = jnp.sum(asked, axis=1, keepdims=True)
    allowed = jnp.concatenate([asked] * (batch // per_step), axis=0) == owner

    kv = kv_ref[...].reshape(rows, both)
    keys, values = kv[:, :HEAD_DIM], kv[:, HEAD_DIM:]
    contexts = []
    for head in range(width // HEAD_DIM):
        for copy in copies[4 + 2 * head : 6 + 2 * head]:
            copy.start()
        span = slice(head * HEAD_DIM, (head + 1) * HEAD_DIM)
        scores = lax.dot_general(
            query_ref[:, span], keys, (((1,), (1,)), ((), ())), preferred_element_type=F32
        ) * (1.0 / HEAD_DIM**0.5)
        scores = jnp.where(allowed, scores, -1e30)
        largest = jnp.max(scores, axis=1, keepdims=True)
        weights = jnp.where(allowed, jnp.exp(scores - largest), 0.0)
        total = jnp.sum(weights, axis=1, keepdims=True)
        summed = jnp.dot(weights.astype(BF16), values, preferred_element_type=F32)
        contexts.append((summed / total).astype(BF16))
    for copy in copies[4 + 2 * len(contexts) :]:
        copy.start()
    context = jnp.concatenate(contexts, axis=1)
    for first_by in range(SIDE):
        for second_by in range(SIDE):
            at = first_by * SIDE + second_by
            copies[at].wait()
            branch = jnp.dot(
                context, buffer[:, at * wide : (at + 1) * wide], preferred_element_type=F32
            )
            outs[first_by][second_by] = branch.astype(BF16)


def attend(tile_source, tile_count, row_request, query, kv, out_weight):
    batch, width = query.shape
    ranks = SIDE * SIDE
    columns = out_weight.shape[1] // ranks
    return kernel_call(
        attend_kernel,
        [tile_source, tile_count, row_request, query, kv, in_hbm(out_weight)],
        [IN_SMEM, IN_SMEM, IN_VMEM, IN_VMEM, IN_VMEM, IN_HBM],
        [pltpu.VMEM((SIDE, batch, columns), BF16) for _ in range(SIDE)],
        [pltpu.VMEM(out_weight.shape, BF16), pltpu.SemaphoreType.DMA((ranks,))],
        flops=2 * batch * width * out_weight.shape[1],
        moved=12 * 1024 * 1024,
        transcendentals=batch * 4 * 512,
    )


def mix_kernel(gate_ref, local_ref, *refs):
    sources, out_ref = refs[:SIDE], refs[SIDE]
    steps, batch, width = local_ref.shape
    gate = jnp.tanh(jnp.full((1, width), gate_ref[0, 0], F32))
    for step in range(steps):
        span = slice(step * batch, (step + 1) * batch)
        total = sources[0][span].astype(F32)
        for source in sources[1:]:
            total = total + source[span].astype(F32)
        out_ref[step] = (local_ref[step].astype(F32) + gate * total).astype(BF16)


def mix(gate, local, sources):
    return kernel_call(
        mix_kernel,
        [gate.reshape(1, 1), local, *map(in_vmem, sources)],
        [IN_SMEM, IN_VMEM] + [IN_VMEM] * SIDE,
        jax.ShapeDtypeStruct(local.shape, BF16),
        flops=SIDE * local.size,
        moved=12 * local.size,
    )


def body(
    vision_rows,
    tile_count,
    tile_source,
    row_request,
    proj_weight,
    proj_bias,
    kv_weight,
    query_weight,
    out_weight,
    norm_gain,
    attn_gate,
    states,
):
    groups = lax.axis_size("group")
    ranks = lax.axis_size(TP)
    tile_rows, features = vision_rows.shape[2:]
    per_group = vision_rows.shape[1] // groups
    half_rows = groups * tile_rows
    batch = STEPS * states.shape[1]
    width = states.shape[2]
    height = batch + 16
    block = (features, half_rows)

    with jax.named_scope("gather_rows"):
        mine = vision_rows[0].reshape(groups, per_group, tile_rows, features)
        mine = mine.transpose(1, 3, 0, 2).reshape(per_group, 1, *block)
        near_a = [mine[0]] + [along(mine[0], X, by) for by in HOPS[1:]]
        near_b = [mine[1]] + [along(mine[1], Z, by) for by in HOPS[1:]]
        near_a, near_b = join(
            near_a + near_b,
            [(i, 0, i // SIDE, i % SIDE, 1) for i in range(2 * SIDE)],
            [(SIDE, *block)] * 2,
        )
        far = [along(near_a, Z, 1), along(near_a, Z, 3), along(near_b, X, 1), along(near_b, X, 3)]

    with jax.named_scope("project"):
        weight, kv_here = load(proj_weight.reshape(ranks, *block[:1], -1), kv_weight)

        def origins(across, chosen=HOPS):
            return (0, [(across, hop) for hop in chosen]), (1, [(hop, across) for hop in chosen])

        accum, token = project(proj_bias[None, :], [near_a, near_b], origins(0), weight)

    with jax.named_scope("gather_states"):
        gain_rows = jnp.broadcast_to(norm_gain[None, :], (16, width))
        (carried,) = join(
            [states.reshape(batch, width), gain_rows],
            [(0, 0, 0, 0, batch), (1, 0, 0, batch, 16)],
            [(height, width)],
            [token],
        )
        carried = carried.reshape(1, height, width)
        arrived = [shift(carried, groups, SECOND, by) for by in HOPS[1:]]

    with jax.named_scope("gather_rows"):
        cut = join(
            far,
            [(i, i % 2 * 2, i, 0, 2) for i in range(4)],
            [(2, *block)] * 4,
            [token],
        )
        last = [along(cut[0], Z, 1), along(cut[1], Z, 3), along(cut[2], X, 1), along(cut[3], X, 3)]

    with jax.named_scope("project"):
        accum, _ = project(accum, [far[0], far[2]], origins(1), weight)
        accum, _ = project(accum, [far[1], far[3]], origins(3), weight)
        low_a, low_b = origins(2, HOPS[:2])
        high_a, high_b = origins(2, HOPS[2:])
        kv = kv_partials(accum, last, (low_a, high_a, low_b, high_b), weight, kv_here, arrived)

    with jax.named_scope("gather_states"):
        (states_near,) = join(
            [carried] + arrived,
            [(i, 0, 0, i, 1) for i in range(SIDE)],
            [(SIDE, height, width)],
        )
        states_all = [states_near] + [shift(states_near, groups, FIRST, by) for by in HOPS[1:]]

    with jax.named_scope("kv"):
        kv = [kv[0]] + [shift(kv[by], groups, FIRST, by) for by in HOPS[1:]]
        kv = sum_blocks(kv, after=states_all[1:])
        kv = [kv[0]] + [shift(kv[by], groups, SECOND, by) for by in HOPS[1:]]
        kv = [part.reshape(groups, tile_rows, 2 * HEAD_DIM) for part in kv]
        (kv,) = sum_blocks(kv, copies=2)
        kv = lax.all_to_all(kv, ("group", "pr"), 0, 0)

    with jax.named_scope("query"):
        query = queries(states_all, query_weight, batch)

    with jax.named_scope("attend"):
        branch = attend(tile_source, tile_count, row_request, query, kv, out_weight)

    with jax.named_scope("mix"):
        branch = [branch[0]] + [shift(branch[by], groups, FIRST, by) for by in HOPS[1:]]
        branch = sum_blocks(branch)
        branch = [branch[0]] + [shift(branch[by], groups, SECOND, by) for by in HOPS[1:]]
        return mix(attn_gate, states, branch)


def solution(mesh):
    groups = mesh.shape["group"]
    split = Mesh(mesh.devices.reshape(groups, SIDE, 2, 2), ("group",) + TP)
    in_specs = (
        P("group", None, None, TP),
        P(),
        P(),
        P("group", None),
        P(None, TP),
        P(TP),
        P(None, TP, None),
        P(None, TP),
        P(TP, None),
        P(TP),
        P(),
        P(None, "group", TP),
    )
    out_specs = P(None, "group", TP)
    return jax.shard_map(body, mesh=split, in_specs=in_specs, out_specs=out_specs, check_vma=False)
```

time: 226 us -> 161 us (0.71)
  the two profiles are of different devices: /device:TPU:0 before, /device:TPU:30 now
where the time goes in v4:
time: 161 us; the launch traced here: 159 us
  waiting for transfers between devices  77.5 us (48%)
  starting transfers between devices  49.5 us (31%)
  Pallas kernels  29.4 us (18%)
  local copies, waits for them, and re-layouts  2.08 us (1%)
    ppermute x18, waiting for transfers between devices, shift(): return lax.ppermute(value, EVERY, pairs)  42.5 us
    ppermute x14, waiting for transfers between devices, along(): lax.ppermute(value, axis, [(i, (i + by) % SIDE) for i in range(SIDE)])  34.9 us
    pallas_call x15, Pallas kernels, kernel_call(): pl.pallas_call(kernel, in_specs=specs, out_specs=jax.tree.map(lambda _: I...  29.4 us
    ppermute x14, starting transfers between devices, along(): lax.ppermute(value, axis, [(i, (i + by) % SIDE) for i in range(SIDE)])  22.3 us
    ppermute x18, starting transfers between devices, shift(): return lax.ppermute(value, EVERY, pairs)  21.6 us
    all_to_all x1, starting transfers between devices, body(): kv = lax.all_to_all(kv, ('group', 'pr'), 0, 0)  5.61 us
  transfers between devices with their start and end apart: 33, of which 22 were waited for; matrix products, arithmetic and copies ran while one was open for 1% of the time, Pallas kernels for 11%

profile of v4, /device:TPU:30, one launch (start us, length us, event | category | flops | bytes accessed | tf_op | source)
XLA Modules:
  0.0 159.3 jit_solution(12338941741128127355)
XLA Ops:
  10.2 3.9 %collective-permute-start.5 = (bf16[1,480,256]{2,1,0:T(8,128)(2,1)S(1)}, bf16[1,480,256]{2,1,0:T(8,128)(2,1)S(1)}, u32[]{:S(2)}, u32[]{:S(2)}) collective-permute-start(bf16[1,480,256]{2,1,0:T(8,128)(2,1)S(1)} %copy.22.refs_4_), channel_id=1, source_target_pairs={{0,8},{4,12},{8,0},{12,4},{1,9},{5,13},{9,1},{13,5},{2,10},{6,14},... | collective-permute-start | bytes 737288 | tf_op jit(solution)/shard_map/gather_rows/ppermute | solution.py:32
  15.7 3.1 %collective-permute-done.4.refs_6_ = bf16[1,480,256]{2,1,0:T(8,128)(2,1)S(1)} collective-permute-done((bf16[1,480,256]{2,1,0:T(8,128)(2,1)S(1)}, bf16[1,480,256]{2,1,0:T(8,128)(2,1)S(1)}, u32[]{:S(2)}, u32[]{:S(2)}) %collective-permute-start.4) | collective-permute-done | bytes 245792 | tf_op jit(solution)/shard_map/gather_rows/ppermute | solution.py:32
  20.6 2.6 %gather_rows.2 = (bf16[4,480,256]{2,1,0:T(8,128)(2,1)S(1)}, bf16[4,480,256]{2,1,0:T(8,128)(2,1)S(1)}) custom-call(bf16[1,480,256]{2,1,0:T(8,128)(2,1)S(1)} %copy.21.refs_0_, bf16[1,480,256]{2,1,0:T(8,128)(2,1)S(1)} %collective-permute-done.refs_1_, bf16[1,480,256]{2,1,0:T(8,128)(2,1)S(1)} %collective-permute-done.1.refs_2_, ...), custom_call_target="tpu_custom_call" | custom-call | bytes 3932160 | tf_op jit(solution)/shard_map/gather_rows/pallas_call | solution.py:58
  29.3 3.9 %project.5 = (bf16[16,480,512]{2,1,0:T(8,128)(2,1)S(1)}, bf16[2,512,1024]{2,1,0:T(8,128)(2,1)S(1)}) custom-call(bf16[16,480,512]{2,1,0:T(8,128)(2,1)} %bitcast.24, bf16[2,512,1024]{2,1,0:T(8,128)(2,1)} %refs_1_.1), custom_call_target="tpu_custom_call" | custom-call | bytes 19922944 | tf_op jit(solution)/shard_map/project/pallas_call | solution.py:58
  34.8 11.4 %collective-permute-done.12.refs_0_ = bf16[4,480,256]{2,1,0:T(8,128)(2,1)S(1)} collective-permute-done((bf16[4,480,256]{2,1,0:T(8,128)(2,1)S(1)}, bf16[4,480,256]{2,1,0:T(8,128)(2,1)S(1)}, u32[]{:S(2)}, u32[]{:S(2)}) %collective-permute-start.12) | collective-permute-done | bytes 983072 | tf_op jit(solution)/shard_map/gather_rows/ppermute | solution.py:32
  47.1 3.3 %collective-permute-start.8 = (bf16[1,144,512]{2,1,0:T(8,128)(2,1)S(1)}, bf16[1,144,512]{2,1,0:T(8,128)(2,1)S(1)}, u32[]{:S(2)}, u32[]{:S(2)}) collective-permute-start(bf16[1,144,512]{2,1,0:T(8,128)(2,1)S(1)} %bitcast.17), channel_id=1, source_target_pairs={{0,8},{1,9},{2,10},{3,11},{4,12},{5,13},{6,14},{7,15},{8,0},{9,1},... | collective-permute-start | bytes 442376 | tf_op jit(solution)/shard_map/gather_states/ppermute | solution.py:46
  50.5 3.4 %collective-permute-done.15.refs_3_.refs_1_ = bf16[4,480,256]{2,1,0:T(8,128)(2,1)S(1)} collective-permute-done((bf16[4,480,256]{2,1,0:T(8,128)(2,1)S(1)}, bf16[4,480,256]{2,1,0:T(8,128)(2,1)S(1)}, u32[]{:S(2)}, u32[]{:S(2)}) %collective-permute-start.15) | collective-permute-done | bytes 983072 | tf_op jit(solution)/shard_map/gather_rows/ppermute | solution.py:32
  55.2 3.2 %collective-permute-start.17 = (bf16[2,480,256]{2,1,0:T(8,128)(2,1)S(1)}, bf16[2,480,256]{2,1,0:T(8,128)(2,1)S(1)}, u32[]{:S(2)}, u32[]{:S(2)}) collective-permute-start(bf16[2,480,256]{2,1,0:T(8,128)(2,1)S(1)} %get-tuple-element.38), channel_id=1, source_target_pairs={{0,12},{4,0},{8,4},{12,8},{1,13},{5,1},{9,5},{13,9},{2,14},{6,2},{... | collective-permute-start | bytes 1474568 | tf_op jit(solution)/shard_map/gather_rows/ppermute | solution.py:32
  64.7 9.4 %collective-permute-done.16.refs_0_ = bf16[2,480,256]{2,1,0:T(8,128)(2,1)S(1)} collective-permute-done((bf16[2,480,256]{2,1,0:T(8,128)(2,1)S(1)}, bf16[2,480,256]{2,1,0:T(8,128)(2,1)S(1)}, u32[]{:S(2)}, u32[]{:S(2)}) %collective-permute-start.16) | collective-permute-done | bytes 491552 | tf_op jit(solution)/shard_map/gather_rows/ppermute | solution.py:32
  76.3 2.8 %project.9 = (bf16[4,256,256]{2,1,0:T(8,128)(2,1)S(1)}, bf16[4,256,256]{2,1,0:T(8,128)(2,1)S(1)}, bf16[4,256,256]{2,1,0:T(8,128)(2,1)S(1)}, bf16[4,256,256]{2,1,0:T(8,128)(2,1)S(1)}) custom-call(bf16[2,480,256]{2,1,0:T(8,128)(2,1)S(1)} %collective-permute-done.16.refs_0_, bf16[2,480,256]{2,1,0:T(8,128)(2,1)S(1)} %collective-permute-done.17.refs_1_, ...), custom_call_target="tpu_custom_call" | custom-call | flops 1073741824 | bytes 8388608 | tf_op jit(solution)/shard_map/project/pallas_call | solution.py:58
  85.5 3.4 %collective-permute-done.9.refs_1_.refs_4_ = bf16[4,144,512]{2,1,0:T(8,128)(2,1)S(1)} collective-permute-done((bf16[4,144,512]{2,1,0:T(8,128)(2,1)S(1)}, bf16[4,144,512]{2,1,0:T(8,128)(2,1)S(1)}, u32[]{:S(2)}, u32[]{:S(2)}) %collective-permute-start.9) | collective-permute-done | bytes 589856 | tf_op jit(solution)/shard_map/gather_states/ppermute | solution.py:46
  88.8 7.7 %collective-permute-done.20.refs_1_ = bf16[4,256,256]{2,1,0:T(8,128)(2,1)S(1)} collective-permute-done((bf16[4,256,256]{2,1,0:T(8,128)(2,1)S(1)}, bf16[4,256,256]{2,1,0:T(8,128)(2,1)S(1)}, u32[]{:S(2)}, u32[]{:S(2)}) %collective-permute-start.20) | collective-permute-done | bytes 524320 | tf_op jit(solution)/shard_map/kv/ppermute | solution.py:46
  96.5 3.0 %collective-permute-done.22.refs_3_ = bf16[4,256,256]{2,1,0:T(8,128)(2,1)S(1)} collective-permute-done((bf16[4,256,256]{2,1,0:T(8,128)(2,1)S(1)}, bf16[4,256,256]{2,1,0:T(8,128)(2,1)S(1)}, u32[]{:S(2)}, u32[]{:S(2)}) %collective-permute-start.22) | collective-permute-done | bytes 524320 | tf_op jit(solution)/shard_map/kv/ppermute | solution.py:46
  99.8 3.2 %collective-permute-start.24 = (bf16[256,256]{1,0:T(8,128)(2,1)S(1)}, bf16[256,256]{1,0:T(8,128)(2,1)S(1)}, u32[]{:S(2)}, u32[]{:S(2)}) collective-permute-start(bf16[256,256]{1,0:T(8,128)(2,1)S(1)} %get-tuple-element.51), channel_id=1, source_target_pairs={{0,12},{1,13},{2,14},{3,15},{4,0},{5,1},{6,2},{7,3},{8,4},{9,5},{1... | collective-permute-start | bytes 393224 | tf_op jit(solution)/shard_map/kv/ppermute | solution.py:46
  104.0 3.0 %collective-permute-done.24 = bf16[256,256]{1,0:T(8,128)(2,1)S(1)} collective-permute-done((bf16[256,256]{1,0:T(8,128)(2,1)S(1)}, bf16[256,256]{1,0:T(8,128)(2,1)S(1)}, u32[]{:S(2)}, u32[]{:S(2)}) %collective-permute-start.24) | collective-permute-done | bytes 131104 | tf_op jit(solution)/shard_map/kv/ppermute | solution.py:46
  107.0 2.7 %collective-permute-done.25 = bf16[256,256]{1,0:T(8,128)(2,1)S(1)} collective-permute-done((bf16[256,256]{1,0:T(8,128)(2,1)S(1)}, bf16[256,256]{1,0:T(8,128)(2,1)S(1)}, u32[]{:S(2)}, u32[]{:S(2)}) %collective-permute-start.25) | collective-permute-done | bytes 131104 | tf_op jit(solution)/shard_map/kv/ppermute | solution.py:46
  111.4 5.6 %all-to-all-start = ((bf16[16,32,256]{2,1,0:T(8,128)(2,1)}), bf16[16,32,256]{2,1,0:T(8,128)(2,1)S(1)}, u32[]{:S(2)}, u32[]{:S(2)}) async-start(bf16[16,32,256]{2,1,0:T(8,128)(2,1)} %kv.3), calls=%async_computation | async-start | bytes 524288 | tf_op jit(solution)/shard_map/kv/all_to_all | solution.py:485
  117.0 4.7 %query.1.query_ref = bf16[128,512]{1,0:T(8,128)(2,1)S(1)} custom-call(bf16[4,144,512]{2,1,0:T(8,128)(2,1)S(1)} %gather_states.3.refs_0_, bf16[4,144,512]{2,1,0:T(8,128)(2,1)S(1)} %collective-permute-done.9.refs_1_.refs_4_, bf16[4,144,512]{2,1,0:T(8,128)(2,1)S(1)} %collective-permute-done.10.refs_2_.refs_5_, ...), custom_call_target="tpu_custom_call" | custom-call | flops 1073741824 | bytes 12582912 | tf_op jit(solution)/shard_map/query/pallas_call | solution.py:58
  121.9 6.5 %attend.1 = (bf16[4,128,512]{2,1,0:T(8,128)(2,1)S(1)}, bf16[4,128,512]{2,1,0:T(8,128)(2,1)S(1)}, bf16[4,128,512]{2,1,0:T(8,128)(2,1)S(1)}, bf16[4,128,512]{2,1,0:T(8,128)(2,1)S(1)}) custom-call(s32[8,16]{1,0:T(8,128)S(1)} %copy-done.1, s32[32]{0:T(128)S(1)} %copy-done.2, s32[1,64]{1,0:T(1,128)S(1)} %copy-done.3, bf16[128,512]{1,0:T(8,128)(2,1)S(1)} %query.1.query_ref, ...), custom_call_target="tpu_custom_call" | custom-call | flops 1073741824 | bytes 12582912 | tf_op jit(solution)/shard_map/attend/pallas_call | solution.py:58
  128.4 4.1 %collective-permute-start.26 = (bf16[4,128,512]{2,1,0:T(8,128)(2,1)S(1)}, bf16[4,128,512]{2,1,0:T(8,128)(2,1)S(1)}, u32[]{:S(2)}, u32[]{:S(2)}) collective-permute-start(bf16[4,128,512]{2,1,0:T(8,128)(2,1)S(1)} %get-tuple-element.54), channel_id=1, source_target_pairs={{0,1},{1,2},{2,3},{3,0},{4,5},{5,6},{6,7},{7,4},{8,9},{9,10},{10,1... | collective-permute-start | bytes 1572872 | tf_op jit(solution)/shard_map/mix/ppermute | solution.py:46
  134.8 10.0 %collective-permute-done.26.refs_1_ = bf16[4,128,512]{2,1,0:T(8,128)(2,1)S(1)} collective-permute-done((bf16[4,128,512]{2,1,0:T(8,128)(2,1)S(1)}, bf16[4,128,512]{2,1,0:T(8,128)(2,1)S(1)}, u32[]{:S(2)}, u32[]{:S(2)}) %collective-permute-start.26) | collective-permute-done | bytes 524320 | tf_op jit(solution)/shard_map/mix/ppermute | solution.py:46
  144.8 3.7 %collective-permute-done.27.refs_2_ = bf16[4,128,512]{2,1,0:T(8,128)(2,1)S(1)} collective-permute-done((bf16[4,128,512]{2,1,0:T(8,128)(2,1)S(1)}, bf16[4,128,512]{2,1,0:T(8,128)(2,1)S(1)}, u32[]{:S(2)}, u32[]{:S(2)}) %collective-permute-start.27) | collective-permute-done | bytes 524320 | tf_op jit(solution)/shard_map/mix/ppermute | solution.py:46
  148.9 3.2 %collective-permute-start.30 = (bf16[128,512]{1,0:T(8,128)(2,1)S(1)}, bf16[128,512]{1,0:T(8,128)(2,1)S(1)}, u32[]{:S(2)}, u32[]{:S(2)}) collective-permute-start(bf16[128,512]{1,0:T(8,128)(2,1)S(1)} %get-tuple-element.59), channel_id=1, source_target_pairs={{0,12},{1,13},{2,14},{3,15},{4,0},{5,1},{6,2},{7,3},{8,4},{9,5},{1... | collective-permute-start | bytes 393224 | tf_op jit(solution)/shard_map/mix/ppermute | solution.py:46
  156.0 2.5 %collective-permute-done.31.refs_3_ = bf16[128,512]{1,0:T(8,128)(2,1)S(1)} collective-permute-done((bf16[128,512]{1,0:T(8,128)(2,1)S(1)}, bf16[128,512]{1,0:T(8,128)(2,1)S(1)}, u32[]{:S(2)}, u32[]{:S(2)}) %collective-permute-start.31) | collective-permute-done | bytes 131104 | tf_op jit(solution)/shard_map/mix/ppermute | solution.py:46
  (73 shorter events, 48.3 us)
Async XLA Ops:
  1.8 13.9 %collective-permute-start.1 = (bf16[1,480,256]{2,1,0:T(8,128)(2,1)S(1)}, bf16[1,480,256]{2,1,0:T(8,128)(2,1)S(1)}, u32[]{:S(2)}, u32[]{:S(2)}) collective-permute-start(bf16[1,480,256]{2,1,0:T(8,128)(2,1)S(1)} %copy.21.refs_0_), channel_id=1, source_target_pairs={{0,3},{1,0},{2,1},{3,2},{4,7},{5,4},{6,5},{7,6},{8,11},{9,8},{10,9... | collective-permute-start | bytes 737288 | tf_op jit(solution)/shard_map/gather_rows/ppermute | solution.py:32
  3.4 12.3 %collective-permute-start.2 = (bf16[1,480,256]{2,1,0:T(8,128)(2,1)S(1)}, bf16[1,480,256]{2,1,0:T(8,128)(2,1)S(1)}, u32[]{:S(2)}, u32[]{:S(2)}) collective-permute-start(bf16[1,480,256]{2,1,0:T(8,128)(2,1)S(1)} %copy.21.refs_0_), channel_id=1, source_target_pairs={{0,2},{1,3},{2,0},{3,1},{4,6},{5,7},{6,4},{7,5},{8,10},{9,11},{10,... | collective-permute-start | bytes 737288 | tf_op jit(solution)/shard_map/gather_rows/ppermute | solution.py:32
  4.9 10.8 %collective-permute-start.3 = (bf16[1,480,256]{2,1,0:T(8,128)(2,1)S(1)}, bf16[1,480,256]{2,1,0:T(8,128)(2,1)S(1)}, u32[]{:S(2)}, u32[]{:S(2)}) collective-permute-start(bf16[1,480,256]{2,1,0:T(8,128)(2,1)S(1)} %copy.22.refs_4_), channel_id=1, source_target_pairs={{0,4},{4,8},{8,12},{12,0},{1,5},{5,9},{9,13},{13,1},{2,6},{6,10},{... | collective-permute-start | bytes 737288 | tf_op jit(solution)/shard_map/gather_rows/ppermute | solution.py:32
  6.9 11.9 %collective-permute-start.4 = (bf16[1,480,256]{2,1,0:T(8,128)(2,1)S(1)}, bf16[1,480,256]{2,1,0:T(8,128)(2,1)S(1)}, u32[]{:S(2)}, u32[]{:S(2)}) collective-permute-start(bf16[1,480,256]{2,1,0:T(8,128)(2,1)S(1)} %copy.22.refs_4_), channel_id=1, source_target_pairs={{0,12},{4,0},{8,4},{12,8},{1,13},{5,1},{9,5},{13,9},{2,14},{6,2},{... | collective-permute-start | bytes 737288 | tf_op jit(solution)/shard_map/gather_rows/ppermute | solution.py:32
  23.2 23.0 %collective-permute-start.12 = (bf16[4,480,256]{2,1,0:T(8,128)(2,1)S(1)}, bf16[4,480,256]{2,1,0:T(8,128)(2,1)S(1)}, u32[]{:S(2)}, u32[]{:S(2)}) collective-permute-start(bf16[4,480,256]{2,1,0:T(8,128)(2,1)S(1)} %get-tuple-element.33.refs_0_), channel_id=1, source_target_pairs={{0,4},{4,8},{8,12},{12,0},{1,5},{5,9},{9,13},{13,1},{2,6},{6,10},{... | collective-permute-start | bytes 2949128 | tf_op jit(solution)/shard_map/gather_rows/ppermute | solution.py:32
  24.4 22.7 %collective-permute-start.14 = (bf16[4,480,256]{2,1,0:T(8,128)(2,1)S(1)}, bf16[4,480,256]{2,1,0:T(8,128)(2,1)S(1)}, u32[]{:S(2)}, u32[]{:S(2)}) collective-permute-start(bf16[4,480,256]{2,1,0:T(8,128)(2,1)S(1)} %get-tuple-element.34.refs_1_), channel_id=1, source_target_pairs={{0,1},{1,2},{2,3},{3,0},{4,5},{5,6},{6,7},{7,4},{8,9},{9,10},{10,1... | collective-permute-start | bytes 2949128 | tf_op jit(solution)/shard_map/gather_rows/ppermute | solution.py:32
  26.5 24.0 %collective-permute-start.13 = (bf16[4,480,256]{2,1,0:T(8,128)(2,1)S(1)}, bf16[4,480,256]{2,1,0:T(8,128)(2,1)S(1)}, u32[]{:S(2)}, u32[]{:S(2)}) collective-permute-start(bf16[4,480,256]{2,1,0:T(8,128)(2,1)S(1)} %get-tuple-element.33.refs_0_), channel_id=1, source_target_pairs={{0,12},{4,0},{8,4},{12,8},{1,13},{5,1},{9,5},{13,9},{2,14},{6,2},{... | collective-permute-start | bytes 2949128 | tf_op jit(solution)/shard_map/gather_rows/ppermute | solution.py:32
  28.6 25.3 %collective-permute-start.15 = (bf16[4,480,256]{2,1,0:T(8,128)(2,1)S(1)}, bf16[4,480,256]{2,1,0:T(8,128)(2,1)S(1)}, u32[]{:S(2)}, u32[]{:S(2)}) collective-permute-start(bf16[4,480,256]{2,1,0:T(8,128)(2,1)S(1)} %get-tuple-element.34.refs_1_), channel_id=1, source_target_pairs={{0,3},{1,0},{2,1},{3,2},{4,7},{5,4},{6,5},{7,6},{8,11},{9,8},{10,9... | collective-permute-start | bytes 2949128 | tf_op jit(solution)/shard_map/gather_rows/ppermute | solution.py:32
  34.7 23.7 %collective-permute-start.6 = (bf16[1,144,512]{2,1,0:T(8,128)(2,1)S(1)}, bf16[1,144,512]{2,1,0:T(8,128)(2,1)S(1)}, u32[]{:S(2)}, u32[]{:S(2)}) collective-permute-start(bf16[1,144,512]{2,1,0:T(8,128)(2,1)S(1)} %bitcast.15), channel_id=1, source_target_pairs={{0,4},{1,5},{2,6},{3,7},{4,8},{5,9},{6,10},{7,11},{8,12},{9,13},{1... | collective-permute-start | bytes 442376 | tf_op jit(solution)/shard_map/gather_states/ppermute | solution.py:46
  46.2 12.6 %collective-permute-start.7 = (bf16[1,144,512]{2,1,0:T(8,128)(2,1)S(1)}, bf16[1,144,512]{2,1,0:T(8,128)(2,1)S(1)}, u32[]{:S(2)}, u32[]{:S(2)}) collective-permute-start(bf16[1,144,512]{2,1,0:T(8,128)(2,1)S(1)} %bitcast.16), channel_id=1, source_target_pairs={{0,12},{1,13},{2,14},{3,15},{4,0},{5,1},{6,2},{7,3},{8,4},{9,5},{1... | collective-permute-start | bytes 442376 | tf_op jit(solution)/shard_map/gather_states/ppermute | solution.py:46
  47.1 13.3 %collective-permute-start.8 = (bf16[1,144,512]{2,1,0:T(8,128)(2,1)S(1)}, bf16[1,144,512]{2,1,0:T(8,128)(2,1)S(1)}, u32[]{:S(2)}, u32[]{:S(2)}) collective-permute-start(bf16[1,144,512]{2,1,0:T(8,128)(2,1)S(1)} %bitcast.17), channel_id=1, source_target_pairs={{0,8},{1,9},{2,10},{3,11},{4,12},{5,13},{6,14},{7,15},{8,0},{9,1},... | collective-permute-start | bytes 442376 | tf_op jit(solution)/shard_map/gather_states/ppermute | solution.py:46
  55.1 19.0 %collective-permute-start.16 = (bf16[2,480,256]{2,1,0:T(8,128)(2,1)S(1)}, bf16[2,480,256]{2,1,0:T(8,128)(2,1)S(1)}, u32[]{:S(2)}, u32[]{:S(2)}) collective-permute-start(bf16[2,480,256]{2,1,0:T(8,128)(2,1)S(1)} %get-tuple-element.37), channel_id=1, source_target_pairs={{0,4},{4,8},{8,12},{12,0},{1,5},{5,9},{9,13},{13,1},{2,6},{6,10},{... | collective-permute-start | bytes 1474568 | tf_op jit(solution)/shard_map/gather_rows/ppermute | solution.py:32
  55.2 21.1 %collective-permute-start.17 = (bf16[2,480,256]{2,1,0:T(8,128)(2,1)S(1)}, bf16[2,480,256]{2,1,0:T(8,128)(2,1)S(1)}, u32[]{:S(2)}, u32[]{:S(2)}) collective-permute-start(bf16[2,480,256]{2,1,0:T(8,128)(2,1)S(1)} %get-tuple-element.38), channel_id=1, source_target_pairs={{0,12},{4,0},{8,4},{12,8},{1,13},{5,1},{9,5},{13,9},{2,14},{6,2},{... | collective-permute-start | bytes 1474568 | tf_op jit(solution)/shard_map/gather_rows/ppermute | solution.py:32
  58.4 17.9 %collective-permute-start.18 = (bf16[2,480,256]{2,1,0:T(8,128)(2,1)S(1)}, bf16[2,480,256]{2,1,0:T(8,128)(2,1)S(1)}, u32[]{:S(2)}, u32[]{:S(2)}) collective-permute-start(bf16[2,480,256]{2,1,0:T(8,128)(2,1)S(1)} %get-tuple-element.39), channel_id=1, source_target_pairs={{0,1},{1,2},{2,3},{3,0},{4,5},{5,6},{6,7},{7,4},{8,9},{9,10},{10,1... | collective-permute-start | bytes 1474568 | tf_op jit(solution)/shard_map/gather_rows/ppermute | solution.py:32
  58.7 17.5 %collective-permute-start.19 = (bf16[2,480,256]{2,1,0:T(8,128)(2,1)S(1)}, bf16[2,480,256]{2,1,0:T(8,128)(2,1)S(1)}, u32[]{:S(2)}, u32[]{:S(2)}) collective-permute-start(bf16[2,480,256]{2,1,0:T(8,128)(2,1)S(1)} %get-tuple-element.40), channel_id=1, source_target_pairs={{0,3},{1,0},{2,1},{3,2},{4,7},{5,4},{6,5},{7,6},{8,11},{9,8},{10,9... | collective-permute-start | bytes 1474568 | tf_op jit(solution)/shard_map/gather_rows/ppermute | solution.py:32
  61.2 20.0 %collective-permute-start.10 = (bf16[4,144,512]{2,1,0:T(8,128)(2,1)S(1)}, bf16[4,144,512]{2,1,0:T(8,128)(2,1)S(1)}, u32[]{:S(2)}, u32[]{:S(2)}) collective-permute-start(bf16[4,144,512]{2,1,0:T(8,128)(2,1)S(1)} %gather_states.3.refs_0_), channel_id=1, source_target_pairs={{0,3},{1,0},{2,1},{3,2},{4,7},{5,4},{6,5},{7,6},{8,11},{9,8},{10,9... | collective-permute-start | bytes 1769480 | tf_op jit(solution)/shard_map/gather_states/ppermute | solution.py:46
  74.1 11.4 %collective-permute-start.11 = (bf16[4,144,512]{2,1,0:T(8,128)(2,1)S(1)}, bf16[4,144,512]{2,1,0:T(8,128)(2,1)S(1)}, u32[]{:S(2)}, u32[]{:S(2)}) collective-permute-start(bf16[4,144,512]{2,1,0:T(8,128)(2,1)S(1)} %gather_states.3.refs_0_), channel_id=1, source_target_pairs={{0,2},{1,3},{2,0},{3,1},{4,6},{5,7},{6,4},{7,5},{8,10},{9,11},{10,... | collective-permute-start | bytes 1769480 | tf_op jit(solution)/shard_map/gather_states/ppermute | solution.py:46
  76.3 12.6 %collective-permute-start.9 = (bf16[4,144,512]{2,1,0:T(8,128)(2,1)S(1)}, bf16[4,144,512]{2,1,0:T(8,128)(2,1)S(1)}, u32[]{:S(2)}, u32[]{:S(2)}) collective-permute-start(bf16[4,144,512]{2,1,0:T(8,128)(2,1)S(1)} %gather_states.3.refs_0_), channel_id=1, source_target_pairs={{0,1},{1,2},{2,3},{3,0},{4,5},{5,6},{6,7},{7,4},{8,9},{9,10},{10,1... | collective-permute-start | bytes 1769480 | tf_op jit(solution)/shard_map/gather_states/ppermute | solution.py:46
  79.1 17.5 %collective-permute-start.20 = (bf16[4,256,256]{2,1,0:T(8,128)(2,1)S(1)}, bf16[4,256,256]{2,1,0:T(8,128)(2,1)S(1)}, u32[]{:S(2)}, u32[]{:S(2)}) collective-permute-start(bf16[4,256,256]{2,1,0:T(8,128)(2,1)S(1)} %get-tuple-element.46), channel_id=1, source_target_pairs={{0,1},{1,2},{2,3},{3,0},{4,5},{5,6},{6,7},{7,4},{8,9},{9,10},{10,1... | collective-permute-start | bytes 1572872 | tf_op jit(solution)/shard_map/kv/ppermute | solution.py:46
  81.1 15.5 %collective-permute-start.21 = (bf16[4,256,256]{2,1,0:T(8,128)(2,1)S(1)}, bf16[4,256,256]{2,1,0:T(8,128)(2,1)S(1)}, u32[]{:S(2)}, u32[]{:S(2)}) collective-permute-start(bf16[4,256,256]{2,1,0:T(8,128)(2,1)S(1)} %get-tuple-element.47), channel_id=1, source_target_pairs={{0,3},{1,0},{2,1},{3,2},{4,7},{5,4},{6,5},{7,6},{8,11},{9,8},{10,9... | collective-permute-start | bytes 1572872 | tf_op jit(solution)/shard_map/kv/ppermute | solution.py:46
  81.2 18.3 %collective-permute-start.22 = (bf16[4,256,256]{2,1,0:T(8,128)(2,1)S(1)}, bf16[4,256,256]{2,1,0:T(8,128)(2,1)S(1)}, u32[]{:S(2)}, u32[]{:S(2)}) collective-permute-start(bf16[4,256,256]{2,1,0:T(8,128)(2,1)S(1)} %get-tuple-element.48), channel_id=1, source_target_pairs={{0,2},{1,3},{2,0},{3,1},{4,6},{5,7},{6,4},{7,5},{8,10},{9,11},{10,... | collective-permute-start | bytes 1572872 | tf_op jit(solution)/shard_map/kv/ppermute | solution.py:46
  128.4 16.4 %collective-permute-start.26 = (bf16[4,128,512]{2,1,0:T(8,128)(2,1)S(1)}, bf16[4,128,512]{2,1,0:T(8,128)(2,1)S(1)}, u32[]{:S(2)}, u32[]{:S(2)}) collective-permute-start(bf16[4,128,512]{2,1,0:T(8,128)(2,1)S(1)} %get-tuple-element.54), channel_id=1, source_target_pairs={{0,1},{1,2},{2,3},{3,0},{4,5},{5,6},{6,7},{7,4},{8,9},{9,10},{10,1... | collective-permute-start | bytes 1572872 | tf_op jit(solution)/shard_map/mix/ppermute | solution.py:46
  132.5 16.0 %collective-permute-start.27 = (bf16[4,128,512]{2,1,0:T(8,128)(2,1)S(1)}, bf16[4,128,512]{2,1,0:T(8,128)(2,1)S(1)}, u32[]{:S(2)}, u32[]{:S(2)}) collective-permute-start(bf16[4,128,512]{2,1,0:T(8,128)(2,1)S(1)} %get-tuple-element.55), channel_id=1, source_target_pairs={{0,3},{1,0},{2,1},{3,2},{4,7},{5,4},{6,5},{7,6},{8,11},{9,8},{10,9... | collective-permute-start | bytes 1572872 | tf_op jit(solution)/shard_map/mix/ppermute | solution.py:46
  132.5 16.0 %collective-permute-start.28 = (bf16[4,128,512]{2,1,0:T(8,128)(2,1)S(1)}, bf16[4,128,512]{2,1,0:T(8,128)(2,1)S(1)}, u32[]{:S(2)}, u32[]{:S(2)}) collective-permute-start(bf16[4,128,512]{2,1,0:T(8,128)(2,1)S(1)} %get-tuple-element.56), channel_id=1, source_target_pairs={{0,2},{1,3},{2,0},{3,1},{4,6},{5,7},{6,4},{7,5},{8,10},{9,11},{10,... | collective-permute-start | bytes 1572872 | tf_op jit(solution)/shard_map/mix/ppermute | solution.py:46
  (14 other events, 148.4 us)

commit v5 on v4

v5 whole, which is shorter than its diff:
```python
import functools

import jax
import jax.numpy as jnp
from jax import lax
from jax.experimental import pallas as pl
from jax.experimental.pallas import tpu as pltpu
from jax.sharding import Mesh, PartitionSpec as P

D = 8192
KV_HEADS = 8
HEAD_DIM = 128
MAXT = 4
STEPS = 2
SIDE = 4
F32 = jnp.float32
BF16 = jnp.bfloat16
TP = ("z", "xh", "pr")
EVERY = ("group",) + TP
FIRST, SECOND = 0, 1
HOPS = (0, 1, 3, 2)
GRANT = 16 * 1024 * 1024
ANY = pl.BlockSpec(memory_space=pl.ANY)
IN_HBM = pl.BlockSpec(memory_space=pltpu.HBM)
IN_VMEM = pl.BlockSpec(memory_space=pltpu.VMEM)
IN_SMEM = pl.BlockSpec(memory_space=pltpu.SMEM)


def shift(value, groups, order, by):
    pairs = []
    for group in range(groups):
        for z in range(SIDE):
            for x in range(SIDE):
                if group % 2 == order:
                    other = z * SIDE + (x + by) % SIDE
                else:
                    other = (z + by) % SIDE * SIDE + x
                base = group * SIDE * SIDE
                pairs.append((base + z * SIDE + x, base + other))
    return lax.ppermute(value, EVERY, pairs)


def in_hbm(value):
    return pltpu.with_memory_space_constraint(value, pltpu.HBM)


def in_vmem(value):
    return pltpu.with_memory_space_constraint(value, pltpu.VMEM)


def kernel_call(kernel, operands, specs, out, scratch=(), flops=0, moved=0, transcendentals=0):
    return pl.pallas_call(
        kernel,
        in_specs=specs,
        out_specs=jax.tree.map(lambda _: IN_VMEM, out),
        out_shape=out,
        scratch_shapes=list(scratch),
        compiler_params=pltpu.CompilerParams(vmem_limit_bytes=GRANT),
        cost_estimate=pl.CostEstimate(
            flops=flops, bytes_accessed=moved, transcendentals=transcendentals
        ),
    )(*operands)


def wrap(value):
    return lax.rem(value + SIDE, SIDE)


def position():
    z = lax.axis_index("z")
    x = lax.axis_index("xh") * 2 + lax.axis_index("pr")
    return z, x, lax.rem(lax.axis_index("group"), 2)


def rank_from_here(first_by, second_by):
    z, x, core = position()
    first = jnp.where(core == 0, x, z)
    second = jnp.where(core == 0, z, x)
    first, second = wrap(first + first_by), wrap(second + second_by)
    return jnp.where(core == 0, second * SIDE + first, first * SIDE + second)


def join_kernel(moves, *refs):
    copies = []
    sem = refs[-1]
    for at, (source, low, target, first, count) in enumerate(moves):
        copies.append(
            pltpu.make_async_copy(
                refs[source].at[pl.ds(low, count)], refs[target].at[pl.ds(first, count)], sem.at[at]
            )
        )
    for copy in copies:
        copy.start()
    for copy in copies:
        copy.wait()


def join(arrays, moves, shapes, after=()):
    offset = len(arrays) + len(after)
    moves = [(a, low, offset + b, first, count) for a, low, b, first, count in moves]
    moved = 4 * sum(a.size for a in arrays)
    return kernel_call(
        functools.partial(join_kernel, moves),
        [*arrays, *after],
        [ANY] * offset,
        [pltpu.VMEM(shape, BF16) for shape in shapes],
        [pltpu.SemaphoreType.DMA((len(moves),))],
        moved=moved,
    )


def load_kernel(count, *refs):
    outs, sems = refs[-2 * count : -count], refs[-count:]
    copies = [pltpu.make_async_copy(refs[i], outs[i], sems[i]) for i in range(count)]
    for copy in copies:
        copy.start()
    for copy in copies:
        copy.wait()


def load(*values, after=()):
    return kernel_call(
        functools.partial(load_kernel, len(values)),
        [*map(in_hbm, values), *after],
        [IN_HBM] * len(values) + [ANY] * len(after),
        [pltpu.VMEM(value.shape, value.dtype) for value in values],
        [pltpu.SemaphoreType.DMA(()) for _ in values],
        moved=4 * sum(value.size for value in values),
    )


def fetcher(weight_ref, buffer, sem, shifts):
    z, x, core = position()
    first = jnp.where(core == 0, x, z)

    def fetch(by, start):
        at = shifts.index(by)
        to_x = pltpu.make_async_copy(
            weight_ref.at[:, wrap(first + by)], buffer.at[at], sem.at[at]
        )
        to_z = pltpu.make_async_copy(weight_ref.at[wrap(first + by)], buffer.at[at], sem.at[at])
        if start:
            pl.when(core == 0)(to_x.start)
            pl.when(core != 0)(to_z.start)
        else:
            to_z.wait()

    return fetch, jnp.where(core == 0, z, x)


def head_copies(kv_weight_ref, kv_buffer, kv_sem):
    span = pl.ds(pl.multiple_of(lax.axis_index("group") * HEAD_DIM, HEAD_DIM), HEAD_DIM)
    return [
        pltpu.make_async_copy(kv_weight_ref.at[i, :, span], kv_buffer.at[i], kv_sem.at[i])
        for i in range(2)
    ]


def contract_far_kernel(weight_ref, kv_weight_ref, states_ref, gain_ref, vision_ref, *refs):
    low_ref, high_ref, carried_ref, sent_ref = refs[:4]
    buffer, sem, kv_buffer, kv_sem, sent_sem = refs[4:]
    features = low_ref.shape[1]
    fetch, second = fetcher(weight_ref, buffer, sem, (2,))
    kv_copies = head_copies(kv_weight_ref, kv_buffer, kv_sem)
    for copy in kv_copies:
        copy.start()
    fetch(2, True)
    vision_copy = pltpu.make_async_copy(vision_ref, sent_ref, sent_sem)
    vision_copy.start()
    steps, batch, width = states_ref.shape
    carried_ref[: steps * batch] = states_ref[...].reshape(steps * batch, width)
    carried_ref[steps * batch :] = jnp.broadcast_to(gain_ref[...].reshape(1, -1), (16, width))
    for copy in kv_copies:
        copy.wait()
    weight = jnp.concatenate([kv_buffer[0], kv_buffer[1]], axis=1)
    fetch(2, False)
    for by in range(SIDE):
        rows = buffer[0, wrap(second + by)]
        part = jnp.dot(rows, weight, preferred_element_type=F32).astype(BF16)
        (low_ref if by < 2 else high_ref)[by % 2] = part
    vision_copy.wait()


def contract_near_kernel(weight_ref, kv_weight_ref, bias_ref, _, *refs):
    outs, biased_ref, (buffer, sem, kv_buffer, kv_sem) = refs[:3], refs[3], refs[4:]
    shifts = (1, 3, 0)
    features = outs[0].shape[1]
    fetch, second = fetcher(weight_ref, buffer, sem, shifts)
    kv_copies = head_copies(kv_weight_ref, kv_buffer, kv_sem)
    for copy in kv_copies:
        copy.start()
    for by in shifts:
        fetch(by, True)
    for copy in kv_copies:
        copy.wait()
    weight = jnp.concatenate([kv_buffer[0], kv_buffer[1]], axis=1)
    bias = jnp.broadcast_to(bias_ref[...].reshape(1, -1), (16, weight.shape[0]))
    biased_ref[...] = jnp.dot(bias, weight, preferred_element_type=F32)
    for out, by in zip(outs, shifts):
        fetch(by, False)
        rows = buffer[shifts.index(by)].reshape(SIDE * features, -1)
        part = jnp.dot(rows, weight, preferred_element_type=F32).astype(BF16)
        for at in range(SIDE):
            out[wrap(at - second)] = part[at * features : (at + 1) * features]


def contract_scratch(count, features, width):
    return [
        pltpu.VMEM((count, SIDE, features, width), BF16),
        pltpu.SemaphoreType.DMA((count,)),
        pltpu.VMEM((2, width, HEAD_DIM), BF16),
        pltpu.SemaphoreType.DMA((2,)),
    ]


def contract(proj_weight, kv_weight, proj_bias, states, norm_gain, vision_rows):
    total, width = proj_weight.shape
    features = vision_rows.shape[3]
    weight = in_hbm(proj_weight.reshape(SIDE, SIDE, features, width))
    kv_weight = in_hbm(kv_weight)
    flops = total * width * HEAD_DIM
    rows = states.shape[0] * states.shape[1] + 16
    low, high, carried, sent = kernel_call(
        contract_far_kernel,
        [weight, kv_weight, states, norm_gain, in_hbm(vision_rows)],
        [IN_HBM, IN_HBM, IN_VMEM, IN_VMEM, IN_HBM],
        [pltpu.VMEM((2, features, 2 * HEAD_DIM), BF16)] * 2
        + [
            jax.ShapeDtypeStruct((rows, states.shape[2]), BF16),
            pltpu.VMEM(vision_rows.shape, BF16),
        ],
        contract_scratch(1, features, width) + [pltpu.SemaphoreType.DMA(())],
        flops=flops,
        moved=4 * 1024 * 1024,
    )
    one, three, own, biased = kernel_call(
        contract_near_kernel,
        [weight, kv_weight, proj_bias, low],
        [IN_HBM, IN_HBM, IN_VMEM, ANY],
        [pltpu.VMEM((SIDE, features, 2 * HEAD_DIM), BF16)] * 3
        + [jax.ShapeDtypeStruct((16, 2 * HEAD_DIM), F32)],
        contract_scratch(3, features, width),
        flops=3 * flops,
        moved=10 * 1024 * 1024,
    )
    return low, high, one, three, own, biased, carried, sent


def merge_kernel(one_ref, low_ref, three_ref, high_ref, up_ref, down_ref):
    half = low_ref.shape[0]
    for at in range(2 * half):
        if at < half:
            up_ref[at] = (one_ref[at].astype(F32) + low_ref[at].astype(F32)).astype(BF16)
            down_ref[at] = three_ref[at]
        else:
            up_ref[at] = one_ref[at]
            down_ref[at] = (three_ref[at].astype(F32) + high_ref[at - half].astype(F32)).astype(
                BF16
            )


def merge(one, low, three, high):
    return kernel_call(
        merge_kernel,
        [in_vmem(value) for value in (one, low, three, high)],
        [IN_VMEM] * 4,
        [pltpu.VMEM(one.shape, BF16)] * 2,
        flops=one.size,
        moved=8 * one.size,
    )


def kv_kernel(same_ref, other_ref, merged_ref, biased_ref, *outs):
    bias = biased_ref[:1]
    for first_by in range(SIDE):
        for second_by in range(SIDE):
            rank = rank_from_here(first_by, second_by)
            tiles = [ref[at, rank] for ref in (same_ref, other_ref) for at in range(SIDE)]
            rows = jnp.concatenate(tiles, axis=0)
            part = jnp.dot(rows, merged_ref[...], preferred_element_type=F32)
            outs[first_by][second_by] = (part + bias).astype(BF16)


def kv_partials(same, other, merged, biased):
    _, tiles, tile_rows, features = same.shape
    count = 2 * SIDE * tile_rows
    return kernel_call(
        kv_kernel,
        [in_vmem(value) for value in (same, other, merged, biased)],
        [IN_VMEM] * 4,
        [pltpu.VMEM((SIDE, count, 2 * HEAD_DIM), BF16) for _ in range(SIDE)],
        flops=4 * count * tiles * features * HEAD_DIM,
        moved=12 * 1024 * 1024,
    )


def sum_kernel(*refs, sources, count):
    sources, outs = refs[:sources], refs[-count:]
    for at in range(count):
        total = sources[0][at].astype(F32)
        for source in sources[1:]:
            total = total + source[at].astype(F32)
        outs[at][...] = total.astype(BF16)


def sum_blocks(sources, after=()):
    count, rows, width = sources[0].shape
    return kernel_call(
        functools.partial(sum_kernel, sources=len(sources), count=count),
        [*map(in_vmem, sources), *after],
        [IN_VMEM] * len(sources) + [ANY] * len(after),
        [pltpu.VMEM((rows, width), BF16) for _ in range(count)],
        flops=len(sources) * sources[0].size,
        moved=10 * sources[0].size,
    )


def query_kernel(full_ref, weight_ref, out_ref, held, held_sem, buffer, sem):
    ranks, _, width = full_ref.shape
    batch = out_ref.shape[0]
    pieces = sem.shape[0]
    deep = buffer.shape[0] // pieces
    states = pltpu.make_async_copy(full_ref, held, held_sem)
    states.start()
    copies = [
        pltpu.make_async_copy(
            weight_ref.at[pl.ds(i * deep, deep)], buffer.at[pl.ds(i * deep, deep)], sem.at[i]
        )
        for i in range(pieces)
    ]
    for copy in copies:
        copy.start()
    states.wait()
    total = jnp.zeros((batch, 1), F32)
    for rank in range(ranks):
        hidden = held[rank, :batch, :].astype(F32)
        total += jnp.sum(hidden * hidden, axis=1, keepdims=True)
    inverse = lax.rsqrt(total / D + 1e-05)
    accum = jnp.zeros(out_ref.shape, F32)
    for rank in range(ranks):
        hidden = held[rank, :batch, :].astype(F32)
        gain = held[rank, batch : batch + 16, :].astype(F32)[:1]
        normed = (hidden * inverse * gain).astype(BF16)
        if rank * width % deep == 0:
            copies[rank * width // deep].wait()
        span = slice(rank * width, (rank + 1) * width)
        accum += jnp.dot(normed, buffer[span, :], preferred_element_type=F32)
    out_ref[...] = accum.astype(BF16)


def queries(full, query_weight, batch):
    columns = query_weight.shape[1]
    return kernel_call(
        query_kernel,
        [full, in_hbm(query_weight)],
        [ANY, IN_HBM],
        pltpu.VMEM((batch, columns), BF16),
        [
            pltpu.VMEM(full.shape, BF16),
            pltpu.SemaphoreType.DMA(()),
            pltpu.VMEM(query_weight.shape, BF16),
            pltpu.SemaphoreType.DMA((2,)),
        ],
        flops=2 * batch * D * columns,
        moved=12 * 1024 * 1024,
    )


def attend_kernel(
    source_ref, count_ref, request_ref, query_ref, own_ref, other_ref, weight_ref, *outs
):
    batch, width = query_ref.shape
    columns = outs[0].shape[2]
    half_rows = own_ref.shape[0]
    rows = 2 * half_rows
    slots = source_ref.shape[1]
    group = lax.axis_index("group")
    pair = lax.axis_index("pr")

    head = lax.axis_index("z") * 2 + lax.axis_index("xh")
    column = lax.broadcasted_iota(jnp.int32, (1, rows), 1) // (rows // slots)
    tile = jnp.zeros((1, rows), jnp.int32)
    for spot in range(slots):
        parity, far = spot // (slots // 2), spot % (slots // 2)
        encoder = wrap(head // 2 - HOPS[far % SIDE]) * 2 + lax.rem(head + far // SIDE, 2)
        tile = jnp.where(column == spot, encoder * 2 + lax.rem(parity + pair, 2), tile)
    owner = jnp.full((1, rows), -1, jnp.int32)
    for place in range(slots):
        request = place // MAXT
        valid = place % MAXT < count_ref[group * (slots // MAXT) + request]
        label = jnp.where(valid, request, -1)
        owner = jnp.where(tile == source_ref[group, place], label, owner)
    per_step = request_ref.shape[1]
    here = lax.broadcasted_iota(jnp.int32, (per_step, per_step), 0)
    there = lax.broadcasted_iota(jnp.int32, (per_step, per_step), 1)
    asked = jnp.where(here == there, request_ref[...], 0)
    asked = jnp.sum(asked, axis=1, keepdims=True)
    allowed = jnp.concatenate([asked] * (batch // per_step), axis=0) == owner

    keys = jnp.concatenate([own_ref[:, :HEAD_DIM], other_ref[:, :HEAD_DIM]], axis=0)
    values = jnp.concatenate([own_ref[:, HEAD_DIM:], other_ref[:, HEAD_DIM:]], axis=0)
    contexts = []
    for head in range(width // HEAD_DIM):
        span = slice(head * HEAD_DIM, (head + 1) * HEAD_DIM)
        scores = lax.dot_general(
            query_ref[:, span], keys, (((1,), (1,)), ((), ())), preferred_element_type=F32
        ) * (1.0 / HEAD_DIM**0.5)
        scores = jnp.where(allowed, scores, -1e30)
        largest = jnp.max(scores, axis=1, keepdims=True)
        weights = jnp.where(allowed, jnp.exp(scores - largest), 0.0)
        total = jnp.sum(weights, axis=1, keepdims=True)
        summed = jnp.dot(weights.astype(BF16), values, preferred_element_type=F32)
        contexts.append((summed / total).astype(BF16))
    context = jnp.concatenate(contexts, axis=1)
    for first_by in range(SIDE):
        for second_by in range(SIDE):
            rank = rank_from_here(first_by, second_by)
            span = pl.ds(pl.multiple_of(rank * columns, columns), columns)
            branch = jnp.dot(context, weight_ref[:, span], preferred_element_type=F32)
            outs[first_by][second_by] = branch.astype(BF16)


def attend(tile_source, tile_count, row_request, query, own, other, out_weight):
    batch, width = query.shape
    ranks = SIDE * SIDE
    columns = out_weight.shape[1] // ranks
    return kernel_call(
        attend_kernel,
        [tile_source, tile_count, row_request]
        + [in_vmem(value) for value in (query, own, other, out_weight)],
        [IN_SMEM, IN_SMEM] + [IN_VMEM] * 5,
        [pltpu.VMEM((SIDE, batch, columns), BF16) for _ in range(SIDE)],
        flops=2 * batch * width * out_weight.shape[1],
        moved=12 * 1024 * 1024,
        transcendentals=batch * 4 * 512,
    )


def mix_kernel(gate_ref, local_ref, *refs):
    sources, out_ref = refs[:SIDE], refs[SIDE]
    steps, batch, width = local_ref.shape
    gate = jnp.tanh(jnp.full((1, width), gate_ref[0, 0], F32))
    for step in range(steps):
        span = slice(step * batch, (step + 1) * batch)
        total = sources[0][span].astype(F32)
        for source in sources[1:]:
            total = total + source[span].astype(F32)
        out_ref[step] = (local_ref[step].astype(F32) + gate * total).astype(BF16)


def mix(gate, local, sources):
    return kernel_call(
        mix_kernel,
        [gate.reshape(1, 1), local, *map(in_vmem, sources)],
        [IN_SMEM, IN_VMEM] + [IN_VMEM] * SIDE,
        jax.ShapeDtypeStruct(local.shape, BF16),
        flops=SIDE * local.size,
        moved=12 * local.size,
    )


def body(
    vision_rows,
    tile_count,
    tile_source,
    row_request,
    proj_weight,
    proj_bias,
    kv_weight,
    query_weight,
    out_weight,
    norm_gain,
    attn_gate,
    states,
):
    groups = lax.axis_size("group")
    ranks = lax.axis_size(TP)
    tile_rows, features = vision_rows.shape[2:]
    per_group = vision_rows.shape[1] // groups
    slots = groups * per_group
    batch = STEPS * states.shape[1]
    width = states.shape[2]

    def spread(blocks, order):
        return [blocks[0]] + [shift(blocks[by], groups, order, by) for by in HOPS[1:]]

    def around(block, by):
        return lax.ppermute(block, "group", [(g, (g + 2 * by) % groups) for g in range(groups)])

    with jax.named_scope("contract"):
        low, high, one, three, own, biased, carried, sent = contract(
            proj_weight, kv_weight, proj_bias, states, norm_gain, vision_rows
        )
        low, high = shift(low, groups, FIRST, 1), shift(high, groups, FIRST, 3)

    with jax.named_scope("gather_states"):
        full = lax.all_gather(carried, TP)

    with jax.named_scope("gather_rows"):
        after, before = around(sent, 1), around(sent, 3)
        near = [sent, after, before, around(after, 1)]

    with jax.named_scope("contract"):
        up, down = merge(one, low, three, high)
        up, down = shift(up, groups, FIRST, 1), shift(down, groups, FIRST, 3)
        merged = sum_blocks([own, up, down], after=[near[3]])

    with jax.named_scope("gather_rows"):
        (same,) = join(
            near,
            [(i, 0, 0, i, 1) for i in range(SIDE)],
            [(SIDE, *vision_rows.shape[1:])],
            [merged[1]],
        )
        other = lax.ppermute(same, "group", [(g, g ^ 1) for g in range(groups)])

    with jax.named_scope("contract"):
        merged = [part[None] for part in spread(merged, SECOND)]
        (merged,) = sum_blocks(merged, after=[other])

    with jax.named_scope("kv"):
        kv = kv_partials(same, other, merged, biased)
        kv = sum_blocks(spread(kv, FIRST))
        kv = [part[None] for part in spread(kv, SECOND)]
        (out_here,) = load(out_weight, after=[full])
        (kv,) = sum_blocks(kv, after=[out_here])
        halves = []
        for flip in range(2):
            pairs = [
                (g * ranks + t, t // 2 * ranks + 2 * g + (t + flip) % 2)
                for g in range(groups)
                for t in range(ranks)
            ]
            halves.append(lax.ppermute(kv, EVERY, pairs))

    with jax.named_scope("query"):
        query = queries(full, query_weight, batch)

    with jax.named_scope("attend"):
        branch = attend(tile_source, tile_count, row_request, query, *halves, out_here)

    with jax.named_scope("mix"):
        branch = sum_blocks(spread(branch, FIRST))
        return mix(attn_gate, states, spread(branch, SECOND))


def solution(mesh):
    groups = mesh.shape["group"]
    split = Mesh(mesh.devices.reshape(groups, SIDE, 2, 2), ("group",) + TP)
    in_specs = (
        P("group", None, None, TP),
        P(),
        P(),
        P("group", None),
        P(None, TP),
        P(TP),
        P(None, TP, None),
        P(None, TP),
        P(TP, None),
        P(TP),
        P(),
        P(None, "group", TP),
    )
    out_specs = P(None, "group", TP)
    return jax.shard_map(body, mesh=split, in_specs=in_specs, out_specs=out_specs, check_vma=False)
```

time: 161 us -> 148 us (0.919); the launches traced: 159 us -> 148 us
  starting transfers between devices: 49.5 us -> 35.9 us
  between operations: 0.85 us -> 14.3 us
  Pallas kernels: 29.4 us -> 23 us
  waiting for transfers between devices: 77.5 us -> 71.6 us
    ppermute x14 -> x6, waiting for transfers between devices: 34.9 us -> 21.6 us  [the longest x3 17.9 us: around(): lax.ppermute(block, 'group', [(g, (g + 2 * by) % groups) for g in range(g...]
    ppermute x14 -> x6, starting transfers between devices: 22.3 us -> 10.6 us  [the longest x2 8.24 us: body(): halves.append(lax.ppermute(kv, EVERY, pairs))]
    ppermute x18 -> x19, waiting for transfers between devices: 42.5 us -> 50 us  [shift(): return lax.ppermute(value, EVERY, pairs)]
    pallas_call x15 -> x14, Pallas kernels: 29.4 us -> 23 us  [kernel_call(): pl.pallas_call(kernel, in_specs=specs, out_specs=jax.tree.map(lambda _: I...]
    all_to_all x1 -> x0, starting transfers between devices: 5.61 us -> none  [body(): kv = lax.all_to_all(kv, ('group', 'pr'), 0, 0)]
    ppermute x18 -> x19, starting transfers between devices: 21.6 us -> 25.3 us  [shift(): return lax.ppermute(value, EVERY, pairs)]
    unnamed x10 -> x18, local copies, waits for them, and re-layouts: 0.02 us -> 3.29 us
  transfers between devices with their start and end apart: 33 -> 26, of which waited for: 22 -> 17; matrix products, arithmetic and copies ran while one was open for 1% -> 0% of each run, Pallas kernels for 11% -> 11%
where the time goes in v5:
time: 148 us
  waiting for transfers between devices  71.6 us (48%)
  starting transfers between devices  35.9 us (24%)
  Pallas kernels  23 us (16%)
  between operations  14.3 us (10%)
  local copies, waits for them, and re-layouts  3.29 us (2%)
    ppermute x19, waiting for transfers between devices, shift(): return lax.ppermute(value, EVERY, pairs)  50 us
    ppermute x19, starting transfers between devices, shift(): return lax.ppermute(value, EVERY, pairs)  25.3 us
    pallas_call x14, Pallas kernels, kernel_call(): pl.pallas_call(kernel, in_specs=specs, out_specs=jax.tree.map(lambda _: I...  23 us
    ppermute x3, waiting for transfers between devices, around(): lax.ppermute(block, 'group', [(g, (g + 2 * by) % groups) for g in range(g...  17.9 us
    ppermute x2, starting transfers between devices, body(): halves.append(lax.ppermute(kv, EVERY, pairs))  8.24 us
    ppermute x2, waiting for transfers between devices, body(): halves.append(lax.ppermute(kv, EVERY, pairs))  3.77 us
    unnamed x18, local copies, waits for them, and re-layouts  3.29 us
  transfers between devices with their start and end apart: 26, of which 17 were waited for; matrix products, arithmetic and copies ran while one was open for 0% of the time, Pallas kernels for 11%

profile of v5, /device:TPU:30, one launch (start us, length us, event | category | flops | bytes accessed | tf_op | source)
XLA Modules:
  0.0 148.0 jit_solution(595185480455338890)
XLA Ops:
  8.1 3.3 %contract.5 = (bf16[2,480,256]{2,1,0:T(8,128)(2,1)S(1)}, bf16[2,480,256]{2,1,0:T(8,128)(2,1)S(1)}, bf16[144,512]{1,0:T(8,128)(2,1)}, bf16[1,16,32,480]{3,2,1,0:T(8,128)(2,1)S(1)}) custom-call(bf16[4,4,480,512]{3,2,1,0:T(8,128)(2,1)} %bitcast.22, bf16[2,512,1024]{2,1,0:T(8,128)(2,1)} %kv_weight_ref.3, bf16[2,64,512]{2,1,0:T(8,128)(2,1)S(1)} %copy-done.2, ...), custom_call_target="tpu_custom_call" | custom-call | flops 503316480 | bytes 4194304 | tf_op jit(solution)/shard_map/contract/pallas_call | solution.py:52
  13.7 5.4 %contract.6 = (bf16[4,480,256]{2,1,0:T(8,128)(2,1)S(1)}, bf16[4,480,256]{2,1,0:T(8,128)(2,1)S(1)}, bf16[4,480,256]{2,1,0:T(8,128)(2,1)S(1)}, f32[16,256]{1,0:T(8,128)S(1)}) custom-call(bf16[4,4,480,512]{3,2,1,0:T(8,128)(2,1)} %bitcast.23, bf16[2,512,1024]{2,1,0:T(8,128)(2,1)} %kv_weight_ref.3, bf16[512]{0:T(512)(128)(2,1)S(1)} %copy-done.6, ...), custom_call_target="tpu_custom_call" | custom-call | flops 1509949440 | bytes 10485760 | tf_op jit(solution)/shard_map/contract/pallas_call | solution.py:52
  24.4 3.3 %collective-permute-done.refs_1_ = bf16[1,16,32,480]{3,2,1,0:T(8,128)(2,1)S(1)} collective-permute-done((bf16[1,16,32,480]{3,2,1,0:T(8,128)(2,1)S(1)}, bf16[1,16,32,480]{3,2,1,0:T(8,128)(2,1)S(1)}, u32[]{:S(2)}, u32[]{:S(2)}) %collective-permute-start) | collective-permute-done | bytes 491552 | tf_op jit(solution)/shard_map/gather_rows/ppermute | solution.py:488
  29.7 12.7 %collective-permute-done.2.refs_3_ = bf16[1,16,32,480]{3,2,1,0:T(8,128)(2,1)S(1)} collective-permute-done((bf16[1,16,32,480]{3,2,1,0:T(8,128)(2,1)S(1)}, bf16[1,16,32,480]{3,2,1,0:T(8,128)(2,1)S(1)}, u32[]{:S(2)}, u32[]{:S(2)}) %collective-permute-start.2) | collective-permute-done | bytes 491552 | tf_op jit(solution)/shard_map/gather_rows/ppermute | solution.py:488
  42.7 1.9 %collective-permute-done.1.refs_2_ = bf16[1,16,32,480]{3,2,1,0:T(8,128)(2,1)S(1)} collective-permute-done((bf16[1,16,32,480]{3,2,1,0:T(8,128)(2,1)S(1)}, bf16[1,16,32,480]{3,2,1,0:T(8,128)(2,1)S(1)}, u32[]{:S(2)}, u32[]{:S(2)}) %collective-permute-start.1) | collective-permute-done | bytes 491552 | tf_op jit(solution)/shard_map/gather_rows/ppermute | solution.py:488
  45.0 3.2 %collective-permute-start.9 = (bf16[480,256]{1,0:T(8,128)(2,1)S(1)}, bf16[480,256]{1,0:T(8,128)(2,1)S(1)}, u32[]{:S(2)}, u32[]{:S(2)}) collective-permute-start(bf16[480,256]{1,0:T(8,128)(2,1)S(1)} %get-tuple-element.46), channel_id=1, source_target_pairs={{0,12},{1,13},{2,14},{3,15},{4,0},{5,1},{6,2},{7,3},{8,4},{9,5},{1... | collective-permute-start | bytes 737288 | tf_op jit(solution)/shard_map/contract/ppermute | solution.py:40
  48.2 10.1 %collective-permute-done.8 = bf16[480,256]{1,0:T(8,128)(2,1)S(1)} collective-permute-done((bf16[480,256]{1,0:T(8,128)(2,1)S(1)}, bf16[480,256]{1,0:T(8,128)(2,1)S(1)}, u32[]{:S(2)}, u32[]{:S(2)}) %collective-permute-start.8) | collective-permute-done | bytes 245792 | tf_op jit(solution)/shard_map/contract/ppermute | solution.py:40
  58.3 4.4 %collective-permute-done.10 = bf16[480,256]{1,0:T(8,128)(2,1)S(1)} collective-permute-done((bf16[480,256]{1,0:T(8,128)(2,1)S(1)}, bf16[480,256]{1,0:T(8,128)(2,1)S(1)}, u32[]{:S(2)}, u32[]{:S(2)}) %collective-permute-start.10) | collective-permute-done | bytes 245792 | tf_op jit(solution)/shard_map/contract/ppermute | solution.py:40
  67.6 5.7 %collective-permute-done.11.refs_1_ = bf16[4,256,256]{2,1,0:T(8,128)(2,1)S(1)} collective-permute-done((bf16[4,256,256]{2,1,0:T(8,128)(2,1)S(1)}, bf16[4,256,256]{2,1,0:T(8,128)(2,1)S(1)}, u32[]{:S(2)}, u32[]{:S(2)}) %collective-permute-start.11) | collective-permute-done | bytes 524320 | tf_op jit(solution)/shard_map/kv/ppermute | solution.py:40
  74.8 5.7 %collective-permute-done.13.refs_3_ = bf16[4,256,256]{2,1,0:T(8,128)(2,1)S(1)} collective-permute-done((bf16[4,256,256]{2,1,0:T(8,128)(2,1)S(1)}, bf16[4,256,256]{2,1,0:T(8,128)(2,1)S(1)}, u32[]{:S(2)}, u32[]{:S(2)}) %collective-permute-start.13) | collective-permute-done | bytes 524320 | tf_op jit(solution)/shard_map/kv/ppermute | solution.py:40
  81.1 2.0 %collective-permute-start.14 = (bf16[256,256]{1,0:T(8,128)(2,1)S(1)}, bf16[256,256]{1,0:T(8,128)(2,1)S(1)}, u32[]{:S(2)}, u32[]{:S(2)}) collective-permute-start(bf16[256,256]{1,0:T(8,128)(2,1)S(1)} %get-tuple-element.54), channel_id=1, source_target_pairs={{0,4},{1,5},{2,6},{3,7},{4,8},{5,9},{6,10},{7,11},{8,12},{9,13},{1... | collective-permute-start | bytes 393224 | tf_op jit(solution)/shard_map/kv/ppermute | solution.py:40
  86.1 3.4 %kv.6.refs_4_.weight_ref = bf16[512,8192]{1,0:T(8,128)(2,1)S(1)} custom-call(bf16[512,8192]{1,0:T(8,128)(2,1)} %refs_0_.1, bf16[16,144,512]{2,1,0:T(8,128)(2,1)S(1)} %bitcast.12), custom_call_target="tpu_custom_call" | custom-call | bytes 16777216 | tf_op jit(solution)/shard_map/kv/pallas_call | solution.py:52
  89.6 2.3 %collective-permute-start.17 = (bf16[256,256]{1,0:T(8,128)(2,1)S(1)}, bf16[256,256]{1,0:T(8,128)(2,1)S(1)}, u32[]{:S(2)}, u32[]{:S(2)}) collective-permute-start(bf16[256,256]{1,0:T(8,128)(2,1)S(1)} %kv.7), channel_id=1, source_target_pairs={{0,0},{1,1},{2,16},{3,17},{4,32},{5,33},{6,48},{7,49},{8,64},{9,65... | collective-permute-start | bytes 393224 | tf_op jit(solution)/shard_map/kv/ppermute | solution.py:534
  91.9 5.9 %collective-permute-start.18 = (bf16[256,256]{1,0:T(8,128)(2,1)S(1)}, bf16[256,256]{1,0:T(8,128)(2,1)S(1)}, u32[]{:S(2)}, u32[]{:S(2)}) collective-permute-start(bf16[256,256]{1,0:T(8,128)(2,1)S(1)} %kv.7), channel_id=1, source_target_pairs={{0,1},{1,0},{2,17},{3,16},{4,33},{5,32},{6,49},{7,48},{8,65},{9,64... | collective-permute-start | bytes 393224 | tf_op jit(solution)/shard_map/kv/ppermute | solution.py:534
  97.9 4.4 %query.1.query_ref = bf16[128,512]{1,0:T(8,128)(2,1)S(1)} custom-call(bf16[16,144,512]{2,1,0:T(8,128)(2,1)S(1)} %bitcast.13, bf16[8192,512]{1,0:T(8,128)(2,1)} %weight_ref.1), custom_call_target="tpu_custom_call" | custom-call | flops 1073741824 | bytes 12582912 | tf_op jit(solution)/shard_map/query/pallas_call | solution.py:52
  103.4 2.7 %collective-permute-done.18.other_ref = bf16[256,256]{1,0:T(8,128)(2,1)S(1)} collective-permute-done((bf16[256,256]{1,0:T(8,128)(2,1)S(1)}, bf16[256,256]{1,0:T(8,128)(2,1)S(1)}, u32[]{:S(2)}, u32[]{:S(2)}) %collective-permute-start.18) | collective-permute-done | bytes 131104 | tf_op jit(solution)/shard_map/kv/ppermute | solution.py:534
  106.0 3.0 %attend.1 = (bf16[4,128,512]{2,1,0:T(8,128)(2,1)S(1)}, bf16[4,128,512]{2,1,0:T(8,128)(2,1)S(1)}, bf16[4,128,512]{2,1,0:T(8,128)(2,1)S(1)}, bf16[4,128,512]{2,1,0:T(8,128)(2,1)S(1)}) custom-call(s32[8,16]{1,0:T(8,128)S(1)} %copy-done.4, s32[32]{0:T(128)S(1)} %copy-done.7, s32[1,64]{1,0:T(1,128)S(1)} %copy-done.8, bf16[128,512]{1,0:T(8,128)(2,1)S(1)} %query.1.query_ref, ...), custom_call_target="tpu_custom_call" | custom-call | flops 1073741824 | bytes 12582912 | tf_op jit(solution)/shard_map/attend/pallas_call | solution.py:52
  109.1 5.0 %collective-permute-start.19 = (bf16[4,128,512]{2,1,0:T(8,128)(2,1)S(1)}, bf16[4,128,512]{2,1,0:T(8,128)(2,1)S(1)}, u32[]{:S(2)}, u32[]{:S(2)}) collective-permute-start(bf16[4,128,512]{2,1,0:T(8,128)(2,1)S(1)} %get-tuple-element.58), channel_id=1, source_target_pairs={{0,1},{1,2},{2,3},{3,0},{4,5},{5,6},{6,7},{7,4},{8,9},{9,10},{10,1... | collective-permute-start | bytes 1572872 | tf_op jit(solution)/shard_map/mix/ppermute | solution.py:40
  114.0 2.3 %collective-permute-start.21 = (bf16[4,128,512]{2,1,0:T(8,128)(2,1)S(1)}, bf16[4,128,512]{2,1,0:T(8,128)(2,1)S(1)}, u32[]{:S(2)}, u32[]{:S(2)}) collective-permute-start(bf16[4,128,512]{2,1,0:T(8,128)(2,1)S(1)} %get-tuple-element.60), channel_id=1, source_target_pairs={{0,2},{1,3},{2,0},{3,1},{4,6},{5,7},{6,4},{7,5},{8,10},{9,11},{10,... | collective-permute-start | bytes 1572872 | tf_op jit(solution)/shard_map/mix/ppermute | solution.py:40
  116.3 10.1 %collective-permute-done.19.refs_1_ = bf16[4,128,512]{2,1,0:T(8,128)(2,1)S(1)} collective-permute-done((bf16[4,128,512]{2,1,0:T(8,128)(2,1)S(1)}, bf16[4,128,512]{2,1,0:T(8,128)(2,1)S(1)}, u32[]{:S(2)}, u32[]{:S(2)}) %collective-permute-start.19) | collective-permute-done | bytes 524320 | tf_op jit(solution)/shard_map/mix/ppermute | solution.py:40
  126.4 4.0 %collective-permute-done.20.refs_2_ = bf16[4,128,512]{2,1,0:T(8,128)(2,1)S(1)} collective-permute-done((bf16[4,128,512]{2,1,0:T(8,128)(2,1)S(1)}, bf16[4,128,512]{2,1,0:T(8,128)(2,1)S(1)}, u32[]{:S(2)}, u32[]{:S(2)}) %collective-permute-start.20) | collective-permute-done | bytes 524320 | tf_op jit(solution)/shard_map/mix/ppermute | solution.py:40
  130.8 3.2 %collective-permute-start.23 = (bf16[128,512]{1,0:T(8,128)(2,1)S(1)}, bf16[128,512]{1,0:T(8,128)(2,1)S(1)}, u32[]{:S(2)}, u32[]{:S(2)}) collective-permute-start(bf16[128,512]{1,0:T(8,128)(2,1)S(1)} %get-tuple-element.63), channel_id=1, source_target_pairs={{0,12},{1,13},{2,14},{3,15},{4,0},{5,1},{6,2},{7,3},{8,4},{9,5},{1... | collective-permute-start | bytes 393224 | tf_op jit(solution)/shard_map/mix/ppermute | solution.py:40
  134.6 2.3 %collective-permute-done.22.refs_1_ = bf16[128,512]{1,0:T(8,128)(2,1)S(1)} collective-permute-done((bf16[128,512]{1,0:T(8,128)(2,1)S(1)}, bf16[128,512]{1,0:T(8,128)(2,1)S(1)}, u32[]{:S(2)}, u32[]{:S(2)}) %collective-permute-start.22) | collective-permute-done | bytes 131104 | tf_op jit(solution)/shard_map/mix/ppermute | solution.py:40
  137.9 2.5 %collective-permute-done.24.refs_3_ = bf16[128,512]{1,0:T(8,128)(2,1)S(1)} collective-permute-done((bf16[128,512]{1,0:T(8,128)(2,1)S(1)}, bf16[128,512]{1,0:T(8,128)(2,1)S(1)}, u32[]{:S(2)}, u32[]{:S(2)}) %collective-permute-start.24) | collective-permute-done | bytes 131104 | tf_op jit(solution)/shard_map/mix/ppermute | solution.py:40
  (61 shorter events, 25.1 us)
Async XLA Ops:
  6.5 77.9 %all-gather.3.cloned.1.call-start = ((), (), s32[]{:S(2)}) async-start(), calls=%async_computation | async-start | bytes 2506752 | tf_op jit(solution)/shard_map/gather_states/all_gather | solution.py:497
  11.4 8.9 %collective-permute-start.3 = (bf16[2,480,256]{2,1,0:T(8,128)(2,1)S(1)}, bf16[2,480,256]{2,1,0:T(8,128)(2,1)S(1)}, u32[]{:S(2)}, u32[]{:S(2)}) collective-permute-start(bf16[2,480,256]{2,1,0:T(8,128)(2,1)S(1)} %get-tuple-element.37._), channel_id=1, source_target_pairs={{0,1},{1,2},{2,3},{3,0},{4,5},{5,6},{6,7},{7,4},{8,9},{9,10},{10,1... | collective-permute-start | bytes 1474568 | tf_op jit(solution)/shard_map/contract/ppermute | solution.py:40
  12.0 10.0 %collective-permute-start.4 = (bf16[2,480,256]{2,1,0:T(8,128)(2,1)S(1)}, bf16[2,480,256]{2,1,0:T(8,128)(2,1)S(1)}, u32[]{:S(2)}, u32[]{:S(2)}) collective-permute-start(bf16[2,480,256]{2,1,0:T(8,128)(2,1)S(1)} %get-tuple-element.41), channel_id=1, source_target_pairs={{0,3},{1,0},{2,1},{3,2},{4,7},{5,4},{6,5},{7,6},{8,11},{9,8},{10,9... | collective-permute-start | bytes 1474568 | tf_op jit(solution)/shard_map/contract/ppermute | solution.py:40
  13.5 14.2 %collective-permute-start = (bf16[1,16,32,480]{3,2,1,0:T(8,128)(2,1)S(1)}, bf16[1,16,32,480]{3,2,1,0:T(8,128)(2,1)S(1)}, u32[]{:S(2)}, u32[]{:S(2)}) collective-permute-start(bf16[1,16,32,480]{3,2,1,0:T(8,128)(2,1)S(1)} %get-tuple-element.36.refs_0_), channel_id=1, source_target_pairs={{0,32},{16,48},{32,64},{48,80},{64,96},{80,112},{96,0},{112,16},{1... | collective-permute-start | bytes 1474568 | tf_op jit(solution)/shard_map/gather_rows/ppermute | solution.py:488
  22.3 20.1 %collective-permute-start.5 = (bf16[4,480,256]{2,1,0:T(8,128)(2,1)S(1)}, bf16[4,480,256]{2,1,0:T(8,128)(2,1)S(1)}, u32[]{:S(2)}, u32[]{:S(2)}) collective-permute-start(bf16[4,480,256]{2,1,0:T(8,128)(2,1)S(1)} %get-tuple-element.42), channel_id=1, source_target_pairs={{0,1},{1,2},{2,3},{3,0},{4,5},{5,6},{6,7},{7,4},{8,9},{9,10},{10,1... | collective-permute-start | bytes 2949128 | tf_op jit(solution)/shard_map/contract/ppermute | solution.py:40
  22.6 19.8 %collective-permute-start.6 = (bf16[4,480,256]{2,1,0:T(8,128)(2,1)S(1)}, bf16[4,480,256]{2,1,0:T(8,128)(2,1)S(1)}, u32[]{:S(2)}, u32[]{:S(2)}) collective-permute-start(bf16[4,480,256]{2,1,0:T(8,128)(2,1)S(1)} %get-tuple-element.43), channel_id=1, source_target_pairs={{0,3},{1,0},{2,1},{3,2},{4,7},{5,4},{6,5},{7,6},{8,11},{9,8},{10,9... | collective-permute-start | bytes 2949128 | tf_op jit(solution)/shard_map/contract/ppermute | solution.py:40
  27.7 14.7 %collective-permute-start.2 = (bf16[1,16,32,480]{3,2,1,0:T(8,128)(2,1)S(1)}, bf16[1,16,32,480]{3,2,1,0:T(8,128)(2,1)S(1)}, u32[]{:S(2)}, u32[]{:S(2)}) collective-permute-start(bf16[1,16,32,480]{3,2,1,0:T(8,128)(2,1)S(1)} %collective-permute-done.refs_1_), channel_id=1, source_target_pairs={{0,32},{16,48},{32,64},{48,80},{64,96},{80,112},{96,0},{112,16},{1... | collective-permute-start | bytes 1474568 | tf_op jit(solution)/shard_map/gather_rows/ppermute | solution.py:488
  29.0 15.6 %collective-permute-start.1 = (bf16[1,16,32,480]{3,2,1,0:T(8,128)(2,1)S(1)}, bf16[1,16,32,480]{3,2,1,0:T(8,128)(2,1)S(1)}, u32[]{:S(2)}, u32[]{:S(2)}) collective-permute-start(bf16[1,16,32,480]{3,2,1,0:T(8,128)(2,1)S(1)} %get-tuple-element.36.refs_0_), channel_id=1, source_target_pairs={{0,96},{16,112},{32,0},{48,16},{64,32},{80,48},{96,64},{112,80},{1... | collective-permute-start | bytes 1474568 | tf_op jit(solution)/shard_map/gather_rows/ppermute | solution.py:488
  44.8 17.9 %collective-permute-start.7 = (bf16[4,16,32,480]{3,2,1,0:T(8,128)(2,1)S(1)}, bf16[4,16,32,480]{3,2,1,0:T(8,128)(2,1)S(1)}, u32[]{:S(2)}, u32[]{:S(2)}) collective-permute-start(bf16[4,16,32,480]{3,2,1,0:T(8,128)(2,1)S(1)} %gather_rows.1.same_ref), channel_id=1, source_target_pairs={{0,16},{16,0},{32,48},{48,32},{64,80},{80,64},{96,112},{112,96},{1... | collective-permute-start | bytes 5898248 | tf_op jit(solution)/shard_map/gather_rows/ppermute | solution.py:515
  44.9 13.4 %collective-permute-start.8 = (bf16[480,256]{1,0:T(8,128)(2,1)S(1)}, bf16[480,256]{1,0:T(8,128)(2,1)S(1)}, u32[]{:S(2)}, u32[]{:S(2)}) collective-permute-start(bf16[480,256]{1,0:T(8,128)(2,1)S(1)} %get-tuple-element.44.refs_4_), channel_id=1, source_target_pairs={{0,4},{1,5},{2,6},{3,7},{4,8},{5,9},{6,10},{7,11},{8,12},{9,13},{1... | collective-permute-start | bytes 737288 | tf_op jit(solution)/shard_map/contract/ppermute | solution.py:40
  45.0 13.3 %collective-permute-start.9 = (bf16[480,256]{1,0:T(8,128)(2,1)S(1)}, bf16[480,256]{1,0:T(8,128)(2,1)S(1)}, u32[]{:S(2)}, u32[]{:S(2)}) collective-permute-start(bf16[480,256]{1,0:T(8,128)(2,1)S(1)} %get-tuple-element.46), channel_id=1, source_target_pairs={{0,12},{1,13},{2,14},{3,15},{4,0},{5,1},{6,2},{7,3},{8,4},{9,5},{1... | collective-permute-start | bytes 737288 | tf_op jit(solution)/shard_map/contract/ppermute | solution.py:40
  48.2 14.5 %collective-permute-start.10 = (bf16[480,256]{1,0:T(8,128)(2,1)S(1)}, bf16[480,256]{1,0:T(8,128)(2,1)S(1)}, u32[]{:S(2)}, u32[]{:S(2)}) collective-permute-start(bf16[480,256]{1,0:T(8,128)(2,1)S(1)} %get-tuple-element.47), channel_id=1, source_target_pairs={{0,8},{1,9},{2,10},{3,11},{4,12},{5,13},{6,14},{7,15},{8,0},{9,1},... | collective-permute-start | bytes 737288 | tf_op jit(solution)/shard_map/contract/ppermute | solution.py:40
  64.1 9.2 %collective-permute-start.11 = (bf16[4,256,256]{2,1,0:T(8,128)(2,1)S(1)}, bf16[4,256,256]{2,1,0:T(8,128)(2,1)S(1)}, u32[]{:S(2)}, u32[]{:S(2)}) collective-permute-start(bf16[4,256,256]{2,1,0:T(8,128)(2,1)S(1)} %get-tuple-element.50), channel_id=1, source_target_pairs={{0,1},{1,2},{2,3},{3,0},{4,5},{5,6},{6,7},{7,4},{8,9},{9,10},{10,1... | collective-permute-start | bytes 1572872 | tf_op jit(solution)/shard_map/kv/ppermute | solution.py:40
  64.4 10.4 %collective-permute-start.12 = (bf16[4,256,256]{2,1,0:T(8,128)(2,1)S(1)}, bf16[4,256,256]{2,1,0:T(8,128)(2,1)S(1)}, u32[]{:S(2)}, u32[]{:S(2)}) collective-permute-start(bf16[4,256,256]{2,1,0:T(8,128)(2,1)S(1)} %get-tuple-element.51), channel_id=1, source_target_pairs={{0,3},{1,0},{2,1},{3,2},{4,7},{5,4},{6,5},{7,6},{8,11},{9,8},{10,9... | collective-permute-start | bytes 1572872 | tf_op jit(solution)/shard_map/kv/ppermute | solution.py:40
  66.2 14.2 %collective-permute-start.13 = (bf16[4,256,256]{2,1,0:T(8,128)(2,1)S(1)}, bf16[4,256,256]{2,1,0:T(8,128)(2,1)S(1)}, u32[]{:S(2)}, u32[]{:S(2)}) collective-permute-start(bf16[4,256,256]{2,1,0:T(8,128)(2,1)S(1)} %get-tuple-element.52), channel_id=1, source_target_pairs={{0,2},{1,3},{2,0},{3,1},{4,6},{5,7},{6,4},{7,5},{8,10},{9,11},{10,... | collective-permute-start | bytes 1572872 | tf_op jit(solution)/shard_map/kv/ppermute | solution.py:40
  80.7 8.8 %collective-permute-start.16 = (bf16[256,256]{1,0:T(8,128)(2,1)S(1)}, bf16[256,256]{1,0:T(8,128)(2,1)S(1)}, u32[]{:S(2)}, u32[]{:S(2)}) collective-permute-start(bf16[256,256]{1,0:T(8,128)(2,1)S(1)} %get-tuple-element.56), channel_id=1, source_target_pairs={{0,8},{1,9},{2,10},{3,11},{4,12},{5,13},{6,14},{7,15},{8,0},{9,1},... | collective-permute-start | bytes 393224 | tf_op jit(solution)/shard_map/kv/ppermute | solution.py:40
  81.1 8.4 %collective-permute-start.14 = (bf16[256,256]{1,0:T(8,128)(2,1)S(1)}, bf16[256,256]{1,0:T(8,128)(2,1)S(1)}, u32[]{:S(2)}, u32[]{:S(2)}) collective-permute-start(bf16[256,256]{1,0:T(8,128)(2,1)S(1)} %get-tuple-element.54), channel_id=1, source_target_pairs={{0,4},{1,5},{2,6},{3,7},{4,8},{5,9},{6,10},{7,11},{8,12},{9,13},{1... | collective-permute-start | bytes 393224 | tf_op jit(solution)/shard_map/kv/ppermute | solution.py:40
  89.6 13.7 %collective-permute-start.17 = (bf16[256,256]{1,0:T(8,128)(2,1)S(1)}, bf16[256,256]{1,0:T(8,128)(2,1)S(1)}, u32[]{:S(2)}, u32[]{:S(2)}) collective-permute-start(bf16[256,256]{1,0:T(8,128)(2,1)S(1)} %kv.7), channel_id=1, source_target_pairs={{0,0},{1,1},{2,16},{3,17},{4,32},{5,33},{6,48},{7,49},{8,64},{9,65... | collective-permute-start | bytes 393224 | tf_op jit(solution)/shard_map/kv/ppermute | solution.py:534
  91.9 14.1 %collective-permute-start.18 = (bf16[256,256]{1,0:T(8,128)(2,1)S(1)}, bf16[256,256]{1,0:T(8,128)(2,1)S(1)}, u32[]{:S(2)}, u32[]{:S(2)}) collective-permute-start(bf16[256,256]{1,0:T(8,128)(2,1)S(1)} %kv.7), channel_id=1, source_target_pairs={{0,1},{1,0},{2,17},{3,16},{4,33},{5,32},{6,49},{7,48},{8,65},{9,64... | collective-permute-start | bytes 393224 | tf_op jit(solution)/shard_map/kv/ppermute | solution.py:534
  109.1 17.3 %collective-permute-start.19 = (bf16[4,128,512]{2,1,0:T(8,128)(2,1)S(1)}, bf16[4,128,512]{2,1,0:T(8,128)(2,1)S(1)}, u32[]{:S(2)}, u32[]{:S(2)}) collective-permute-start(bf16[4,128,512]{2,1,0:T(8,128)(2,1)S(1)} %get-tuple-element.58), channel_id=1, source_target_pairs={{0,1},{1,2},{2,3},{3,0},{4,5},{5,6},{6,7},{7,4},{8,9},{9,10},{10,1... | collective-permute-start | bytes 1572872 | tf_op jit(solution)/shard_map/mix/ppermute | solution.py:40
  114.0 16.3 %collective-permute-start.20 = (bf16[4,128,512]{2,1,0:T(8,128)(2,1)S(1)}, bf16[4,128,512]{2,1,0:T(8,128)(2,1)S(1)}, u32[]{:S(2)}, u32[]{:S(2)}) collective-permute-start(bf16[4,128,512]{2,1,0:T(8,128)(2,1)S(1)} %get-tuple-element.59), channel_id=1, source_target_pairs={{0,3},{1,0},{2,1},{3,2},{4,7},{5,4},{6,5},{7,6},{8,11},{9,8},{10,9... | collective-permute-start | bytes 1572872 | tf_op jit(solution)/shard_map/mix/ppermute | solution.py:40
  114.0 16.3 %collective-permute-start.21 = (bf16[4,128,512]{2,1,0:T(8,128)(2,1)S(1)}, bf16[4,128,512]{2,1,0:T(8,128)(2,1)S(1)}, u32[]{:S(2)}, u32[]{:S(2)}) collective-permute-start(bf16[4,128,512]{2,1,0:T(8,128)(2,1)S(1)} %get-tuple-element.60), channel_id=1, source_target_pairs={{0,2},{1,3},{2,0},{3,1},{4,6},{5,7},{6,4},{7,5},{8,10},{9,11},{10,... | collective-permute-start | bytes 1572872 | tf_op jit(solution)/shard_map/mix/ppermute | solution.py:40
  130.8 7.1 %collective-permute-start.23 = (bf16[128,512]{1,0:T(8,128)(2,1)S(1)}, bf16[128,512]{1,0:T(8,128)(2,1)S(1)}, u32[]{:S(2)}, u32[]{:S(2)}) collective-permute-start(bf16[128,512]{1,0:T(8,128)(2,1)S(1)} %get-tuple-element.63), channel_id=1, source_target_pairs={{0,12},{1,13},{2,14},{3,15},{4,0},{5,1},{6,2},{7,3},{8,4},{9,5},{1... | collective-permute-start | bytes 393224 | tf_op jit(solution)/shard_map/mix/ppermute | solution.py:40
  134.0 6.5 %collective-permute-start.24 = (bf16[128,512]{1,0:T(8,128)(2,1)S(1)}, bf16[128,512]{1,0:T(8,128)(2,1)S(1)}, u32[]{:S(2)}, u32[]{:S(2)}) collective-permute-start(bf16[128,512]{1,0:T(8,128)(2,1)S(1)} %get-tuple-element.64), channel_id=1, source_target_pairs={{0,8},{1,9},{2,10},{3,11},{4,12},{5,13},{6,14},{7,15},{8,0},{9,1},... | collective-permute-start | bytes 393224 | tf_op jit(solution)/shard_map/mix/ppermute | solution.py:40
  (11 other events, 119.3 us)
Sparse Core Ops, SparseCore 0:
  11.5 50.6 all-gather.2

commit v6 on v5

--- a/solution.py
+++ b/solution.py
@@ -158,18 +158,25 @@
 
 def contract_far_kernel(weight_ref, kv_weight_ref, states_ref, gain_ref, vision_ref, *refs):
     low_ref, high_ref, carried_ref, sent_ref = refs[:4]
-    buffer, sem, kv_buffer, kv_sem, sent_sem = refs[4:]
+    buffer, sem, kv_buffer, kv_sem, gain_buffer, sent_sem = refs[4:]
     features = low_ref.shape[1]
     fetch, second = fetcher(weight_ref, buffer, sem, (2,))
     kv_copies = head_copies(kv_weight_ref, kv_buffer, kv_sem)
     for copy in kv_copies:
         copy.start()
     fetch(2, True)
-    vision_copy = pltpu.make_async_copy(vision_ref, sent_ref, sent_sem)
-    vision_copy.start()
     steps, batch, width = states_ref.shape
-    carried_ref[: steps * batch] = states_ref[...].reshape(steps * batch, width)
-    carried_ref[steps * batch :] = jnp.broadcast_to(gain_ref[...].reshape(1, -1), (16, width))
+    others = [
+        pltpu.make_async_copy(vision_ref, sent_ref, sent_sem.at[0]),
+        pltpu.make_async_copy(gain_ref, gain_buffer, sent_sem.at[1]),
+    ] + [
+        pltpu.make_async_copy(
+            states_ref.at[i], carried_ref.at[pl.ds(i * batch, batch)], sent_sem.at[2 + i]
+        )
+        for i in range(steps)
+    ]
+    for copy in others:
+        copy.start()
     for copy in kv_copies:
         copy.wait()
     weight = jnp.concatenate([kv_buffer[0], kv_buffer[1]], axis=1)
@@ -178,7 +185,9 @@
         rows = buffer[0, wrap(second + by)]
         part = jnp.dot(rows, weight, preferred_element_type=F32).astype(BF16)
         (low_ref if by < 2 else high_ref)[by % 2] = part
-    vision_copy.wait()
+    for copy in others:
+        copy.wait()
+    carried_ref[steps * batch :] = jnp.broadcast_to(gain_buffer[...].reshape(1, -1), (16, width))
 
 
 def contract_near_kernel(weight_ref, kv_weight_ref, bias_ref, _, *refs):
@@ -222,14 +231,15 @@
     rows = states.shape[0] * states.shape[1] + 16
     low, high, carried, sent = kernel_call(
         contract_far_kernel,
-        [weight, kv_weight, states, norm_gain, in_hbm(vision_rows)],
-        [IN_HBM, IN_HBM, IN_VMEM, IN_VMEM, IN_HBM],
+        [weight, kv_weight, in_hbm(states), in_hbm(norm_gain), in_hbm(vision_rows)],
+        [IN_HBM] * 5,
         [pltpu.VMEM((2, features, 2 * HEAD_DIM), BF16)] * 2
         + [
             jax.ShapeDtypeStruct((rows, states.shape[2]), BF16),
             pltpu.VMEM(vision_rows.shape, BF16),
         ],
-        contract_scratch(1, features, width) + [pltpu.SemaphoreType.DMA(())],
+        contract_scratch(1, features, width)
+        + [pltpu.VMEM(norm_gain.shape, BF16), pltpu.SemaphoreType.DMA((2 + STEPS,))],
         flops=flops,
         moved=4 * 1024 * 1024,
     )
@@ -270,28 +280,41 @@
     )
 
 
-def kv_kernel(same_ref, other_ref, merged_ref, biased_ref, *outs):
+def kv_kernel(shifts, tokens, same_ref, other_ref, merged_ref, biased_ref, *refs):
+    outs = refs[tokens:]
     bias = biased_ref[:1]
-    for first_by in range(SIDE):
+    for at, by in enumerate(shifts):
         for second_by in range(SIDE):
-            rank = rank_from_here(first_by, second_by)
-            tiles = [ref[at, rank] for ref in (same_ref, other_ref) for at in range(SIDE)]
+            rank = rank_from_here(by, second_by)
+            tile = wrap(rank // SIDE - lax.axis_index("group") // 2) * SIDE + lax.rem(rank, SIDE)
+            tiles = [ref[hop, tile] for ref in (same_ref, other_ref) for hop in range(SIDE)]
             rows = jnp.concatenate(tiles, axis=0)
             part = jnp.dot(rows, merged_ref[...], preferred_element_type=F32)
-            outs[first_by][second_by] = (part + bias).astype(BF16)
+            part = (part + bias).astype(BF16)
+            if len(shifts) == 1:
+                outs[second_by // 2][second_by % 2] = part
+            else:
+                outs[at][second_by] = part
 
 
 def kv_partials(same, other, merged, biased):
     _, tiles, tile_rows, features = same.shape
     count = 2 * SIDE * tile_rows
-    return kernel_call(
-        kv_kernel,
-        [in_vmem(value) for value in (same, other, merged, biased)],
-        [IN_VMEM] * 4,
-        [pltpu.VMEM((SIDE, count, 2 * HEAD_DIM), BF16) for _ in range(SIDE)],
-        flops=4 * count * tiles * features * HEAD_DIM,
-        moved=12 * 1024 * 1024,
-    )
+    operands = [in_vmem(value) for value in (same, other, merged, biased)]
+
+    def call(shifts, shapes, after):
+        return kernel_call(
+            functools.partial(kv_kernel, shifts, len(after)),
+            [*operands, *after],
+            [IN_VMEM] * 4 + [ANY] * len(after),
+            [pltpu.VMEM((size, count, 2 * HEAD_DIM), BF16) for size in shapes],
+            flops=len(shifts) * count * tiles * features * HEAD_DIM,
+            moved=len(shifts) * 3 * 1024 * 1024,
+        )
+
+    low, high = call((2,), (2, 2), [])
+    one, three, own = call((1, 3, 0), (SIDE,) * 3, [low])
+    return low, high, one, three, own
 
 
 def sum_kernel(*refs, sources, count):
@@ -315,62 +338,44 @@
     )
 
 
-def query_kernel(full_ref, weight_ref, out_ref, held, held_sem, buffer, sem):
-    ranks, _, width = full_ref.shape
-    batch = out_ref.shape[0]
-    pieces = sem.shape[0]
-    deep = buffer.shape[0] // pieces
-    states = pltpu.make_async_copy(full_ref, held, held_sem)
-    states.start()
-    copies = [
-        pltpu.make_async_copy(
-            weight_ref.at[pl.ds(i * deep, deep)], buffer.at[pl.ds(i * deep, deep)], sem.at[i]
-        )
-        for i in range(pieces)
-    ]
-    for copy in copies:
-        copy.start()
-    states.wait()
+def query_kernel(batch, *refs):
+    parts, (weight_ref, out_ref) = refs[:SIDE], refs[SIDE:]
     total = jnp.zeros((batch, 1), F32)
-    for rank in range(ranks):
-        hidden = held[rank, :batch, :].astype(F32)
-        total += jnp.sum(hidden * hidden, axis=1, keepdims=True)
+    for part in parts:
+        for at in range(SIDE):
+            hidden = part[at, :batch, :].astype(F32)
+            total += jnp.sum(hidden * hidden, axis=1, keepdims=True)
     inverse = lax.rsqrt(total / D + 1e-05)
     accum = jnp.zeros(out_ref.shape, F32)
-    for rank in range(ranks):
-        hidden = held[rank, :batch, :].astype(F32)
-        gain = held[rank, batch : batch + 16, :].astype(F32)[:1]
-        normed = (hidden * inverse * gain).astype(BF16)
-        if rank * width % deep == 0:
-            copies[rank * width // deep].wait()
-        span = slice(rank * width, (rank + 1) * width)
-        accum += jnp.dot(normed, buffer[span, :], preferred_element_type=F32)
+    for part, far in zip(parts, HOPS):
+        width = part.shape[2]
+        for at, near in enumerate(HOPS):
+            hidden = part[at, :batch, :].astype(F32)
+            gain = part[at, batch : batch + 16, :].astype(F32)[:1]
+            normed = (hidden * inverse * gain).astype(BF16)
+            rank = rank_from_here(-near, -far)
+            rows = pl.ds(pl.multiple_of(rank * width, width), width)
+            accum += jnp.dot(normed, weight_ref[rows, :], preferred_element_type=F32)
     out_ref[...] = accum.astype(BF16)
 
 
-def queries(full, query_weight, batch):
+def queries(parts, query_weight, batch):
     columns = query_weight.shape[1]
     return kernel_call(
-        query_kernel,
-        [full, in_hbm(query_weight)],
-        [ANY, IN_HBM],
+        functools.partial(query_kernel, batch),
+        [*map(in_vmem, parts), in_vmem(query_weight)],
+        [IN_VMEM] * (SIDE + 1),
         pltpu.VMEM((batch, columns), BF16),
-        [
-            pltpu.VMEM(full.shape, BF16),
-            pltpu.SemaphoreType.DMA(()),
-            pltpu.VMEM(query_weight.shape, BF16),
-            pltpu.SemaphoreType.DMA((2,)),
-        ],
         flops=2 * batch * D * columns,
         moved=12 * 1024 * 1024,
     )
 
 
 def attend_kernel(
-    source_ref, count_ref, request_ref, query_ref, own_ref, other_ref, weight_ref, *outs
+    source_ref, count_ref, request_ref, query_ref, own_ref, other_ref, weight_ref, *refs
 ):
+    outs, context_ref = refs[:2], refs[2]
     batch, width = query_ref.shape
-    columns = outs[0].shape[2]
     half_rows = own_ref.shape[0]
     rows = 2 * half_rows
     slots = source_ref.shape[1]
@@ -411,29 +416,49 @@
         total = jnp.sum(weights, axis=1, keepdims=True)
         summed = jnp.dot(weights.astype(BF16), values, preferred_element_type=F32)
         contexts.append((summed / total).astype(BF16))
-    context = jnp.concatenate(contexts, axis=1)
-    for first_by in range(SIDE):
+    context_ref[...] = jnp.concatenate(contexts, axis=1)
+    branch_blocks(context_ref[...], weight_ref, (2,), outs)
+
+
+def branch_blocks(context, weight_ref, shifts, outs):
+    columns = outs[0].shape[2]
+    for at, by in enumerate(shifts):
         for second_by in range(SIDE):
-            rank = rank_from_here(first_by, second_by)
+            rank = rank_from_here(by, second_by)
             span = pl.ds(pl.multiple_of(rank * columns, columns), columns)
-            branch = jnp.dot(context, weight_ref[:, span], preferred_element_type=F32)
-            outs[first_by][second_by] = branch.astype(BF16)
+            part = jnp.dot(context, weight_ref[:, span], preferred_element_type=F32).astype(BF16)
+            if len(shifts) == 1:
+                outs[second_by // 2][second_by % 2] = part
+            else:
+                outs[at][second_by] = part
+
+
+def branch_kernel(context_ref, weight_ref, _, *outs):
+    branch_blocks(context_ref[...], weight_ref, (1, 3, 0), outs)
 
 
 def attend(tile_source, tile_count, row_request, query, own, other, out_weight):
     batch, width = query.shape
-    ranks = SIDE * SIDE
-    columns = out_weight.shape[1] // ranks
-    return kernel_call(
+    columns = out_weight.shape[1] // (SIDE * SIDE)
+    out_weight = in_vmem(out_weight)
+    low, high, context = kernel_call(
         attend_kernel,
-        [tile_source, tile_count, row_request]
-        + [in_vmem(value) for value in (query, own, other, out_weight)],
+        [tile_source, tile_count, row_request, *map(in_vmem, (query, own, other)), out_weight],
         [IN_SMEM, IN_SMEM] + [IN_VMEM] * 5,
-        [pltpu.VMEM((SIDE, batch, columns), BF16) for _ in range(SIDE)],
-        flops=2 * batch * width * out_weight.shape[1],
-        moved=12 * 1024 * 1024,
+        [pltpu.VMEM((2, batch, columns), BF16)] * 2 + [pltpu.VMEM((batch, width), BF16)],
+        flops=batch * width * out_weight.shape[1] // 2,
+        moved=4 * 1024 * 1024,
         transcendentals=batch * 4 * 512,
     )
+    one, three, own = kernel_call(
+        branch_kernel,
+        [in_vmem(context), out_weight, low],
+        [IN_VMEM, IN_VMEM, ANY],
+        [pltpu.VMEM((SIDE, batch, columns), BF16)] * 3,
+        flops=3 * batch * width * out_weight.shape[1] // 2,
+        moved=8 * 1024 * 1024,
+    )
+    return low, high, one, three, own
 
 
 def mix_kernel(gate_ref, local_ref, *refs):
@@ -487,23 +512,33 @@
     def around(block, by):
         return lax.ppermute(block, "group", [(g, (g + 2 * by) % groups) for g in range(groups)])
 
+    def first_sum(blocks, after=()):
+        low, high, one, three, own = blocks
+        low, high = shift(low, groups, FIRST, 1), shift(high, groups, FIRST, 3)
+        up, down = merge(one, low, three, high)
+        up, down = shift(up, groups, FIRST, 1), shift(down, groups, FIRST, 3)
+        return sum_blocks([own, up, down], after)
+
     with jax.named_scope("contract"):
-        low, high, one, three, own, biased, carried, sent = contract(
+        *blocks, biased, carried, sent = contract(
             proj_weight, kv_weight, proj_bias, states, norm_gain, vision_rows
         )
-        low, high = shift(low, groups, FIRST, 1), shift(high, groups, FIRST, 3)
-
-    with jax.named_scope("gather_states"):
-        full = lax.all_gather(carried, TP)
+
+    with jax.named_scope("load"):
+        query_here, out_here = load(query_weight, out_weight, after=[carried])
 
     with jax.named_scope("gather_rows"):
         after, before = around(sent, 1), around(sent, 3)
         near = [sent, after, before, around(after, 1)]
 
     with jax.named_scope("contract"):
-        up, down = merge(one, low, three, high)
-        up, down = shift(up, groups, FIRST, 1), shift(down, groups, FIRST, 3)
-        merged = sum_blocks([own, up, down], after=[near[3]])
+        merged = first_sum(blocks, [near[3], query_here, out_here])
+
+    with jax.named_scope("gather_states"):
+        (carried,) = join(
+            [carried[None]], [(0, 0, 0, 0, 1)], [(1, *carried.shape)], [merged[1]]
+        )
+        arrived = [shift(carried, groups, FIRST, by) for by in HOPS[1:]]
 
     with jax.named_scope("gather_rows"):
         (same,) = join(
@@ -516,31 +551,40 @@
 
     with jax.named_scope("contract"):
         merged = [part[None] for part in spread(merged, SECOND)]
-        (merged,) = sum_blocks(merged, after=[other])
+        (merged,) = sum_blocks(merged, after=[other, *arrived])
 
     with jax.named_scope("kv"):
         kv = kv_partials(same, other, merged, biased)
-        kv = sum_blocks(spread(kv, FIRST))
+
+    with jax.named_scope("gather_states"):
+        (states_near,) = join(
+            [carried] + arrived,
+            [(i, 0, 0, i, 1) for i in range(SIDE)],
+            [(SIDE, *carried.shape[1:])],
+            [kv[0]],
+        )
+        parts = spread([states_near] * SIDE, SECOND)
+
+    with jax.named_scope("kv"):
+        kv = first_sum(kv, parts[1:3])
+        query = queries(parts, query_here, batch)
         kv = [part[None] for part in spread(kv, SECOND)]
-        (out_here,) = load(out_weight, after=[full])
-        (kv,) = sum_blocks(kv, after=[out_here])
+        (kv,) = sum_blocks(kv)
         halves = []
         for flip in range(2):
-            pairs = [
-                (g * ranks + t, t // 2 * ranks + 2 * g + (t + flip) % 2)
-                for g in range(groups)
-                for t in range(ranks)
-            ]
+            pairs = []
+            for g in range(groups):
+                for t in range(ranks):
+                    tile = (t // SIDE - g // 2) % SIDE * SIDE + t % SIDE
+                    home = tile // 2 * ranks + 2 * g + (tile + flip) % 2
+                    pairs.append((g * ranks + t, home))
             halves.append(lax.ppermute(kv, EVERY, pairs))
-
-    with jax.named_scope("query"):
-        query = queries(full, query_weight, batch)
 
     with jax.named_scope("attend"):
         branch = attend(tile_source, tile_count, row_request, query, *halves, out_here)
 
     with jax.named_scope("mix"):
-        branch = sum_blocks(spread(branch, FIRST))
+        branch = first_sum(branch)
         return mix(attn_gate, states, spread(branch, SECOND))
 
 

time: 148 us -> 135 us (0.912)
  between operations: 14.3 us -> 0.89 us
  starting transfers between devices: 35.9 us -> 41.9 us
  local copies, waits for them, and re-layouts: 3.29 us -> 0.03 us
  waiting for transfers between devices: 71.6 us -> 68.6 us
    ppermute x19 -> x27, starting transfers between devices: 25.3 us -> 34.1 us  [shift(): return lax.ppermute(value, EVERY, pairs)]
    ppermute x3, waiting for transfers between devices: 17.9 us -> 12.1 us  [around(): lax.ppermute(block, 'group', [(g, (g + 2 * by) % groups) for g in range(g...]
    unnamed x18 -> x10, local copies, waits for them, and re-layouts: 3.29 us -> 0.03 us
    ppermute x2, starting transfers between devices: 8.24 us -> 5.41 us  [body(): halves.append(lax.ppermute(kv, EVERY, pairs))]
    ppermute x2, waiting for transfers between devices: 3.77 us -> 6.29 us  [body(): halves.append(lax.ppermute(kv, EVERY, pairs))]
    pallas_call x14 -> x20, Pallas kernels: 23 us -> 23.6 us  [kernel_call(): pl.pallas_call(kernel, in_specs=specs, out_specs=jax.tree.map(lambda _: I...]
    ppermute x19 -> x27, waiting for transfers between devices: 50 us -> 50.3 us  [shift(): return lax.ppermute(value, EVERY, pairs)]
  transfers between devices with their start and end apart: 26 -> 33, of which waited for: 17 -> 22; matrix products, arithmetic and copies ran while one was open for 0% -> 0% of each run, Pallas kernels for 11% -> 13%
where the time goes in v6:
time: 135 us
  waiting for transfers between devices  68.6 us (51%)
  starting transfers between devices  41.9 us (31%)
  Pallas kernels  23.6 us (17%)
    ppermute x27, waiting for transfers between devices, shift(): return lax.ppermute(value, EVERY, pairs)  50.3 us
    ppermute x27, starting transfers between devices, shift(): return lax.ppermute(value, EVERY, pairs)  34.1 us
    pallas_call x20, Pallas kernels, kernel_call(): pl.pallas_call(kernel, in_specs=specs, out_specs=jax.tree.map(lambda _: I...  23.6 us
    ppermute x3, waiting for transfers between devices, around(): lax.ppermute(block, 'group', [(g, (g + 2 * by) % groups) for g in range(g...  12.1 us
    ppermute x2, waiting for transfers between devices, body(): halves.append(lax.ppermute(kv, EVERY, pairs))  6.29 us
    ppermute x2, starting transfers between devices, body(): halves.append(lax.ppermute(kv, EVERY, pairs))  5.41 us
  transfers between devices with their start and end apart: 33, of which 22 were waited for; matrix products, arithmetic and copies ran while one was open for 0% of the time, Pallas kernels for 13%

profile of v6, /device:TPU:30, one launch (start us, length us, event | category | flops | bytes accessed | tf_op | source)
XLA Modules:
  0.0 135.1 jit_solution(8800941982814541242)
XLA Ops:
  0.0 2.6 %contract.5 = (bf16[2,480,256]{2,1,0:T(8,128)(2,1)S(1)}, bf16[2,480,256]{2,1,0:T(8,128)(2,1)S(1)}, bf16[144,512]{1,0:T(8,128)(2,1)S(1)}, bf16[1,16,32,480]{3,2,1,0:T(8,128)(2,1)S(1)}) custom-call(bf16[4,4,480,512]{3,2,1,0:T(8,128)(2,1)} %bitcast.21, bf16[2,512,1024]{2,1,0:T(8,128)(2,1)} %kv_weight_ref.3, bf16[2,64,512]{2,1,0:T(8,128)(2,1)} %local_ref.1, ...), custom_call_target="tpu_custom_call" | custom-call | flops 503316480 | bytes 4194304 | tf_op jit(solution)/shard_map/contract/pallas_call | solution.py:52
  5.0 5.4 %contract.6 = (bf16[4,480,256]{2,1,0:T(8,128)(2,1)S(1)}, bf16[4,480,256]{2,1,0:T(8,128)(2,1)S(1)}, bf16[4,480,256]{2,1,0:T(8,128)(2,1)S(1)}, f32[16,256]{1,0:T(8,128)S(1)}) custom-call(bf16[4,4,480,512]{3,2,1,0:T(8,128)(2,1)} %bitcast.22, bf16[2,512,1024]{2,1,0:T(8,128)(2,1)} %kv_weight_ref.3, bf16[512]{0:T(512)(128)(2,1)S(1)} %copy-done.2, ...), custom_call_target="tpu_custom_call" | custom-call | flops 1509949440 | bytes 10485760 | tf_op jit(solution)/shard_map/contract/pallas_call | solution.py:52
  15.6 3.3 %collective-permute-done.4.refs_1_ = bf16[1,16,32,480]{3,2,1,0:T(8,128)(2,1)S(1)} collective-permute-done((bf16[1,16,32,480]{3,2,1,0:T(8,128)(2,1)S(1)}, bf16[1,16,32,480]{3,2,1,0:T(8,128)(2,1)S(1)}, u32[]{:S(2)}, u32[]{:S(2)}) %collective-permute-start.4) | collective-permute-done | bytes 491552 | tf_op jit(solution)/shard_map/gather_rows/ppermute | solution.py:513
  20.9 5.8 %load.1 = (bf16[8192,512]{1,0:T(8,128)(2,1)S(1)}, bf16[512,8192]{1,0:T(8,128)(2,1)S(1)}) custom-call(bf16[8192,512]{1,0:T(8,128)(2,1)} %refs_0_.1, bf16[512,8192]{1,0:T(8,128)(2,1)} %refs_1_.1, bf16[144,512]{1,0:T(8,128)(2,1)S(1)} %get-tuple-element.44.refs_2_), custom_call_target="tpu_custom_call" | custom-call | bytes 33554432 | tf_op jit(solution)/shard_map/load/pallas_call | solution.py:52
  26.7 6.8 %collective-permute-done.5.refs_3_ = bf16[1,16,32,480]{3,2,1,0:T(8,128)(2,1)S(1)} collective-permute-done((bf16[1,16,32,480]{3,2,1,0:T(8,128)(2,1)S(1)}, bf16[1,16,32,480]{3,2,1,0:T(8,128)(2,1)S(1)}, u32[]{:S(2)}, u32[]{:S(2)}) %collective-permute-start.5) | collective-permute-done | bytes 491552 | tf_op jit(solution)/shard_map/gather_rows/ppermute | solution.py:513
  38.4 3.2 %collective-permute-start.12 = (bf16[480,256]{1,0:T(8,128)(2,1)S(1)}, bf16[480,256]{1,0:T(8,128)(2,1)S(1)}, u32[]{:S(2)}, u32[]{:S(2)}) collective-permute-start(bf16[480,256]{1,0:T(8,128)(2,1)S(1)} %get-tuple-element.57), channel_id=1, source_target_pairs={{0,12},{1,13},{2,14},{3,15},{4,0},{5,1},{6,2},{7,3},{8,4},{9,5},{1... | collective-permute-start | bytes 737288 | tf_op jit(solution)/shard_map/contract/ppermute | solution.py:40
  44.1 6.6 %collective-permute-done.8.refs_7_.refs_3_ = bf16[1,144,512]{2,1,0:T(8,128)(2,1)S(1)} collective-permute-done((bf16[1,144,512]{2,1,0:T(8,128)(2,1)S(1)}, bf16[1,144,512]{2,1,0:T(8,128)(2,1)S(1)}, u32[]{:S(2)}, u32[]{:S(2)}) %collective-permute-start.8) | collective-permute-done | bytes 147488 | tf_op jit(solution)/shard_map/gather_states/ppermute | solution.py:40
  51.5 2.2 %collective-permute-start.17 = (bf16[2,256,256]{2,1,0:T(8,128)(2,1)S(1)}, bf16[2,256,256]{2,1,0:T(8,128)(2,1)S(1)}, u32[]{:S(2)}, u32[]{:S(2)}) collective-permute-start(bf16[2,256,256]{2,1,0:T(8,128)(2,1)S(1)} %get-tuple-element.60.refs_4_.refs_0_), channel_id=1, source_target_pairs={{0,1},{1,2},{2,3},{3,0},{4,5},{5,6},{6,7},{7,4},{8,9},{9,10},{10,1... | collective-permute-start | bytes 786440 | tf_op jit(solution)/shard_map/kv/ppermute | solution.py:40
  54.6 3.2 %collective-permute-start.15 = (bf16[4,144,512]{2,1,0:T(8,128)(2,1)S(1)}, bf16[4,144,512]{2,1,0:T(8,128)(2,1)S(1)}, u32[]{:S(2)}, u32[]{:S(2)}) collective-permute-start(bf16[4,144,512]{2,1,0:T(8,128)(2,1)S(1)} %gather_states.3.refs_0_), channel_id=1, source_target_pairs={{0,12},{1,13},{2,14},{3,15},{4,0},{5,1},{6,2},{7,3},{8,4},{9,5},{1... | collective-permute-start | bytes 1769480 | tf_op jit(solution)/shard_map/gather_states/ppermute | solution.py:40
  58.9 3.6 %collective-permute-done.18.high_ref = bf16[2,256,256]{2,1,0:T(8,128)(2,1)S(1)} collective-permute-done((bf16[2,256,256]{2,1,0:T(8,128)(2,1)S(1)}, bf16[2,256,256]{2,1,0:T(8,128)(2,1)S(1)}, u32[]{:S(2)}, u32[]{:S(2)}) %collective-permute-start.18) | collective-permute-done | bytes 262176 | tf_op jit(solution)/shard_map/kv/ppermute | solution.py:40
  64.9 2.3 %collective-permute-start.16 = (bf16[4,144,512]{2,1,0:T(8,128)(2,1)S(1)}, bf16[4,144,512]{2,1,0:T(8,128)(2,1)S(1)}, u32[]{:S(2)}, u32[]{:S(2)}) collective-permute-start(bf16[4,144,512]{2,1,0:T(8,128)(2,1)S(1)} %gather_states.3.refs_0_), channel_id=1, source_target_pairs={{0,8},{1,9},{2,10},{3,11},{4,12},{5,13},{6,14},{7,15},{8,0},{9,1},... | collective-permute-start | bytes 1769480 | tf_op jit(solution)/shard_map/gather_states/ppermute | solution.py:40
  68.8 8.0 %collective-permute-done.19.refs_1_ = bf16[4,256,256]{2,1,0:T(8,128)(2,1)S(1)} collective-permute-done((bf16[4,256,256]{2,1,0:T(8,128)(2,1)S(1)}, bf16[4,256,256]{2,1,0:T(8,128)(2,1)S(1)}, u32[]{:S(2)}, u32[]{:S(2)}) %collective-permute-start.19) | collective-permute-done | bytes 524320 | tf_op jit(solution)/shard_map/kv/ppermute | solution.py:40
  76.8 2.8 %collective-permute-done.20.refs_2_ = bf16[4,256,256]{2,1,0:T(8,128)(2,1)S(1)} collective-permute-done((bf16[4,256,256]{2,1,0:T(8,128)(2,1)S(1)}, bf16[4,256,256]{2,1,0:T(8,128)(2,1)S(1)}, u32[]{:S(2)}, u32[]{:S(2)}) %collective-permute-start.20) | collective-permute-done | bytes 524320 | tf_op jit(solution)/shard_map/kv/ppermute | solution.py:40
  82.7 2.6 %collective-permute-start.22 = (bf16[256,256]{1,0:T(8,128)(2,1)S(1)}, bf16[256,256]{1,0:T(8,128)(2,1)S(1)}, u32[]{:S(2)}, u32[]{:S(2)}) collective-permute-start(bf16[256,256]{1,0:T(8,128)(2,1)S(1)} %get-tuple-element.69), channel_id=1, source_target_pairs={{0,12},{1,13},{2,14},{3,15},{4,0},{5,1},{6,2},{7,3},{8,4},{9,5},{1... | collective-permute-start | bytes 393224 | tf_op jit(solution)/shard_map/kv/ppermute | solution.py:40
  88.3 2.8 %collective-permute-start.24 = (bf16[256,256]{1,0:T(8,128)(2,1)S(1)}, bf16[256,256]{1,0:T(8,128)(2,1)S(1)}, u32[]{:S(2)}, u32[]{:S(2)}) collective-permute-start(bf16[256,256]{1,0:T(8,128)(2,1)S(1)} %kv.11), channel_id=1, source_target_pairs={{0,0},{1,1},{2,16},{3,17},{4,32},{5,33},{6,48},{7,49},{8,64},{9,65... | collective-permute-start | bytes 393224 | tf_op jit(solution)/shard_map/kv/ppermute | solution.py:581
  91.1 2.6 %collective-permute-start.25 = (bf16[256,256]{1,0:T(8,128)(2,1)S(1)}, bf16[256,256]{1,0:T(8,128)(2,1)S(1)}, u32[]{:S(2)}, u32[]{:S(2)}) collective-permute-start(bf16[256,256]{1,0:T(8,128)(2,1)S(1)} %kv.11), channel_id=1, source_target_pairs={{0,1},{1,0},{2,17},{3,16},{4,33},{5,32},{6,49},{7,48},{8,65},{9,64... | collective-permute-start | bytes 393224 | tf_op jit(solution)/shard_map/kv/ppermute | solution.py:581
  95.4 5.6 %collective-permute-done.24.own_ref = bf16[256,256]{1,0:T(8,128)(2,1)S(1)} collective-permute-done((bf16[256,256]{1,0:T(8,128)(2,1)S(1)}, bf16[256,256]{1,0:T(8,128)(2,1)S(1)}, u32[]{:S(2)}, u32[]{:S(2)}) %collective-permute-start.24) | collective-permute-done | bytes 131104 | tf_op jit(solution)/shard_map/kv/ppermute | solution.py:581
  101.7 2.2 %attend.2 = (bf16[2,128,512]{2,1,0:T(8,128)(2,1)S(1)}, bf16[2,128,512]{2,1,0:T(8,128)(2,1)S(1)}, bf16[128,512]{1,0:T(8,128)(2,1)S(1)}) custom-call(s32[8,16]{1,0:T(8,128)S(1)} %copy-done.1, s32[32]{0:T(128)S(1)} %copy-done.3, s32[1,64]{1,0:T(1,128)S(1)} %copy-done.4, bf16[128,512]{1,0:T(8,128)(2,1)S(1)} %kv.7.query_ref, ...), custom_call_target="tpu_custom_call" | custom-call | flops 268435456 | bytes 4194304 | tf_op jit(solution)/shard_map/attend/pallas_call | solution.py:52
  107.2 3.2 %collective-permute-done.26.low_ref = bf16[2,128,512]{2,1,0:T(8,128)(2,1)S(1)} collective-permute-done((bf16[2,128,512]{2,1,0:T(8,128)(2,1)S(1)}, bf16[2,128,512]{2,1,0:T(8,128)(2,1)S(1)}, u32[]{:S(2)}, u32[]{:S(2)}) %collective-permute-start.26) | collective-permute-done | bytes 262176 | tf_op jit(solution)/shard_map/mix/ppermute | solution.py:40
  110.4 3.2 %collective-permute-done.27.high_ref = bf16[2,128,512]{2,1,0:T(8,128)(2,1)S(1)} collective-permute-done((bf16[2,128,512]{2,1,0:T(8,128)(2,1)S(1)}, bf16[2,128,512]{2,1,0:T(8,128)(2,1)S(1)}, u32[]{:S(2)}, u32[]{:S(2)}) %collective-permute-start.27) | collective-permute-done | bytes 262176 | tf_op jit(solution)/shard_map/mix/ppermute | solution.py:40
  115.8 8.6 %collective-permute-done.28.refs_1_ = bf16[4,128,512]{2,1,0:T(8,128)(2,1)S(1)} collective-permute-done((bf16[4,128,512]{2,1,0:T(8,128)(2,1)S(1)}, bf16[4,128,512]{2,1,0:T(8,128)(2,1)S(1)}, u32[]{:S(2)}, u32[]{:S(2)}) %collective-permute-start.28) | collective-permute-done | bytes 524320 | tf_op jit(solution)/shard_map/mix/ppermute | solution.py:40
  124.6 3.2 %collective-permute-start.31 = (bf16[128,512]{1,0:T(8,128)(2,1)S(1)}, bf16[128,512]{1,0:T(8,128)(2,1)S(1)}, u32[]{:S(2)}, u32[]{:S(2)}) collective-permute-start(bf16[128,512]{1,0:T(8,128)(2,1)S(1)} %get-tuple-element.81), channel_id=1, source_target_pairs={{0,12},{1,13},{2,14},{3,15},{4,0},{5,1},{6,2},{7,3},{8,4},{9,5},{1... | collective-permute-start | bytes 393224 | tf_op jit(solution)/shard_map/mix/ppermute | solution.py:40
  128.5 2.3 %collective-permute-done.30.refs_1_ = bf16[128,512]{1,0:T(8,128)(2,1)S(1)} collective-permute-done((bf16[128,512]{1,0:T(8,128)(2,1)S(1)}, bf16[128,512]{1,0:T(8,128)(2,1)S(1)}, u32[]{:S(2)}, u32[]{:S(2)}) %collective-permute-start.30) | collective-permute-done | bytes 131104 | tf_op jit(solution)/shard_map/mix/ppermute | solution.py:40
  131.8 2.5 %collective-permute-done.32.refs_3_ = bf16[128,512]{1,0:T(8,128)(2,1)S(1)} collective-permute-done((bf16[128,512]{1,0:T(8,128)(2,1)S(1)}, bf16[128,512]{1,0:T(8,128)(2,1)S(1)}, u32[]{:S(2)}, u32[]{:S(2)}) %collective-permute-start.32) | collective-permute-done | bytes 131104 | tf_op jit(solution)/shard_map/mix/ppermute | solution.py:40
  (72 shorter events, 39.4 us)
Async XLA Ops:
  2.6 8.9 %collective-permute-start = (bf16[2,480,256]{2,1,0:T(8,128)(2,1)S(1)}, bf16[2,480,256]{2,1,0:T(8,128)(2,1)S(1)}, u32[]{:S(2)}, u32[]{:S(2)}) collective-permute-start(bf16[2,480,256]{2,1,0:T(8,128)(2,1)S(1)} %get-tuple-element.45._), channel_id=1, source_target_pairs={{0,1},{1,2},{2,3},{3,0},{4,5},{5,6},{6,7},{7,4},{8,9},{9,10},{10,1... | collective-permute-start | bytes 1474568 | tf_op jit(solution)/shard_map/contract/ppermute | solution.py:40
  3.2 10.0 %collective-permute-start.1 = (bf16[2,480,256]{2,1,0:T(8,128)(2,1)S(1)}, bf16[2,480,256]{2,1,0:T(8,128)(2,1)S(1)}, u32[]{:S(2)}, u32[]{:S(2)}) collective-permute-start(bf16[2,480,256]{2,1,0:T(8,128)(2,1)S(1)} %get-tuple-element.49), channel_id=1, source_target_pairs={{0,3},{1,0},{2,1},{3,2},{4,7},{5,4},{6,5},{7,6},{8,11},{9,8},{10,9... | collective-permute-start | bytes 1474568 | tf_op jit(solution)/shard_map/contract/ppermute | solution.py:40
  4.7 14.2 %collective-permute-start.4 = (bf16[1,16,32,480]{3,2,1,0:T(8,128)(2,1)S(1)}, bf16[1,16,32,480]{3,2,1,0:T(8,128)(2,1)S(1)}, u32[]{:S(2)}, u32[]{:S(2)}) collective-permute-start(bf16[1,16,32,480]{3,2,1,0:T(8,128)(2,1)S(1)} %get-tuple-element.52.refs_0_), channel_id=1, source_target_pairs={{0,32},{16,48},{32,64},{48,80},{64,96},{80,112},{96,0},{112,16},{1... | collective-permute-start | bytes 1474568 | tf_op jit(solution)/shard_map/gather_rows/ppermute | solution.py:513
  13.5 20.0 %collective-permute-start.2 = (bf16[4,480,256]{2,1,0:T(8,128)(2,1)S(1)}, bf16[4,480,256]{2,1,0:T(8,128)(2,1)S(1)}, u32[]{:S(2)}, u32[]{:S(2)}) collective-permute-start(bf16[4,480,256]{2,1,0:T(8,128)(2,1)S(1)} %get-tuple-element.50), channel_id=1, source_target_pairs={{0,1},{1,2},{2,3},{3,0},{4,5},{5,6},{6,7},{7,4},{8,9},{9,10},{10,1... | collective-permute-start | bytes 2949128 | tf_op jit(solution)/shard_map/contract/ppermute | solution.py:40
  13.8 19.6 %collective-permute-start.3 = (bf16[4,480,256]{2,1,0:T(8,128)(2,1)S(1)}, bf16[4,480,256]{2,1,0:T(8,128)(2,1)S(1)}, u32[]{:S(2)}, u32[]{:S(2)}) collective-permute-start(bf16[4,480,256]{2,1,0:T(8,128)(2,1)S(1)} %get-tuple-element.51), channel_id=1, source_target_pairs={{0,3},{1,0},{2,1},{3,2},{4,7},{5,4},{6,5},{7,6},{8,11},{9,8},{10,9... | collective-permute-start | bytes 2949128 | tf_op jit(solution)/shard_map/contract/ppermute | solution.py:40
  18.9 14.6 %collective-permute-start.5 = (bf16[1,16,32,480]{3,2,1,0:T(8,128)(2,1)S(1)}, bf16[1,16,32,480]{3,2,1,0:T(8,128)(2,1)S(1)}, u32[]{:S(2)}, u32[]{:S(2)}) collective-permute-start(bf16[1,16,32,480]{3,2,1,0:T(8,128)(2,1)S(1)} %collective-permute-done.4.refs_1_), channel_id=1, source_target_pairs={{0,32},{16,48},{32,64},{48,80},{64,96},{80,112},{96,0},{112,16},{1... | collective-permute-start | bytes 1474568 | tf_op jit(solution)/shard_map/gather_rows/ppermute | solution.py:513
  20.3 15.6 %collective-permute-start.9 = (bf16[1,16,32,480]{3,2,1,0:T(8,128)(2,1)S(1)}, bf16[1,16,32,480]{3,2,1,0:T(8,128)(2,1)S(1)}, u32[]{:S(2)}, u32[]{:S(2)}) collective-permute-start(bf16[1,16,32,480]{3,2,1,0:T(8,128)(2,1)S(1)} %get-tuple-element.52.refs_0_), channel_id=1, source_target_pairs={{0,96},{16,112},{32,0},{48,16},{64,32},{80,48},{96,64},{112,80},{1... | collective-permute-start | bytes 1474568 | tf_op jit(solution)/shard_map/gather_rows/ppermute | solution.py:513
  36.0 14.9 %collective-permute-start.10 = (bf16[4,16,32,480]{3,2,1,0:T(8,128)(2,1)S(1)}, bf16[4,16,32,480]{3,2,1,0:T(8,128)(2,1)S(1)}, u32[]{:S(2)}, u32[]{:S(2)}) collective-permute-start(bf16[4,16,32,480]{3,2,1,0:T(8,128)(2,1)S(1)} %gather_rows.1.same_ref), channel_id=1, source_target_pairs={{0,16},{16,0},{32,48},{48,32},{64,80},{80,64},{96,112},{112,96},{1... | collective-permute-start | bytes 5898248 | tf_op jit(solution)/shard_map/gather_rows/ppermute | solution.py:550
  38.4 12.4 %collective-permute-start.11 = (bf16[480,256]{1,0:T(8,128)(2,1)S(1)}, bf16[480,256]{1,0:T(8,128)(2,1)S(1)}, u32[]{:S(2)}, u32[]{:S(2)}) collective-permute-start(bf16[480,256]{1,0:T(8,128)(2,1)S(1)} %get-tuple-element.55.refs_1_.refs_4_), channel_id=1, source_target_pairs={{0,4},{1,5},{2,6},{3,7},{4,8},{5,9},{6,10},{7,11},{8,12},{9,13},{1... | collective-permute-start | bytes 737288 | tf_op jit(solution)/shard_map/contract/ppermute | solution.py:40
  38.4 12.4 %collective-permute-start.12 = (bf16[480,256]{1,0:T(8,128)(2,1)S(1)}, bf16[480,256]{1,0:T(8,128)(2,1)S(1)}, u32[]{:S(2)}, u32[]{:S(2)}) collective-permute-start(bf16[480,256]{1,0:T(8,128)(2,1)S(1)} %get-tuple-element.57), channel_id=1, source_target_pairs={{0,12},{1,13},{2,14},{3,15},{4,0},{5,1},{6,2},{7,3},{8,4},{9,5},{1... | collective-permute-start | bytes 737288 | tf_op jit(solution)/shard_map/contract/ppermute | solution.py:40
  41.7 9.3 %collective-permute-start.13 = (bf16[480,256]{1,0:T(8,128)(2,1)S(1)}, bf16[480,256]{1,0:T(8,128)(2,1)S(1)}, u32[]{:S(2)}, u32[]{:S(2)}) collective-permute-start(bf16[480,256]{1,0:T(8,128)(2,1)S(1)} %get-tuple-element.58), channel_id=1, source_target_pairs={{0,8},{1,9},{2,10},{3,11},{4,12},{5,13},{6,14},{7,15},{8,0},{9,1},... | collective-permute-start | bytes 737288 | tf_op jit(solution)/shard_map/contract/ppermute | solution.py:40
  51.5 7.3 %collective-permute-start.17 = (bf16[2,256,256]{2,1,0:T(8,128)(2,1)S(1)}, bf16[2,256,256]{2,1,0:T(8,128)(2,1)S(1)}, u32[]{:S(2)}, u32[]{:S(2)}) collective-permute-start(bf16[2,256,256]{2,1,0:T(8,128)(2,1)S(1)} %get-tuple-element.60.refs_4_.refs_0_), channel_id=1, source_target_pairs={{0,1},{1,2},{2,3},{3,0},{4,5},{5,6},{6,7},{7,4},{8,9},{9,10},{10,1... | collective-permute-start | bytes 786440 | tf_op jit(solution)/shard_map/kv/ppermute | solution.py:40
  53.7 8.7 %collective-permute-start.18 = (bf16[2,256,256]{2,1,0:T(8,128)(2,1)S(1)}, bf16[2,256,256]{2,1,0:T(8,128)(2,1)S(1)}, u32[]{:S(2)}, u32[]{:S(2)}) collective-permute-start(bf16[2,256,256]{2,1,0:T(8,128)(2,1)S(1)} %get-tuple-element.64), channel_id=1, source_target_pairs={{0,3},{1,0},{2,1},{3,2},{4,7},{5,4},{6,5},{7,6},{8,11},{9,8},{10,9... | collective-permute-start | bytes 786440 | tf_op jit(solution)/shard_map/kv/ppermute | solution.py:40
  54.5 14.3 %collective-permute-start.14 = (bf16[4,144,512]{2,1,0:T(8,128)(2,1)S(1)}, bf16[4,144,512]{2,1,0:T(8,128)(2,1)S(1)}, u32[]{:S(2)}, u32[]{:S(2)}) collective-permute-start(bf16[4,144,512]{2,1,0:T(8,128)(2,1)S(1)} %gather_states.3.refs_0_), channel_id=1, source_target_pairs={{0,4},{1,5},{2,6},{3,7},{4,8},{5,9},{6,10},{7,11},{8,12},{9,13},{1... | collective-permute-start | bytes 1769480 | tf_op jit(solution)/shard_map/gather_states/ppermute | solution.py:40
  54.6 14.2 %collective-permute-start.15 = (bf16[4,144,512]{2,1,0:T(8,128)(2,1)S(1)}, bf16[4,144,512]{2,1,0:T(8,128)(2,1)S(1)}, u32[]{:S(2)}, u32[]{:S(2)}) collective-permute-start(bf16[4,144,512]{2,1,0:T(8,128)(2,1)S(1)} %gather_states.3.refs_0_), channel_id=1, source_target_pairs={{0,12},{1,13},{2,14},{3,15},{4,0},{5,1},{6,2},{7,3},{8,4},{9,5},{1... | collective-permute-start | bytes 1769480 | tf_op jit(solution)/shard_map/gather_states/ppermute | solution.py:40
  62.6 14.2 %collective-permute-start.19 = (bf16[4,256,256]{2,1,0:T(8,128)(2,1)S(1)}, bf16[4,256,256]{2,1,0:T(8,128)(2,1)S(1)}, u32[]{:S(2)}, u32[]{:S(2)}) collective-permute-start(bf16[4,256,256]{2,1,0:T(8,128)(2,1)S(1)} %get-tuple-element.65), channel_id=1, source_target_pairs={{0,1},{1,2},{2,3},{3,0},{4,5},{5,6},{6,7},{7,4},{8,9},{9,10},{10,1... | collective-permute-start | bytes 1572872 | tf_op jit(solution)/shard_map/kv/ppermute | solution.py:40
  62.9 16.7 %collective-permute-start.20 = (bf16[4,256,256]{2,1,0:T(8,128)(2,1)S(1)}, bf16[4,256,256]{2,1,0:T(8,128)(2,1)S(1)}, u32[]{:S(2)}, u32[]{:S(2)}) collective-permute-start(bf16[4,256,256]{2,1,0:T(8,128)(2,1)S(1)} %get-tuple-element.66), channel_id=1, source_target_pairs={{0,3},{1,0},{2,1},{3,2},{4,7},{5,4},{6,5},{7,6},{8,11},{9,8},{10,9... | collective-permute-start | bytes 1572872 | tf_op jit(solution)/shard_map/kv/ppermute | solution.py:40
  64.9 28.8 %collective-permute-start.16 = (bf16[4,144,512]{2,1,0:T(8,128)(2,1)S(1)}, bf16[4,144,512]{2,1,0:T(8,128)(2,1)S(1)}, u32[]{:S(2)}, u32[]{:S(2)}) collective-permute-start(bf16[4,144,512]{2,1,0:T(8,128)(2,1)S(1)} %gather_states.3.refs_0_), channel_id=1, source_target_pairs={{0,8},{1,9},{2,10},{3,11},{4,12},{5,13},{6,14},{7,15},{8,0},{9,1},... | collective-permute-start | bytes 1769480 | tf_op jit(solution)/shard_map/gather_states/ppermute | solution.py:40
  80.8 7.4 %collective-permute-start.21 = (bf16[256,256]{1,0:T(8,128)(2,1)S(1)}, bf16[256,256]{1,0:T(8,128)(2,1)S(1)}, u32[]{:S(2)}, u32[]{:S(2)}) collective-permute-start(bf16[256,256]{1,0:T(8,128)(2,1)S(1)} %get-tuple-element.68), channel_id=1, source_target_pairs={{0,4},{1,5},{2,6},{3,7},{4,8},{5,9},{6,10},{7,11},{8,12},{9,13},{1... | collective-permute-start | bytes 393224 | tf_op jit(solution)/shard_map/kv/ppermute | solution.py:40
  88.3 12.7 %collective-permute-start.24 = (bf16[256,256]{1,0:T(8,128)(2,1)S(1)}, bf16[256,256]{1,0:T(8,128)(2,1)S(1)}, u32[]{:S(2)}, u32[]{:S(2)}) collective-permute-start(bf16[256,256]{1,0:T(8,128)(2,1)S(1)} %kv.11), channel_id=1, source_target_pairs={{0,0},{1,1},{2,16},{3,17},{4,32},{5,33},{6,48},{7,49},{8,64},{9,65... | collective-permute-start | bytes 393224 | tf_op jit(solution)/shard_map/kv/ppermute | solution.py:581
  91.1 10.6 %collective-permute-start.25 = (bf16[256,256]{1,0:T(8,128)(2,1)S(1)}, bf16[256,256]{1,0:T(8,128)(2,1)S(1)}, u32[]{:S(2)}, u32[]{:S(2)}) collective-permute-start(bf16[256,256]{1,0:T(8,128)(2,1)S(1)} %kv.11), channel_id=1, source_target_pairs={{0,1},{1,0},{2,17},{3,16},{4,33},{5,32},{6,49},{7,48},{8,65},{9,64... | collective-permute-start | bytes 393224 | tf_op jit(solution)/shard_map/kv/ppermute | solution.py:581
  106.0 7.6 %collective-permute-start.27 = (bf16[2,128,512]{2,1,0:T(8,128)(2,1)S(1)}, bf16[2,128,512]{2,1,0:T(8,128)(2,1)S(1)}, u32[]{:S(2)}, u32[]{:S(2)}) collective-permute-start(bf16[2,128,512]{2,1,0:T(8,128)(2,1)S(1)} %get-tuple-element.76), channel_id=1, source_target_pairs={{0,3},{1,0},{2,1},{3,2},{4,7},{5,4},{6,5},{7,6},{8,11},{9,8},{10,9... | collective-permute-start | bytes 786440 | tf_op jit(solution)/shard_map/mix/ppermute | solution.py:40
  113.7 10.7 %collective-permute-start.28 = (bf16[4,128,512]{2,1,0:T(8,128)(2,1)S(1)}, bf16[4,128,512]{2,1,0:T(8,128)(2,1)S(1)}, u32[]{:S(2)}, u32[]{:S(2)}) collective-permute-start(bf16[4,128,512]{2,1,0:T(8,128)(2,1)S(1)} %get-tuple-element.77), channel_id=1, source_target_pairs={{0,1},{1,2},{2,3},{3,0},{4,5},{5,6},{6,7},{7,4},{8,9},{9,10},{10,1... | collective-permute-start | bytes 1572872 | tf_op jit(solution)/shard_map/mix/ppermute | solution.py:40
  113.8 10.6 %collective-permute-start.29 = (bf16[4,128,512]{2,1,0:T(8,128)(2,1)S(1)}, bf16[4,128,512]{2,1,0:T(8,128)(2,1)S(1)}, u32[]{:S(2)}, u32[]{:S(2)}) collective-permute-start(bf16[4,128,512]{2,1,0:T(8,128)(2,1)S(1)} %get-tuple-element.78), channel_id=1, source_target_pairs={{0,3},{1,0},{2,1},{3,2},{4,7},{5,4},{6,5},{7,6},{8,11},{9,8},{10,9... | collective-permute-start | bytes 1572872 | tf_op jit(solution)/shard_map/mix/ppermute | solution.py:40
  (14 other events, 229.7 us)

commit v7 on v6

--- a/solution.py
+++ b/solution.py
@@ -372,9 +372,8 @@
 
 
 def attend_kernel(
-    source_ref, count_ref, request_ref, query_ref, own_ref, other_ref, weight_ref, *refs
+    source_ref, count_ref, request_ref, query_ref, own_ref, other_ref, weight_ref, *outs
 ):
-    outs, context_ref = refs[:2], refs[2]
     batch, width = query_ref.shape
     half_rows = own_ref.shape[0]
     rows = 2 * half_rows
@@ -416,49 +415,29 @@
         total = jnp.sum(weights, axis=1, keepdims=True)
         summed = jnp.dot(weights.astype(BF16), values, preferred_element_type=F32)
         contexts.append((summed / total).astype(BF16))
-    context_ref[...] = jnp.concatenate(contexts, axis=1)
-    branch_blocks(context_ref[...], weight_ref, (2,), outs)
-
-
-def branch_blocks(context, weight_ref, shifts, outs):
+    context = jnp.concatenate(contexts, axis=1)
     columns = outs[0].shape[2]
-    for at, by in enumerate(shifts):
+    for first_by in range(SIDE):
         for second_by in range(SIDE):
-            rank = rank_from_here(by, second_by)
+            rank = rank_from_here(first_by, second_by)
             span = pl.ds(pl.multiple_of(rank * columns, columns), columns)
-            part = jnp.dot(context, weight_ref[:, span], preferred_element_type=F32).astype(BF16)
-            if len(shifts) == 1:
-                outs[second_by // 2][second_by % 2] = part
-            else:
-                outs[at][second_by] = part
-
-
-def branch_kernel(context_ref, weight_ref, _, *outs):
-    branch_blocks(context_ref[...], weight_ref, (1, 3, 0), outs)
+            branch = jnp.dot(context, weight_ref[:, span], preferred_element_type=F32)
+            outs[first_by][second_by] = branch.astype(BF16)
 
 
 def attend(tile_source, tile_count, row_request, query, own, other, out_weight):
     batch, width = query.shape
     columns = out_weight.shape[1] // (SIDE * SIDE)
-    out_weight = in_vmem(out_weight)
-    low, high, context = kernel_call(
+    return kernel_call(
         attend_kernel,
-        [tile_source, tile_count, row_request, *map(in_vmem, (query, own, other)), out_weight],
+        [tile_source, tile_count, row_request]
+        + [in_vmem(value) for value in (query, own, other, out_weight)],
         [IN_SMEM, IN_SMEM] + [IN_VMEM] * 5,
-        [pltpu.VMEM((2, batch, columns), BF16)] * 2 + [pltpu.VMEM((batch, width), BF16)],
-        flops=batch * width * out_weight.shape[1] // 2,
-        moved=4 * 1024 * 1024,
+        [pltpu.VMEM((SIDE, batch, columns), BF16) for _ in range(SIDE)],
+        flops=2 * batch * width * out_weight.shape[1],
+        moved=12 * 1024 * 1024,
         transcendentals=batch * 4 * 512,
     )
-    one, three, own = kernel_call(
-        branch_kernel,
-        [in_vmem(context), out_weight, low],
-        [IN_VMEM, IN_VMEM, ANY],
-        [pltpu.VMEM((SIDE, batch, columns), BF16)] * 3,
-        flops=3 * batch * width * out_weight.shape[1] // 2,
-        moved=8 * 1024 * 1024,
-    )
-    return low, high, one, three, own
 
 
 def mix_kernel(gate_ref, local_ref, *refs):
@@ -534,12 +513,6 @@
     with jax.named_scope("contract"):
         merged = first_sum(blocks, [near[3], query_here, out_here])
 
-    with jax.named_scope("gather_states"):
-        (carried,) = join(
-            [carried[None]], [(0, 0, 0, 0, 1)], [(1, *carried.shape)], [merged[1]]
-        )
-        arrived = [shift(carried, groups, FIRST, by) for by in HOPS[1:]]
-
     with jax.named_scope("gather_rows"):
         (same,) = join(
             near,
@@ -548,6 +521,12 @@
             [merged[1]],
         )
         other = lax.ppermute(same, "group", [(g, g ^ 1) for g in range(groups)])
+
+    with jax.named_scope("gather_states"):
+        (carried,) = join(
+            [carried[None]], [(0, 0, 0, 0, 1)], [(1, *carried.shape)], [other]
+        )
+        arrived = [shift(carried, groups, FIRST, by) for by in HOPS[1:]]
 
     with jax.named_scope("contract"):
         merged = [part[None] for part in spread(merged, SECOND)]
@@ -584,7 +563,7 @@
         branch = attend(tile_source, tile_count, row_request, query, *halves, out_here)
 
     with jax.named_scope("mix"):
-        branch = first_sum(branch)
+        branch = sum_blocks(spread(branch, FIRST))
         return mix(attn_gate, states, spread(branch, SECOND))
 
 

time: 135 us -> 132 us (0.978)
  waiting for transfers between devices: 68.6 us -> 61.3 us
  starting transfers between devices: 41.9 us -> 46.8 us
    ppermute x27 -> x26, waiting for transfers between devices: 50.3 us -> 43.7 us  [shift(): return lax.ppermute(value, EVERY, pairs)]
    ppermute x27 -> x26, starting transfers between devices: 34.1 us -> 37.1 us  [shift(): return lax.ppermute(value, EVERY, pairs)]
    ppermute x2, starting transfers between devices: 5.41 us -> 7.35 us  [body(): halves.append(lax.ppermute(kv, EVERY, pairs))]
    ppermute x2, waiting for transfers between devices: 6.29 us -> 4.73 us  [body(): halves.append(lax.ppermute(kv, EVERY, pairs))]
    pallas_call x20 -> x18, Pallas kernels: 23.6 us -> 23.3 us  [kernel_call(): pl.pallas_call(kernel, in_specs=specs, out_specs=jax.tree.map(lambda _: I...]
  transfers between devices with their start and end apart: 33 -> 32, of which waited for: 22 -> 24; matrix products, arithmetic and copies ran while one was open for 0% -> 0% of each run, Pallas kernels for 13% -> 12%
where the time goes in v7:
time: 132 us
  waiting for transfers between devices  61.3 us (46%)
  starting transfers between devices  46.8 us (35%)
  Pallas kernels  23.3 us (18%)
    ppermute x26, waiting for transfers between devices, shift(): return lax.ppermute(value, EVERY, pairs)  43.7 us
    ppermute x26, starting transfers between devices, shift(): return lax.ppermute(value, EVERY, pairs)  37.1 us
    pallas_call x18, Pallas kernels, kernel_call(): pl.pallas_call(kernel, in_specs=specs, out_specs=jax.tree.map(lambda _: I...  23.3 us
    ppermute x3, waiting for transfers between devices, around(): lax.ppermute(block, 'group', [(g, (g + 2 * by) % groups) for g in range(g...  12.1 us
    ppermute x2, starting transfers between devices, body(): halves.append(lax.ppermute(kv, EVERY, pairs))  7.35 us
    ppermute x2, waiting for transfers between devices, body(): halves.append(lax.ppermute(kv, EVERY, pairs))  4.73 us
  transfers between devices with their start and end apart: 32, of which 24 were waited for; matrix products, arithmetic and copies ran while one was open for 0% of the time, Pallas kernels for 12%

profile of v7, /device:TPU:30, one launch (start us, length us, event | category | flops | bytes accessed | tf_op | source)
XLA Modules:
  0.0 132.3 jit_solution(3219350195735093950)
XLA Ops:
  0.0 2.6 %contract.5 = (bf16[2,480,256]{2,1,0:T(8,128)(2,1)S(1)}, bf16[2,480,256]{2,1,0:T(8,128)(2,1)S(1)}, bf16[144,512]{1,0:T(8,128)(2,1)S(1)}, bf16[1,16,32,480]{3,2,1,0:T(8,128)(2,1)S(1)}) custom-call(bf16[4,4,480,512]{3,2,1,0:T(8,128)(2,1)} %bitcast.21, bf16[2,512,1024]{2,1,0:T(8,128)(2,1)} %kv_weight_ref.3, bf16[2,64,512]{2,1,0:T(8,128)(2,1)} %local_ref.1, ...), custom_call_target="tpu_custom_call" | custom-call | flops 503316480 | bytes 4194304 | tf_op jit(solution)/shard_map/contract/pallas_call | solution.py:52
  5.0 5.4 %contract.6 = (bf16[4,480,256]{2,1,0:T(8,128)(2,1)S(1)}, bf16[4,480,256]{2,1,0:T(8,128)(2,1)S(1)}, bf16[4,480,256]{2,1,0:T(8,128)(2,1)S(1)}, f32[16,256]{1,0:T(8,128)S(1)}) custom-call(bf16[4,4,480,512]{3,2,1,0:T(8,128)(2,1)} %bitcast.22, bf16[2,512,1024]{2,1,0:T(8,128)(2,1)} %kv_weight_ref.3, bf16[512]{0:T(512)(128)(2,1)S(1)} %copy-done.2, ...), custom_call_target="tpu_custom_call" | custom-call | flops 1509949440 | bytes 10485760 | tf_op jit(solution)/shard_map/contract/pallas_call | solution.py:52
  15.6 3.3 %collective-permute-done.refs_1_ = bf16[1,16,32,480]{3,2,1,0:T(8,128)(2,1)S(1)} collective-permute-done((bf16[1,16,32,480]{3,2,1,0:T(8,128)(2,1)S(1)}, bf16[1,16,32,480]{3,2,1,0:T(8,128)(2,1)S(1)}, u32[]{:S(2)}, u32[]{:S(2)}) %collective-permute-start) | collective-permute-done | bytes 491552 | tf_op jit(solution)/shard_map/gather_rows/ppermute | solution.py:492
  20.9 5.8 %load.1 = (bf16[8192,512]{1,0:T(8,128)(2,1)S(1)}, bf16[512,8192]{1,0:T(8,128)(2,1)S(1)}) custom-call(bf16[8192,512]{1,0:T(8,128)(2,1)} %refs_0_.1, bf16[512,8192]{1,0:T(8,128)(2,1)} %refs_1_.1, bf16[144,512]{1,0:T(8,128)(2,1)S(1)} %get-tuple-element.40.refs_2_), custom_call_target="tpu_custom_call" | custom-call | bytes 33554432 | tf_op jit(solution)/shard_map/load/pallas_call | solution.py:52
  26.7 6.8 %collective-permute-done.2.refs_3_ = bf16[1,16,32,480]{3,2,1,0:T(8,128)(2,1)S(1)} collective-permute-done((bf16[1,16,32,480]{3,2,1,0:T(8,128)(2,1)S(1)}, bf16[1,16,32,480]{3,2,1,0:T(8,128)(2,1)S(1)}, u32[]{:S(2)}, u32[]{:S(2)}) %collective-permute-start.2) | collective-permute-done | bytes 491552 | tf_op jit(solution)/shard_map/gather_rows/ppermute | solution.py:492
  36.2 3.2 %collective-permute-start.12 = (bf16[480,256]{1,0:T(8,128)(2,1)S(1)}, bf16[480,256]{1,0:T(8,128)(2,1)S(1)}, u32[]{:S(2)}, u32[]{:S(2)}) collective-permute-start(bf16[480,256]{1,0:T(8,128)(2,1)S(1)} %get-tuple-element.53), channel_id=1, source_target_pairs={{0,12},{1,13},{2,14},{3,15},{4,0},{5,1},{6,2},{7,3},{8,4},{9,5},{1... | collective-permute-start | bytes 737288 | tf_op jit(solution)/shard_map/contract/ppermute | solution.py:40
  44.1 4.8 %collective-permute-done.12 = bf16[480,256]{1,0:T(8,128)(2,1)S(1)} collective-permute-done((bf16[480,256]{1,0:T(8,128)(2,1)S(1)}, bf16[480,256]{1,0:T(8,128)(2,1)S(1)}, u32[]{:S(2)}, u32[]{:S(2)}) %collective-permute-start.12) | collective-permute-done | bytes 245792 | tf_op jit(solution)/shard_map/contract/ppermute | solution.py:40
  53.8 3.1 %collective-permute-start.15 = (bf16[4,144,512]{2,1,0:T(8,128)(2,1)S(1)}, bf16[4,144,512]{2,1,0:T(8,128)(2,1)S(1)}, u32[]{:S(2)}, u32[]{:S(2)}) collective-permute-start(bf16[4,144,512]{2,1,0:T(8,128)(2,1)S(1)} %gather_states.3.refs_0_), channel_id=1, source_target_pairs={{0,12},{1,13},{2,14},{3,15},{4,0},{5,1},{6,2},{7,3},{8,4},{9,5},{1... | collective-permute-start | bytes 1769480 | tf_op jit(solution)/shard_map/gather_states/ppermute | solution.py:40
  61.1 3.6 %collective-permute-start.16 = (bf16[4,144,512]{2,1,0:T(8,128)(2,1)S(1)}, bf16[4,144,512]{2,1,0:T(8,128)(2,1)S(1)}, u32[]{:S(2)}, u32[]{:S(2)}) collective-permute-start(bf16[4,144,512]{2,1,0:T(8,128)(2,1)S(1)} %gather_states.3.refs_0_), channel_id=1, source_target_pairs={{0,8},{1,9},{2,10},{3,11},{4,12},{5,13},{6,14},{7,15},{8,0},{9,1},... | collective-permute-start | bytes 1769480 | tf_op jit(solution)/shard_map/gather_states/ppermute | solution.py:40
  64.7 2.8 %collective-permute-done.14.refs_1_.refs_3_ = bf16[4,144,512]{2,1,0:T(8,128)(2,1)S(1)} collective-permute-done((bf16[4,144,512]{2,1,0:T(8,128)(2,1)S(1)}, bf16[4,144,512]{2,1,0:T(8,128)(2,1)S(1)}, u32[]{:S(2)}, u32[]{:S(2)}) %collective-permute-start.14) | collective-permute-done | bytes 589856 | tf_op jit(solution)/shard_map/gather_states/ppermute | solution.py:40
  67.6 6.4 %collective-permute-done.19.refs_1_ = bf16[4,256,256]{2,1,0:T(8,128)(2,1)S(1)} collective-permute-done((bf16[4,256,256]{2,1,0:T(8,128)(2,1)S(1)}, bf16[4,256,256]{2,1,0:T(8,128)(2,1)S(1)}, u32[]{:S(2)}, u32[]{:S(2)}) %collective-permute-start.19) | collective-permute-done | bytes 524320 | tf_op jit(solution)/shard_map/kv/ppermute | solution.py:40
  74.0 3.0 %collective-permute-done.20.refs_2_ = bf16[4,256,256]{2,1,0:T(8,128)(2,1)S(1)} collective-permute-done((bf16[4,256,256]{2,1,0:T(8,128)(2,1)S(1)}, bf16[4,256,256]{2,1,0:T(8,128)(2,1)S(1)}, u32[]{:S(2)}, u32[]{:S(2)}) %collective-permute-start.20) | collective-permute-done | bytes 524320 | tf_op jit(solution)/shard_map/kv/ppermute | solution.py:40
  77.2 2.5 %collective-permute-start.23 = (bf16[256,256]{1,0:T(8,128)(2,1)S(1)}, bf16[256,256]{1,0:T(8,128)(2,1)S(1)}, u32[]{:S(2)}, u32[]{:S(2)}) collective-permute-start(bf16[256,256]{1,0:T(8,128)(2,1)S(1)} %get-tuple-element.66), channel_id=1, source_target_pairs={{0,8},{1,9},{2,10},{3,11},{4,12},{5,13},{6,14},{7,15},{8,0},{9,1},... | collective-permute-start | bytes 393224 | tf_op jit(solution)/shard_map/kv/ppermute | solution.py:40
  86.2 2.6 %collective-permute-start.24 = (bf16[256,256]{1,0:T(8,128)(2,1)S(1)}, bf16[256,256]{1,0:T(8,128)(2,1)S(1)}, u32[]{:S(2)}, u32[]{:S(2)}) collective-permute-start(bf16[256,256]{1,0:T(8,128)(2,1)S(1)} %kv.11), channel_id=1, source_target_pairs={{0,0},{1,1},{2,16},{3,17},{4,32},{5,33},{6,48},{7,49},{8,64},{9,65... | collective-permute-start | bytes 393224 | tf_op jit(solution)/shard_map/kv/ppermute | solution.py:560
  88.8 4.7 %collective-permute-start.25 = (bf16[256,256]{1,0:T(8,128)(2,1)S(1)}, bf16[256,256]{1,0:T(8,128)(2,1)S(1)}, u32[]{:S(2)}, u32[]{:S(2)}) collective-permute-start(bf16[256,256]{1,0:T(8,128)(2,1)S(1)} %kv.11), channel_id=1, source_target_pairs={{0,1},{1,0},{2,17},{3,16},{4,33},{5,32},{6,49},{7,48},{8,65},{9,64... | collective-permute-start | bytes 393224 | tf_op jit(solution)/shard_map/kv/ppermute | solution.py:560
  95.2 3.4 %collective-permute-done.24.own_ref = bf16[256,256]{1,0:T(8,128)(2,1)S(1)} collective-permute-done((bf16[256,256]{1,0:T(8,128)(2,1)S(1)}, bf16[256,256]{1,0:T(8,128)(2,1)S(1)}, u32[]{:S(2)}, u32[]{:S(2)}) %collective-permute-start.24) | collective-permute-done | bytes 131104 | tf_op jit(solution)/shard_map/kv/ppermute | solution.py:560
  100.0 3.0 %attend.1 = (bf16[4,128,512]{2,1,0:T(8,128)(2,1)S(1)}, bf16[4,128,512]{2,1,0:T(8,128)(2,1)S(1)}, bf16[4,128,512]{2,1,0:T(8,128)(2,1)S(1)}, bf16[4,128,512]{2,1,0:T(8,128)(2,1)S(1)}) custom-call(s32[8,16]{1,0:T(8,128)S(1)} %copy-done.1, s32[32]{0:T(128)S(1)} %copy-done.3, s32[1,64]{1,0:T(1,128)S(1)} %copy-done.4, bf16[128,512]{1,0:T(8,128)(2,1)S(1)} %kv.7.query_ref, ...), custom_call_target="tpu_custom_call" | custom-call | flops 1073741824 | bytes 12582912 | tf_op jit(solution)/shard_map/attend/pallas_call | solution.py:52
  105.1 3.6 %collective-permute-start.28 = (bf16[4,128,512]{2,1,0:T(8,128)(2,1)S(1)}, bf16[4,128,512]{2,1,0:T(8,128)(2,1)S(1)}, u32[]{:S(2)}, u32[]{:S(2)}) collective-permute-start(bf16[4,128,512]{2,1,0:T(8,128)(2,1)S(1)} %get-tuple-element.70), channel_id=1, source_target_pairs={{0,2},{1,3},{2,0},{3,1},{4,6},{5,7},{6,4},{7,5},{8,10},{9,11},{10,... | collective-permute-start | bytes 1572872 | tf_op jit(solution)/shard_map/mix/ppermute | solution.py:40
  108.7 3.6 %collective-permute-done.26.refs_1_ = bf16[4,128,512]{2,1,0:T(8,128)(2,1)S(1)} collective-permute-done((bf16[4,128,512]{2,1,0:T(8,128)(2,1)S(1)}, bf16[4,128,512]{2,1,0:T(8,128)(2,1)S(1)}, u32[]{:S(2)}, u32[]{:S(2)}) %collective-permute-start.26) | collective-permute-done | bytes 524320 | tf_op jit(solution)/shard_map/mix/ppermute | solution.py:40
  112.3 2.1 %collective-permute-done.27.refs_2_ = bf16[4,128,512]{2,1,0:T(8,128)(2,1)S(1)} collective-permute-done((bf16[4,128,512]{2,1,0:T(8,128)(2,1)S(1)}, bf16[4,128,512]{2,1,0:T(8,128)(2,1)S(1)}, u32[]{:S(2)}, u32[]{:S(2)}) %collective-permute-start.27) | collective-permute-done | bytes 524320 | tf_op jit(solution)/shard_map/mix/ppermute | solution.py:40
  114.4 7.1 %collective-permute-done.28.refs_3_ = bf16[4,128,512]{2,1,0:T(8,128)(2,1)S(1)} collective-permute-done((bf16[4,128,512]{2,1,0:T(8,128)(2,1)S(1)}, bf16[4,128,512]{2,1,0:T(8,128)(2,1)S(1)}, u32[]{:S(2)}, u32[]{:S(2)}) %collective-permute-start.28) | collective-permute-done | bytes 524320 | tf_op jit(solution)/shard_map/mix/ppermute | solution.py:40
  121.8 3.2 %collective-permute-start.30 = (bf16[128,512]{1,0:T(8,128)(2,1)S(1)}, bf16[128,512]{1,0:T(8,128)(2,1)S(1)}, u32[]{:S(2)}, u32[]{:S(2)}) collective-permute-start(bf16[128,512]{1,0:T(8,128)(2,1)S(1)} %get-tuple-element.73), channel_id=1, source_target_pairs={{0,12},{1,13},{2,14},{3,15},{4,0},{5,1},{6,2},{7,3},{8,4},{9,5},{1... | collective-permute-start | bytes 393224 | tf_op jit(solution)/shard_map/mix/ppermute | solution.py:40
  125.7 2.3 %collective-permute-done.29.refs_1_ = bf16[128,512]{1,0:T(8,128)(2,1)S(1)} collective-permute-done((bf16[128,512]{1,0:T(8,128)(2,1)S(1)}, bf16[128,512]{1,0:T(8,128)(2,1)S(1)}, u32[]{:S(2)}, u32[]{:S(2)}) %collective-permute-start.29) | collective-permute-done | bytes 131104 | tf_op jit(solution)/shard_map/mix/ppermute | solution.py:40
  129.0 2.5 %collective-permute-done.31.refs_3_ = bf16[128,512]{1,0:T(8,128)(2,1)S(1)} collective-permute-done((bf16[128,512]{1,0:T(8,128)(2,1)S(1)}, bf16[128,512]{1,0:T(8,128)(2,1)S(1)}, u32[]{:S(2)}, u32[]{:S(2)}) %collective-permute-start.31) | collective-permute-done | bytes 131104 | tf_op jit(solution)/shard_map/mix/ppermute | solution.py:40
  (68 shorter events, 39.9 us)
Async XLA Ops:
  2.6 8.9 %collective-permute-start.3 = (bf16[2,480,256]{2,1,0:T(8,128)(2,1)S(1)}, bf16[2,480,256]{2,1,0:T(8,128)(2,1)S(1)}, u32[]{:S(2)}, u32[]{:S(2)}) collective-permute-start(bf16[2,480,256]{2,1,0:T(8,128)(2,1)S(1)} %get-tuple-element.42._), channel_id=1, source_target_pairs={{0,1},{1,2},{2,3},{3,0},{4,5},{5,6},{6,7},{7,4},{8,9},{9,10},{10,1... | collective-permute-start | bytes 1474568 | tf_op jit(solution)/shard_map/contract/ppermute | solution.py:40
  3.2 10.0 %collective-permute-start.4 = (bf16[2,480,256]{2,1,0:T(8,128)(2,1)S(1)}, bf16[2,480,256]{2,1,0:T(8,128)(2,1)S(1)}, u32[]{:S(2)}, u32[]{:S(2)}) collective-permute-start(bf16[2,480,256]{2,1,0:T(8,128)(2,1)S(1)} %get-tuple-element.46), channel_id=1, source_target_pairs={{0,3},{1,0},{2,1},{3,2},{4,7},{5,4},{6,5},{7,6},{8,11},{9,8},{10,9... | collective-permute-start | bytes 1474568 | tf_op jit(solution)/shard_map/contract/ppermute | solution.py:40
  4.7 14.2 %collective-permute-start = (bf16[1,16,32,480]{3,2,1,0:T(8,128)(2,1)S(1)}, bf16[1,16,32,480]{3,2,1,0:T(8,128)(2,1)S(1)}, u32[]{:S(2)}, u32[]{:S(2)}) collective-permute-start(bf16[1,16,32,480]{3,2,1,0:T(8,128)(2,1)S(1)} %get-tuple-element.41.refs_0_), channel_id=1, source_target_pairs={{0,32},{16,48},{32,64},{48,80},{64,96},{80,112},{96,0},{112,16},{1... | collective-permute-start | bytes 1474568 | tf_op jit(solution)/shard_map/gather_rows/ppermute | solution.py:492
  13.5 20.0 %collective-permute-start.5 = (bf16[4,480,256]{2,1,0:T(8,128)(2,1)S(1)}, bf16[4,480,256]{2,1,0:T(8,128)(2,1)S(1)}, u32[]{:S(2)}, u32[]{:S(2)}) collective-permute-start(bf16[4,480,256]{2,1,0:T(8,128)(2,1)S(1)} %get-tuple-element.47), channel_id=1, source_target_pairs={{0,1},{1,2},{2,3},{3,0},{4,5},{5,6},{6,7},{7,4},{8,9},{9,10},{10,1... | collective-permute-start | bytes 2949128 | tf_op jit(solution)/shard_map/contract/ppermute | solution.py:40
  13.8 19.6 %collective-permute-start.6 = (bf16[4,480,256]{2,1,0:T(8,128)(2,1)S(1)}, bf16[4,480,256]{2,1,0:T(8,128)(2,1)S(1)}, u32[]{:S(2)}, u32[]{:S(2)}) collective-permute-start(bf16[4,480,256]{2,1,0:T(8,128)(2,1)S(1)} %get-tuple-element.48), channel_id=1, source_target_pairs={{0,3},{1,0},{2,1},{3,2},{4,7},{5,4},{6,5},{7,6},{8,11},{9,8},{10,9... | collective-permute-start | bytes 2949128 | tf_op jit(solution)/shard_map/contract/ppermute | solution.py:40
  18.9 14.6 %collective-permute-start.2 = (bf16[1,16,32,480]{3,2,1,0:T(8,128)(2,1)S(1)}, bf16[1,16,32,480]{3,2,1,0:T(8,128)(2,1)S(1)}, u32[]{:S(2)}, u32[]{:S(2)}) collective-permute-start(bf16[1,16,32,480]{3,2,1,0:T(8,128)(2,1)S(1)} %collective-permute-done.refs_1_), channel_id=1, source_target_pairs={{0,32},{16,48},{32,64},{48,80},{64,96},{80,112},{96,0},{112,16},{1... | collective-permute-start | bytes 1474568 | tf_op jit(solution)/shard_map/gather_rows/ppermute | solution.py:492
  20.3 15.6 %collective-permute-start.1 = (bf16[1,16,32,480]{3,2,1,0:T(8,128)(2,1)S(1)}, bf16[1,16,32,480]{3,2,1,0:T(8,128)(2,1)S(1)}, u32[]{:S(2)}, u32[]{:S(2)}) collective-permute-start(bf16[1,16,32,480]{3,2,1,0:T(8,128)(2,1)S(1)} %get-tuple-element.41.refs_0_), channel_id=1, source_target_pairs={{0,96},{16,112},{32,0},{48,16},{64,32},{80,48},{96,64},{112,80},{1... | collective-permute-start | bytes 1474568 | tf_op jit(solution)/shard_map/gather_rows/ppermute | solution.py:492
  36.1 7.6 %collective-permute-start.11 = (bf16[480,256]{1,0:T(8,128)(2,1)S(1)}, bf16[480,256]{1,0:T(8,128)(2,1)S(1)}, u32[]{:S(2)}, u32[]{:S(2)}) collective-permute-start(bf16[480,256]{1,0:T(8,128)(2,1)S(1)} %get-tuple-element.51.refs_4_), channel_id=1, source_target_pairs={{0,4},{1,5},{2,6},{3,7},{4,8},{5,9},{6,10},{7,11},{8,12},{9,13},{1... | collective-permute-start | bytes 737288 | tf_op jit(solution)/shard_map/contract/ppermute | solution.py:40
  36.2 12.7 %collective-permute-start.12 = (bf16[480,256]{1,0:T(8,128)(2,1)S(1)}, bf16[480,256]{1,0:T(8,128)(2,1)S(1)}, u32[]{:S(2)}, u32[]{:S(2)}) collective-permute-start(bf16[480,256]{1,0:T(8,128)(2,1)S(1)} %get-tuple-element.53), channel_id=1, source_target_pairs={{0,12},{1,13},{2,14},{3,15},{4,0},{5,1},{6,2},{7,3},{8,4},{9,5},{1... | collective-permute-start | bytes 737288 | tf_op jit(solution)/shard_map/contract/ppermute | solution.py:40
  39.4 10.1 %collective-permute-start.13 = (bf16[480,256]{1,0:T(8,128)(2,1)S(1)}, bf16[480,256]{1,0:T(8,128)(2,1)S(1)}, u32[]{:S(2)}, u32[]{:S(2)}) collective-permute-start(bf16[480,256]{1,0:T(8,128)(2,1)S(1)} %get-tuple-element.54), channel_id=1, source_target_pairs={{0,8},{1,9},{2,10},{3,11},{4,12},{5,13},{6,14},{7,15},{8,0},{9,1},... | collective-permute-start | bytes 737288 | tf_op jit(solution)/shard_map/contract/ppermute | solution.py:40
  40.4 9.1 %collective-permute-start.10 = (bf16[1,144,512]{2,1,0:T(8,128)(2,1)S(1)}, bf16[1,144,512]{2,1,0:T(8,128)(2,1)S(1)}, u32[]{:S(2)}, u32[]{:S(2)}) collective-permute-start(bf16[1,144,512]{2,1,0:T(8,128)(2,1)S(1)} %gather_states.2.refs_0_), channel_id=1, source_target_pairs={{0,2},{1,3},{2,0},{3,1},{4,6},{5,7},{6,4},{7,5},{8,10},{9,11},{10,... | collective-permute-start | bytes 442376 | tf_op jit(solution)/shard_map/gather_states/ppermute | solution.py:40
  41.6 7.9 %collective-permute-start.8 = (bf16[1,144,512]{2,1,0:T(8,128)(2,1)S(1)}, bf16[1,144,512]{2,1,0:T(8,128)(2,1)S(1)}, u32[]{:S(2)}, u32[]{:S(2)}) collective-permute-start(bf16[1,144,512]{2,1,0:T(8,128)(2,1)S(1)} %gather_states.2.refs_0_), channel_id=1, source_target_pairs={{0,1},{1,2},{2,3},{3,0},{4,5},{5,6},{6,7},{7,4},{8,9},{9,10},{10,1... | collective-permute-start | bytes 442376 | tf_op jit(solution)/shard_map/gather_states/ppermute | solution.py:40
  50.7 7.2 %collective-permute-start.17 = (bf16[2,256,256]{2,1,0:T(8,128)(2,1)S(1)}, bf16[2,256,256]{2,1,0:T(8,128)(2,1)S(1)}, u32[]{:S(2)}, u32[]{:S(2)}) collective-permute-start(bf16[2,256,256]{2,1,0:T(8,128)(2,1)S(1)} %get-tuple-element.56.refs_4_.refs_0_), channel_id=1, source_target_pairs={{0,1},{1,2},{2,3},{3,0},{4,5},{5,6},{6,7},{7,4},{8,9},{9,10},{10,1... | collective-permute-start | bytes 786440 | tf_op jit(solution)/shard_map/kv/ppermute | solution.py:40
  51.1 7.6 %collective-permute-start.18 = (bf16[2,256,256]{2,1,0:T(8,128)(2,1)S(1)}, bf16[2,256,256]{2,1,0:T(8,128)(2,1)S(1)}, u32[]{:S(2)}, u32[]{:S(2)}) collective-permute-start(bf16[2,256,256]{2,1,0:T(8,128)(2,1)S(1)} %get-tuple-element.60), channel_id=1, source_target_pairs={{0,3},{1,0},{2,1},{3,2},{4,7},{5,4},{6,5},{7,6},{8,11},{9,8},{10,9... | collective-permute-start | bytes 786440 | tf_op jit(solution)/shard_map/kv/ppermute | solution.py:40
  53.5 14.0 %collective-permute-start.14 = (bf16[4,144,512]{2,1,0:T(8,128)(2,1)S(1)}, bf16[4,144,512]{2,1,0:T(8,128)(2,1)S(1)}, u32[]{:S(2)}, u32[]{:S(2)}) collective-permute-start(bf16[4,144,512]{2,1,0:T(8,128)(2,1)S(1)} %gather_states.3.refs_0_), channel_id=1, source_target_pairs={{0,4},{1,5},{2,6},{3,7},{4,8},{5,9},{6,10},{7,11},{8,12},{9,13},{1... | collective-permute-start | bytes 1769480 | tf_op jit(solution)/shard_map/gather_states/ppermute | solution.py:40
  53.8 13.8 %collective-permute-start.15 = (bf16[4,144,512]{2,1,0:T(8,128)(2,1)S(1)}, bf16[4,144,512]{2,1,0:T(8,128)(2,1)S(1)}, u32[]{:S(2)}, u32[]{:S(2)}) collective-permute-start(bf16[4,144,512]{2,1,0:T(8,128)(2,1)S(1)} %gather_states.3.refs_0_), channel_id=1, source_target_pairs={{0,12},{1,13},{2,14},{3,15},{4,0},{5,1},{6,2},{7,3},{8,4},{9,5},{1... | collective-permute-start | bytes 1769480 | tf_op jit(solution)/shard_map/gather_states/ppermute | solution.py:40
  58.8 15.1 %collective-permute-start.19 = (bf16[4,256,256]{2,1,0:T(8,128)(2,1)S(1)}, bf16[4,256,256]{2,1,0:T(8,128)(2,1)S(1)}, u32[]{:S(2)}, u32[]{:S(2)}) collective-permute-start(bf16[4,256,256]{2,1,0:T(8,128)(2,1)S(1)} %get-tuple-element.61), channel_id=1, source_target_pairs={{0,1},{1,2},{2,3},{3,0},{4,5},{5,6},{6,7},{7,4},{8,9},{9,10},{10,1... | collective-permute-start | bytes 1572872 | tf_op jit(solution)/shard_map/kv/ppermute | solution.py:40
  59.9 17.1 %collective-permute-start.20 = (bf16[4,256,256]{2,1,0:T(8,128)(2,1)S(1)}, bf16[4,256,256]{2,1,0:T(8,128)(2,1)S(1)}, u32[]{:S(2)}, u32[]{:S(2)}) collective-permute-start(bf16[4,256,256]{2,1,0:T(8,128)(2,1)S(1)} %get-tuple-element.62), channel_id=1, source_target_pairs={{0,3},{1,0},{2,1},{3,2},{4,7},{5,4},{6,5},{7,6},{8,11},{9,8},{10,9... | collective-permute-start | bytes 1572872 | tf_op jit(solution)/shard_map/kv/ppermute | solution.py:40
  61.1 32.4 %collective-permute-start.16 = (bf16[4,144,512]{2,1,0:T(8,128)(2,1)S(1)}, bf16[4,144,512]{2,1,0:T(8,128)(2,1)S(1)}, u32[]{:S(2)}, u32[]{:S(2)}) collective-permute-start(bf16[4,144,512]{2,1,0:T(8,128)(2,1)S(1)} %gather_states.3.refs_0_), channel_id=1, source_target_pairs={{0,8},{1,9},{2,10},{3,11},{4,12},{5,13},{6,14},{7,15},{8,0},{9,1},... | collective-permute-start | bytes 1769480 | tf_op jit(solution)/shard_map/gather_states/ppermute | solution.py:40
  86.2 12.5 %collective-permute-start.24 = (bf16[256,256]{1,0:T(8,128)(2,1)S(1)}, bf16[256,256]{1,0:T(8,128)(2,1)S(1)}, u32[]{:S(2)}, u32[]{:S(2)}) collective-permute-start(bf16[256,256]{1,0:T(8,128)(2,1)S(1)} %kv.11), channel_id=1, source_target_pairs={{0,0},{1,1},{2,16},{3,17},{4,32},{5,33},{6,48},{7,49},{8,64},{9,65... | collective-permute-start | bytes 393224 | tf_op jit(solution)/shard_map/kv/ppermute | solution.py:560
  88.8 11.2 %collective-permute-start.25 = (bf16[256,256]{1,0:T(8,128)(2,1)S(1)}, bf16[256,256]{1,0:T(8,128)(2,1)S(1)}, u32[]{:S(2)}, u32[]{:S(2)}) collective-permute-start(bf16[256,256]{1,0:T(8,128)(2,1)S(1)} %kv.11), channel_id=1, source_target_pairs={{0,1},{1,0},{2,17},{3,16},{4,33},{5,32},{6,49},{7,48},{8,65},{9,64... | collective-permute-start | bytes 393224 | tf_op jit(solution)/shard_map/kv/ppermute | solution.py:560
  103.0 9.2 %collective-permute-start.26 = (bf16[4,128,512]{2,1,0:T(8,128)(2,1)S(1)}, bf16[4,128,512]{2,1,0:T(8,128)(2,1)S(1)}, u32[]{:S(2)}, u32[]{:S(2)}) collective-permute-start(bf16[4,128,512]{2,1,0:T(8,128)(2,1)S(1)} %get-tuple-element.68), channel_id=1, source_target_pairs={{0,1},{1,2},{2,3},{3,0},{4,5},{5,6},{6,7},{7,4},{8,9},{9,10},{10,1... | collective-permute-start | bytes 1572872 | tf_op jit(solution)/shard_map/mix/ppermute | solution.py:40
  103.5 10.9 %collective-permute-start.27 = (bf16[4,128,512]{2,1,0:T(8,128)(2,1)S(1)}, bf16[4,128,512]{2,1,0:T(8,128)(2,1)S(1)}, u32[]{:S(2)}, u32[]{:S(2)}) collective-permute-start(bf16[4,128,512]{2,1,0:T(8,128)(2,1)S(1)} %get-tuple-element.69), channel_id=1, source_target_pairs={{0,3},{1,0},{2,1},{3,2},{4,7},{5,4},{6,5},{7,6},{8,11},{9,8},{10,9... | collective-permute-start | bytes 1572872 | tf_op jit(solution)/shard_map/mix/ppermute | solution.py:40
  105.1 16.3 %collective-permute-start.28 = (bf16[4,128,512]{2,1,0:T(8,128)(2,1)S(1)}, bf16[4,128,512]{2,1,0:T(8,128)(2,1)S(1)}, u32[]{:S(2)}, u32[]{:S(2)}) collective-permute-start(bf16[4,128,512]{2,1,0:T(8,128)(2,1)S(1)} %get-tuple-element.70), channel_id=1, source_target_pairs={{0,2},{1,3},{2,0},{3,1},{4,6},{5,7},{6,4},{7,5},{8,10},{9,11},{10,... | collective-permute-start | bytes 1572872 | tf_op jit(solution)/shard_map/mix/ppermute | solution.py:40
  (13 other events, 224.8 us)

commit v8 on v7

--- a/solution.py
+++ b/solution.py
@@ -540,7 +540,6 @@
             [carried] + arrived,
             [(i, 0, 0, i, 1) for i in range(SIDE)],
             [(SIDE, *carried.shape[1:])],
-            [kv[0]],
         )
         parts = spread([states_near] * SIDE, SECOND)
 

time: 132 us -> 132 us (level)
  no operation moved by 1% of the time
where the time goes in v8:
time: 132 us
  waiting for transfers between devices  61.3 us (46%)
  starting transfers between devices  46.8 us (35%)
  Pallas kernels  23.3 us (18%)
    ppermute x26, waiting for transfers between devices, shift(): return lax.ppermute(value, EVERY, pairs)  43.7 us
    ppermute x26, starting transfers between devices, shift(): return lax.ppermute(value, EVERY, pairs)  37.1 us
    pallas_call x18, Pallas kernels, kernel_call(): pl.pallas_call(kernel, in_specs=specs, out_specs=jax.tree.map(lambda _: I...  23.3 us
    ppermute x3, waiting for transfers between devices, around(): lax.ppermute(block, 'group', [(g, (g + 2 * by) % groups) for g in range(g...  12.1 us
    ppermute x2, starting transfers between devices, body(): halves.append(lax.ppermute(kv, EVERY, pairs))  7.35 us
    ppermute x2, waiting for transfers between devices, body(): halves.append(lax.ppermute(kv, EVERY, pairs))  4.73 us
  transfers between devices with their start and end apart: 32, of which 24 were waited for; matrix products, arithmetic and copies ran while one was open for 0% of the time, Pallas kernels for 12%

profile of v8, /device:TPU:30, one launch (start us, length us, event | category | flops | bytes accessed | tf_op | source)
XLA Modules:
  0.0 132.3 jit_solution(16538644106849469995)
XLA Ops:
  0.0 2.6 %contract.5 = (bf16[2,480,256]{2,1,0:T(8,128)(2,1)S(1)}, bf16[2,480,256]{2,1,0:T(8,128)(2,1)S(1)}, bf16[144,512]{1,0:T(8,128)(2,1)S(1)}, bf16[1,16,32,480]{3,2,1,0:T(8,128)(2,1)S(1)}) custom-call(bf16[4,4,480,512]{3,2,1,0:T(8,128)(2,1)} %bitcast.21, bf16[2,512,1024]{2,1,0:T(8,128)(2,1)} %kv_weight_ref.3, bf16[2,64,512]{2,1,0:T(8,128)(2,1)} %local_ref.1, ...), custom_call_target="tpu_custom_call" | custom-call | flops 503316480 | bytes 4194304 | tf_op jit(solution)/shard_map/contract/pallas_call | solution.py:52
  5.0 5.4 %contract.6 = (bf16[4,480,256]{2,1,0:T(8,128)(2,1)S(1)}, bf16[4,480,256]{2,1,0:T(8,128)(2,1)S(1)}, bf16[4,480,256]{2,1,0:T(8,128)(2,1)S(1)}, f32[16,256]{1,0:T(8,128)S(1)}) custom-call(bf16[4,4,480,512]{3,2,1,0:T(8,128)(2,1)} %bitcast.22, bf16[2,512,1024]{2,1,0:T(8,128)(2,1)} %kv_weight_ref.3, bf16[512]{0:T(512)(128)(2,1)S(1)} %copy-done.2, ...), custom_call_target="tpu_custom_call" | custom-call | flops 1509949440 | bytes 10485760 | tf_op jit(solution)/shard_map/contract/pallas_call | solution.py:52
  15.6 3.3 %collective-permute-done.refs_1_ = bf16[1,16,32,480]{3,2,1,0:T(8,128)(2,1)S(1)} collective-permute-done((bf16[1,16,32,480]{3,2,1,0:T(8,128)(2,1)S(1)}, bf16[1,16,32,480]{3,2,1,0:T(8,128)(2,1)S(1)}, u32[]{:S(2)}, u32[]{:S(2)}) %collective-permute-start) | collective-permute-done | bytes 491552 | tf_op jit(solution)/shard_map/gather_rows/ppermute | solution.py:492
  20.9 5.8 %load.1 = (bf16[8192,512]{1,0:T(8,128)(2,1)S(1)}, bf16[512,8192]{1,0:T(8,128)(2,1)S(1)}) custom-call(bf16[8192,512]{1,0:T(8,128)(2,1)} %refs_0_.1, bf16[512,8192]{1,0:T(8,128)(2,1)} %refs_1_.1, bf16[144,512]{1,0:T(8,128)(2,1)S(1)} %get-tuple-element.40.refs_2_), custom_call_target="tpu_custom_call" | custom-call | bytes 33554432 | tf_op jit(solution)/shard_map/load/pallas_call | solution.py:52
  26.7 6.8 %collective-permute-done.2.refs_3_ = bf16[1,16,32,480]{3,2,1,0:T(8,128)(2,1)S(1)} collective-permute-done((bf16[1,16,32,480]{3,2,1,0:T(8,128)(2,1)S(1)}, bf16[1,16,32,480]{3,2,1,0:T(8,128)(2,1)S(1)}, u32[]{:S(2)}, u32[]{:S(2)}) %collective-permute-start.2) | collective-permute-done | bytes 491552 | tf_op jit(solution)/shard_map/gather_rows/ppermute | solution.py:492
  36.2 3.2 %collective-permute-start.15 = (bf16[480,256]{1,0:T(8,128)(2,1)S(1)}, bf16[480,256]{1,0:T(8,128)(2,1)S(1)}, u32[]{:S(2)}, u32[]{:S(2)}) collective-permute-start(bf16[480,256]{1,0:T(8,128)(2,1)S(1)} %get-tuple-element.53), channel_id=1, source_target_pairs={{0,12},{1,13},{2,14},{3,15},{4,0},{5,1},{6,2},{7,3},{8,4},{9,5},{1... | collective-permute-start | bytes 737288 | tf_op jit(solution)/shard_map/contract/ppermute | solution.py:40
  44.1 4.8 %collective-permute-done.15 = bf16[480,256]{1,0:T(8,128)(2,1)S(1)} collective-permute-done((bf16[480,256]{1,0:T(8,128)(2,1)S(1)}, bf16[480,256]{1,0:T(8,128)(2,1)S(1)}, u32[]{:S(2)}, u32[]{:S(2)}) %collective-permute-start.15) | collective-permute-done | bytes 245792 | tf_op jit(solution)/shard_map/contract/ppermute | solution.py:40
  53.8 3.1 %collective-permute-start.12 = (bf16[4,144,512]{2,1,0:T(8,128)(2,1)S(1)}, bf16[4,144,512]{2,1,0:T(8,128)(2,1)S(1)}, u32[]{:S(2)}, u32[]{:S(2)}) collective-permute-start(bf16[4,144,512]{2,1,0:T(8,128)(2,1)S(1)} %gather_states.3.refs_0_), channel_id=1, source_target_pairs={{0,12},{1,13},{2,14},{3,15},{4,0},{5,1},{6,2},{7,3},{8,4},{9,5},{1... | collective-permute-start | bytes 1769480 | tf_op jit(solution)/shard_map/gather_states/ppermute | solution.py:40
  61.1 3.6 %collective-permute-start.13 = (bf16[4,144,512]{2,1,0:T(8,128)(2,1)S(1)}, bf16[4,144,512]{2,1,0:T(8,128)(2,1)S(1)}, u32[]{:S(2)}, u32[]{:S(2)}) collective-permute-start(bf16[4,144,512]{2,1,0:T(8,128)(2,1)S(1)} %gather_states.3.refs_0_), channel_id=1, source_target_pairs={{0,8},{1,9},{2,10},{3,11},{4,12},{5,13},{6,14},{7,15},{8,0},{9,1},... | collective-permute-start | bytes 1769480 | tf_op jit(solution)/shard_map/gather_states/ppermute | solution.py:40
  64.7 2.8 %collective-permute-done.11.refs_1_.refs_3_ = bf16[4,144,512]{2,1,0:T(8,128)(2,1)S(1)} collective-permute-done((bf16[4,144,512]{2,1,0:T(8,128)(2,1)S(1)}, bf16[4,144,512]{2,1,0:T(8,128)(2,1)S(1)}, u32[]{:S(2)}, u32[]{:S(2)}) %collective-permute-start.11) | collective-permute-done | bytes 589856 | tf_op jit(solution)/shard_map/gather_states/ppermute | solution.py:40
  67.6 6.4 %collective-permute-done.19.refs_1_ = bf16[4,256,256]{2,1,0:T(8,128)(2,1)S(1)} collective-permute-done((bf16[4,256,256]{2,1,0:T(8,128)(2,1)S(1)}, bf16[4,256,256]{2,1,0:T(8,128)(2,1)S(1)}, u32[]{:S(2)}, u32[]{:S(2)}) %collective-permute-start.19) | collective-permute-done | bytes 524320 | tf_op jit(solution)/shard_map/kv/ppermute | solution.py:40
  74.0 3.0 %collective-permute-done.20.refs_2_ = bf16[4,256,256]{2,1,0:T(8,128)(2,1)S(1)} collective-permute-done((bf16[4,256,256]{2,1,0:T(8,128)(2,1)S(1)}, bf16[4,256,256]{2,1,0:T(8,128)(2,1)S(1)}, u32[]{:S(2)}, u32[]{:S(2)}) %collective-permute-start.20) | collective-permute-done | bytes 524320 | tf_op jit(solution)/shard_map/kv/ppermute | solution.py:40
  77.2 2.5 %collective-permute-start.23 = (bf16[256,256]{1,0:T(8,128)(2,1)S(1)}, bf16[256,256]{1,0:T(8,128)(2,1)S(1)}, u32[]{:S(2)}, u32[]{:S(2)}) collective-permute-start(bf16[256,256]{1,0:T(8,128)(2,1)S(1)} %get-tuple-element.66), channel_id=1, source_target_pairs={{0,8},{1,9},{2,10},{3,11},{4,12},{5,13},{6,14},{7,15},{8,0},{9,1},... | collective-permute-start | bytes 393224 | tf_op jit(solution)/shard_map/kv/ppermute | solution.py:40
  86.2 2.6 %collective-permute-start.24 = (bf16[256,256]{1,0:T(8,128)(2,1)S(1)}, bf16[256,256]{1,0:T(8,128)(2,1)S(1)}, u32[]{:S(2)}, u32[]{:S(2)}) collective-permute-start(bf16[256,256]{1,0:T(8,128)(2,1)S(1)} %kv.11), channel_id=1, source_target_pairs={{0,0},{1,1},{2,16},{3,17},{4,32},{5,33},{6,48},{7,49},{8,64},{9,65... | collective-permute-start | bytes 393224 | tf_op jit(solution)/shard_map/kv/ppermute | solution.py:559
  88.8 4.7 %collective-permute-start.25 = (bf16[256,256]{1,0:T(8,128)(2,1)S(1)}, bf16[256,256]{1,0:T(8,128)(2,1)S(1)}, u32[]{:S(2)}, u32[]{:S(2)}) collective-permute-start(bf16[256,256]{1,0:T(8,128)(2,1)S(1)} %kv.11), channel_id=1, source_target_pairs={{0,1},{1,0},{2,17},{3,16},{4,33},{5,32},{6,49},{7,48},{8,65},{9,64... | collective-permute-start | bytes 393224 | tf_op jit(solution)/shard_map/kv/ppermute | solution.py:559
  95.2 3.4 %collective-permute-done.24.own_ref = bf16[256,256]{1,0:T(8,128)(2,1)S(1)} collective-permute-done((bf16[256,256]{1,0:T(8,128)(2,1)S(1)}, bf16[256,256]{1,0:T(8,128)(2,1)S(1)}, u32[]{:S(2)}, u32[]{:S(2)}) %collective-permute-start.24) | collective-permute-done | bytes 131104 | tf_op jit(solution)/shard_map/kv/ppermute | solution.py:559
  100.0 3.0 %attend.1 = (bf16[4,128,512]{2,1,0:T(8,128)(2,1)S(1)}, bf16[4,128,512]{2,1,0:T(8,128)(2,1)S(1)}, bf16[4,128,512]{2,1,0:T(8,128)(2,1)S(1)}, bf16[4,128,512]{2,1,0:T(8,128)(2,1)S(1)}) custom-call(s32[8,16]{1,0:T(8,128)S(1)} %copy-done.1, s32[32]{0:T(128)S(1)} %copy-done.3, s32[1,64]{1,0:T(1,128)S(1)} %copy-done.4, bf16[128,512]{1,0:T(8,128)(2,1)S(1)} %kv.6.query_ref, ...), custom_call_target="tpu_custom_call" | custom-call | flops 1073741824 | bytes 12582912 | tf_op jit(solution)/shard_map/attend/pallas_call | solution.py:52
  105.1 3.6 %collective-permute-start.28 = (bf16[4,128,512]{2,1,0:T(8,128)(2,1)S(1)}, bf16[4,128,512]{2,1,0:T(8,128)(2,1)S(1)}, u32[]{:S(2)}, u32[]{:S(2)}) collective-permute-start(bf16[4,128,512]{2,1,0:T(8,128)(2,1)S(1)} %get-tuple-element.70), channel_id=1, source_target_pairs={{0,2},{1,3},{2,0},{3,1},{4,6},{5,7},{6,4},{7,5},{8,10},{9,11},{10,... | collective-permute-start | bytes 1572872 | tf_op jit(solution)/shard_map/mix/ppermute | solution.py:40
  108.7 3.6 %collective-permute-done.26.refs_1_ = bf16[4,128,512]{2,1,0:T(8,128)(2,1)S(1)} collective-permute-done((bf16[4,128,512]{2,1,0:T(8,128)(2,1)S(1)}, bf16[4,128,512]{2,1,0:T(8,128)(2,1)S(1)}, u32[]{:S(2)}, u32[]{:S(2)}) %collective-permute-start.26) | collective-permute-done | bytes 524320 | tf_op jit(solution)/shard_map/mix/ppermute | solution.py:40
  112.3 2.1 %collective-permute-done.27.refs_2_ = bf16[4,128,512]{2,1,0:T(8,128)(2,1)S(1)} collective-permute-done((bf16[4,128,512]{2,1,0:T(8,128)(2,1)S(1)}, bf16[4,128,512]{2,1,0:T(8,128)(2,1)S(1)}, u32[]{:S(2)}, u32[]{:S(2)}) %collective-permute-start.27) | collective-permute-done | bytes 524320 | tf_op jit(solution)/shard_map/mix/ppermute | solution.py:40
  114.4 7.1 %collective-permute-done.28.refs_3_ = bf16[4,128,512]{2,1,0:T(8,128)(2,1)S(1)} collective-permute-done((bf16[4,128,512]{2,1,0:T(8,128)(2,1)S(1)}, bf16[4,128,512]{2,1,0:T(8,128)(2,1)S(1)}, u32[]{:S(2)}, u32[]{:S(2)}) %collective-permute-start.28) | collective-permute-done | bytes 524320 | tf_op jit(solution)/shard_map/mix/ppermute | solution.py:40
  121.8 3.2 %collective-permute-start.30 = (bf16[128,512]{1,0:T(8,128)(2,1)S(1)}, bf16[128,512]{1,0:T(8,128)(2,1)S(1)}, u32[]{:S(2)}, u32[]{:S(2)}) collective-permute-start(bf16[128,512]{1,0:T(8,128)(2,1)S(1)} %get-tuple-element.73), channel_id=1, source_target_pairs={{0,12},{1,13},{2,14},{3,15},{4,0},{5,1},{6,2},{7,3},{8,4},{9,5},{1... | collective-permute-start | bytes 393224 | tf_op jit(solution)/shard_map/mix/ppermute | solution.py:40
  125.7 2.3 %collective-permute-done.29.refs_1_ = bf16[128,512]{1,0:T(8,128)(2,1)S(1)} collective-permute-done((bf16[128,512]{1,0:T(8,128)(2,1)S(1)}, bf16[128,512]{1,0:T(8,128)(2,1)S(1)}, u32[]{:S(2)}, u32[]{:S(2)}) %collective-permute-start.29) | collective-permute-done | bytes 131104 | tf_op jit(solution)/shard_map/mix/ppermute | solution.py:40
  129.0 2.5 %collective-permute-done.31.refs_3_ = bf16[128,512]{1,0:T(8,128)(2,1)S(1)} collective-permute-done((bf16[128,512]{1,0:T(8,128)(2,1)S(1)}, bf16[128,512]{1,0:T(8,128)(2,1)S(1)}, u32[]{:S(2)}, u32[]{:S(2)}) %collective-permute-start.31) | collective-permute-done | bytes 131104 | tf_op jit(solution)/shard_map/mix/ppermute | solution.py:40
  (68 shorter events, 39.9 us)
Async XLA Ops:
  2.6 8.9 %collective-permute-start.3 = (bf16[2,480,256]{2,1,0:T(8,128)(2,1)S(1)}, bf16[2,480,256]{2,1,0:T(8,128)(2,1)S(1)}, u32[]{:S(2)}, u32[]{:S(2)}) collective-permute-start(bf16[2,480,256]{2,1,0:T(8,128)(2,1)S(1)} %get-tuple-element.42._), channel_id=1, source_target_pairs={{0,1},{1,2},{2,3},{3,0},{4,5},{5,6},{6,7},{7,4},{8,9},{9,10},{10,1... | collective-permute-start | bytes 1474568 | tf_op jit(solution)/shard_map/contract/ppermute | solution.py:40
  3.2 10.0 %collective-permute-start.4 = (bf16[2,480,256]{2,1,0:T(8,128)(2,1)S(1)}, bf16[2,480,256]{2,1,0:T(8,128)(2,1)S(1)}, u32[]{:S(2)}, u32[]{:S(2)}) collective-permute-start(bf16[2,480,256]{2,1,0:T(8,128)(2,1)S(1)} %get-tuple-element.46), channel_id=1, source_target_pairs={{0,3},{1,0},{2,1},{3,2},{4,7},{5,4},{6,5},{7,6},{8,11},{9,8},{10,9... | collective-permute-start | bytes 1474568 | tf_op jit(solution)/shard_map/contract/ppermute | solution.py:40
  4.7 14.2 %collective-permute-start = (bf16[1,16,32,480]{3,2,1,0:T(8,128)(2,1)S(1)}, bf16[1,16,32,480]{3,2,1,0:T(8,128)(2,1)S(1)}, u32[]{:S(2)}, u32[]{:S(2)}) collective-permute-start(bf16[1,16,32,480]{3,2,1,0:T(8,128)(2,1)S(1)} %get-tuple-element.41.refs_0_), channel_id=1, source_target_pairs={{0,32},{16,48},{32,64},{48,80},{64,96},{80,112},{96,0},{112,16},{1... | collective-permute-start | bytes 1474568 | tf_op jit(solution)/shard_map/gather_rows/ppermute | solution.py:492
  13.5 20.0 %collective-permute-start.5 = (bf16[4,480,256]{2,1,0:T(8,128)(2,1)S(1)}, bf16[4,480,256]{2,1,0:T(8,128)(2,1)S(1)}, u32[]{:S(2)}, u32[]{:S(2)}) collective-permute-start(bf16[4,480,256]{2,1,0:T(8,128)(2,1)S(1)} %get-tuple-element.47), channel_id=1, source_target_pairs={{0,1},{1,2},{2,3},{3,0},{4,5},{5,6},{6,7},{7,4},{8,9},{9,10},{10,1... | collective-permute-start | bytes 2949128 | tf_op jit(solution)/shard_map/contract/ppermute | solution.py:40
  13.8 19.6 %collective-permute-start.6 = (bf16[4,480,256]{2,1,0:T(8,128)(2,1)S(1)}, bf16[4,480,256]{2,1,0:T(8,128)(2,1)S(1)}, u32[]{:S(2)}, u32[]{:S(2)}) collective-permute-start(bf16[4,480,256]{2,1,0:T(8,128)(2,1)S(1)} %get-tuple-element.48), channel_id=1, source_target_pairs={{0,3},{1,0},{2,1},{3,2},{4,7},{5,4},{6,5},{7,6},{8,11},{9,8},{10,9... | collective-permute-start | bytes 2949128 | tf_op jit(solution)/shard_map/contract/ppermute | solution.py:40
  18.9 14.6 %collective-permute-start.2 = (bf16[1,16,32,480]{3,2,1,0:T(8,128)(2,1)S(1)}, bf16[1,16,32,480]{3,2,1,0:T(8,128)(2,1)S(1)}, u32[]{:S(2)}, u32[]{:S(2)}) collective-permute-start(bf16[1,16,32,480]{3,2,1,0:T(8,128)(2,1)S(1)} %collective-permute-done.refs_1_), channel_id=1, source_target_pairs={{0,32},{16,48},{32,64},{48,80},{64,96},{80,112},{96,0},{112,16},{1... | collective-permute-start | bytes 1474568 | tf_op jit(solution)/shard_map/gather_rows/ppermute | solution.py:492
  20.3 15.6 %collective-permute-start.1 = (bf16[1,16,32,480]{3,2,1,0:T(8,128)(2,1)S(1)}, bf16[1,16,32,480]{3,2,1,0:T(8,128)(2,1)S(1)}, u32[]{:S(2)}, u32[]{:S(2)}) collective-permute-start(bf16[1,16,32,480]{3,2,1,0:T(8,128)(2,1)S(1)} %get-tuple-element.41.refs_0_), channel_id=1, source_target_pairs={{0,96},{16,112},{32,0},{48,16},{64,32},{80,48},{96,64},{112,80},{1... | collective-permute-start | bytes 1474568 | tf_op jit(solution)/shard_map/gather_rows/ppermute | solution.py:492
  36.1 7.6 %collective-permute-start.14 = (bf16[480,256]{1,0:T(8,128)(2,1)S(1)}, bf16[480,256]{1,0:T(8,128)(2,1)S(1)}, u32[]{:S(2)}, u32[]{:S(2)}) collective-permute-start(bf16[480,256]{1,0:T(8,128)(2,1)S(1)} %get-tuple-element.51.refs_4_), channel_id=1, source_target_pairs={{0,4},{1,5},{2,6},{3,7},{4,8},{5,9},{6,10},{7,11},{8,12},{9,13},{1... | collective-permute-start | bytes 737288 | tf_op jit(solution)/shard_map/contract/ppermute | solution.py:40
  36.2 12.7 %collective-permute-start.15 = (bf16[480,256]{1,0:T(8,128)(2,1)S(1)}, bf16[480,256]{1,0:T(8,128)(2,1)S(1)}, u32[]{:S(2)}, u32[]{:S(2)}) collective-permute-start(bf16[480,256]{1,0:T(8,128)(2,1)S(1)} %get-tuple-element.53), channel_id=1, source_target_pairs={{0,12},{1,13},{2,14},{3,15},{4,0},{5,1},{6,2},{7,3},{8,4},{9,5},{1... | collective-permute-start | bytes 737288 | tf_op jit(solution)/shard_map/contract/ppermute | solution.py:40
  39.4 10.1 %collective-permute-start.16 = (bf16[480,256]{1,0:T(8,128)(2,1)S(1)}, bf16[480,256]{1,0:T(8,128)(2,1)S(1)}, u32[]{:S(2)}, u32[]{:S(2)}) collective-permute-start(bf16[480,256]{1,0:T(8,128)(2,1)S(1)} %get-tuple-element.54), channel_id=1, source_target_pairs={{0,8},{1,9},{2,10},{3,11},{4,12},{5,13},{6,14},{7,15},{8,0},{9,1},... | collective-permute-start | bytes 737288 | tf_op jit(solution)/shard_map/contract/ppermute | solution.py:40
  40.4 9.1 %collective-permute-start.10 = (bf16[1,144,512]{2,1,0:T(8,128)(2,1)S(1)}, bf16[1,144,512]{2,1,0:T(8,128)(2,1)S(1)}, u32[]{:S(2)}, u32[]{:S(2)}) collective-permute-start(bf16[1,144,512]{2,1,0:T(8,128)(2,1)S(1)} %gather_states.2.refs_0_), channel_id=1, source_target_pairs={{0,2},{1,3},{2,0},{3,1},{4,6},{5,7},{6,4},{7,5},{8,10},{9,11},{10,... | collective-permute-start | bytes 442376 | tf_op jit(solution)/shard_map/gather_states/ppermute | solution.py:40
  41.6 7.9 %collective-permute-start.8 = (bf16[1,144,512]{2,1,0:T(8,128)(2,1)S(1)}, bf16[1,144,512]{2,1,0:T(8,128)(2,1)S(1)}, u32[]{:S(2)}, u32[]{:S(2)}) collective-permute-start(bf16[1,144,512]{2,1,0:T(8,128)(2,1)S(1)} %gather_states.2.refs_0_), channel_id=1, source_target_pairs={{0,1},{1,2},{2,3},{3,0},{4,5},{5,6},{6,7},{7,4},{8,9},{9,10},{10,1... | collective-permute-start | bytes 442376 | tf_op jit(solution)/shard_map/gather_states/ppermute | solution.py:40
  50.7 7.2 %collective-permute-start.17 = (bf16[2,256,256]{2,1,0:T(8,128)(2,1)S(1)}, bf16[2,256,256]{2,1,0:T(8,128)(2,1)S(1)}, u32[]{:S(2)}, u32[]{:S(2)}) collective-permute-start(bf16[2,256,256]{2,1,0:T(8,128)(2,1)S(1)} %get-tuple-element.56.refs_0_), channel_id=1, source_target_pairs={{0,1},{1,2},{2,3},{3,0},{4,5},{5,6},{6,7},{7,4},{8,9},{9,10},{10,1... | collective-permute-start | bytes 786440 | tf_op jit(solution)/shard_map/kv/ppermute | solution.py:40
  51.1 7.6 %collective-permute-start.18 = (bf16[2,256,256]{2,1,0:T(8,128)(2,1)S(1)}, bf16[2,256,256]{2,1,0:T(8,128)(2,1)S(1)}, u32[]{:S(2)}, u32[]{:S(2)}) collective-permute-start(bf16[2,256,256]{2,1,0:T(8,128)(2,1)S(1)} %get-tuple-element.60), channel_id=1, source_target_pairs={{0,3},{1,0},{2,1},{3,2},{4,7},{5,4},{6,5},{7,6},{8,11},{9,8},{10,9... | collective-permute-start | bytes 786440 | tf_op jit(solution)/shard_map/kv/ppermute | solution.py:40
  53.5 14.0 %collective-permute-start.11 = (bf16[4,144,512]{2,1,0:T(8,128)(2,1)S(1)}, bf16[4,144,512]{2,1,0:T(8,128)(2,1)S(1)}, u32[]{:S(2)}, u32[]{:S(2)}) collective-permute-start(bf16[4,144,512]{2,1,0:T(8,128)(2,1)S(1)} %gather_states.3.refs_0_), channel_id=1, source_target_pairs={{0,4},{1,5},{2,6},{3,7},{4,8},{5,9},{6,10},{7,11},{8,12},{9,13},{1... | collective-permute-start | bytes 1769480 | tf_op jit(solution)/shard_map/gather_states/ppermute | solution.py:40
  53.8 13.8 %collective-permute-start.12 = (bf16[4,144,512]{2,1,0:T(8,128)(2,1)S(1)}, bf16[4,144,512]{2,1,0:T(8,128)(2,1)S(1)}, u32[]{:S(2)}, u32[]{:S(2)}) collective-permute-start(bf16[4,144,512]{2,1,0:T(8,128)(2,1)S(1)} %gather_states.3.refs_0_), channel_id=1, source_target_pairs={{0,12},{1,13},{2,14},{3,15},{4,0},{5,1},{6,2},{7,3},{8,4},{9,5},{1... | collective-permute-start | bytes 1769480 | tf_op jit(solution)/shard_map/gather_states/ppermute | solution.py:40
  58.8 15.1 %collective-permute-start.19 = (bf16[4,256,256]{2,1,0:T(8,128)(2,1)S(1)}, bf16[4,256,256]{2,1,0:T(8,128)(2,1)S(1)}, u32[]{:S(2)}, u32[]{:S(2)}) collective-permute-start(bf16[4,256,256]{2,1,0:T(8,128)(2,1)S(1)} %get-tuple-element.61), channel_id=1, source_target_pairs={{0,1},{1,2},{2,3},{3,0},{4,5},{5,6},{6,7},{7,4},{8,9},{9,10},{10,1... | collective-permute-start | bytes 1572872 | tf_op jit(solution)/shard_map/kv/ppermute | solution.py:40
  59.9 17.1 %collective-permute-start.20 = (bf16[4,256,256]{2,1,0:T(8,128)(2,1)S(1)}, bf16[4,256,256]{2,1,0:T(8,128)(2,1)S(1)}, u32[]{:S(2)}, u32[]{:S(2)}) collective-permute-start(bf16[4,256,256]{2,1,0:T(8,128)(2,1)S(1)} %get-tuple-element.62), channel_id=1, source_target_pairs={{0,3},{1,0},{2,1},{3,2},{4,7},{5,4},{6,5},{7,6},{8,11},{9,8},{10,9... | collective-permute-start | bytes 1572872 | tf_op jit(solution)/shard_map/kv/ppermute | solution.py:40
  61.1 32.4 %collective-permute-start.13 = (bf16[4,144,512]{2,1,0:T(8,128)(2,1)S(1)}, bf16[4,144,512]{2,1,0:T(8,128)(2,1)S(1)}, u32[]{:S(2)}, u32[]{:S(2)}) collective-permute-start(bf16[4,144,512]{2,1,0:T(8,128)(2,1)S(1)} %gather_states.3.refs_0_), channel_id=1, source_target_pairs={{0,8},{1,9},{2,10},{3,11},{4,12},{5,13},{6,14},{7,15},{8,0},{9,1},... | collective-permute-start | bytes 1769480 | tf_op jit(solution)/shard_map/gather_states/ppermute | solution.py:40
  86.2 12.5 %collective-permute-start.24 = (bf16[256,256]{1,0:T(8,128)(2,1)S(1)}, bf16[256,256]{1,0:T(8,128)(2,1)S(1)}, u32[]{:S(2)}, u32[]{:S(2)}) collective-permute-start(bf16[256,256]{1,0:T(8,128)(2,1)S(1)} %kv.11), channel_id=1, source_target_pairs={{0,0},{1,1},{2,16},{3,17},{4,32},{5,33},{6,48},{7,49},{8,64},{9,65... | collective-permute-start | bytes 393224 | tf_op jit(solution)/shard_map/kv/ppermute | solution.py:559
  88.8 11.2 %collective-permute-start.25 = (bf16[256,256]{1,0:T(8,128)(2,1)S(1)}, bf16[256,256]{1,0:T(8,128)(2,1)S(1)}, u32[]{:S(2)}, u32[]{:S(2)}) collective-permute-start(bf16[256,256]{1,0:T(8,128)(2,1)S(1)} %kv.11), channel_id=1, source_target_pairs={{0,1},{1,0},{2,17},{3,16},{4,33},{5,32},{6,49},{7,48},{8,65},{9,64... | collective-permute-start | bytes 393224 | tf_op jit(solution)/shard_map/kv/ppermute | solution.py:559
  103.0 9.2 %collective-permute-start.26 = (bf16[4,128,512]{2,1,0:T(8,128)(2,1)S(1)}, bf16[4,128,512]{2,1,0:T(8,128)(2,1)S(1)}, u32[]{:S(2)}, u32[]{:S(2)}) collective-permute-start(bf16[4,128,512]{2,1,0:T(8,128)(2,1)S(1)} %get-tuple-element.68), channel_id=1, source_target_pairs={{0,1},{1,2},{2,3},{3,0},{4,5},{5,6},{6,7},{7,4},{8,9},{9,10},{10,1... | collective-permute-start | bytes 1572872 | tf_op jit(solution)/shard_map/mix/ppermute | solution.py:40
  103.5 10.9 %collective-permute-start.27 = (bf16[4,128,512]{2,1,0:T(8,128)(2,1)S(1)}, bf16[4,128,512]{2,1,0:T(8,128)(2,1)S(1)}, u32[]{:S(2)}, u32[]{:S(2)}) collective-permute-start(bf16[4,128,512]{2,1,0:T(8,128)(2,1)S(1)} %get-tuple-element.69), channel_id=1, source_target_pairs={{0,3},{1,0},{2,1},{3,2},{4,7},{5,4},{6,5},{7,6},{8,11},{9,8},{10,9... | collective-permute-start | bytes 1572872 | tf_op jit(solution)/shard_map/mix/ppermute | solution.py:40
  105.1 16.3 %collective-permute-start.28 = (bf16[4,128,512]{2,1,0:T(8,128)(2,1)S(1)}, bf16[4,128,512]{2,1,0:T(8,128)(2,1)S(1)}, u32[]{:S(2)}, u32[]{:S(2)}) collective-permute-start(bf16[4,128,512]{2,1,0:T(8,128)(2,1)S(1)} %get-tuple-element.70), channel_id=1, source_target_pairs={{0,2},{1,3},{2,0},{3,1},{4,6},{5,7},{6,4},{7,5},{8,10},{9,11},{10,... | collective-permute-start | bytes 1572872 | tf_op jit(solution)/shard_map/mix/ppermute | solution.py:40
  (13 other events, 224.8 us)
